TPU v7x, 128 devices: a whole 4x4x4 slice. The times are simulated.
128 devices in a mesh: spec: 2 (over y_lo), slab: 64 (over x, y_hi, z, core).
Axes of the slice: x: 4, y: 4 (y_hi: 2, y_lo: 2; y = y_hi * 2 + y_lo), z: 4, core: 2. Of those that a mesh axis runs over, the one named last changes fastest.
Arguments:
- amplitude: bfloat16 [512, 512, 256], P('slab'), may hold values from 0.5 to 1.5
- displacement: bfloat16 [3, 512, 512, 256], P(None, 'slab'), may hold values from -4 to 4
- support: int32 [512, 512, 256], P('slab'), may hold values 0 or 1
- counts: int32 [512, 512, 128], P(None, 'slab'), may hold values from 0 to 11
- bin_weights: float32 [4], replicated, may hold values from 0.5 to 2
- bin_scales: float32 [4], replicated, may hold values from 0.96 to 1.04
- bragg_vector: float32 [3], replicated, may hold values from 1 to 3
Outputs:
- new_amplitude: float32 [512, 512, 256], P('slab')
- new_displacement: bfloat16 [3, 512, 512, 256], P(None, 'slab')
All inputs are finite; a program needn't handle non-finite values. No bound on the sum of `support` on one device may be relied on, other than what follows from the above.
Results may differ from a plain program's by a relative error of at most 0.015.
Values may be sent and summed in bfloat16 or wider, within the bound.
A program may use at most 128 MiB of HBM per device.

v0:
```python
import math

import jax
import jax.numpy as jnp
from jax import lax
from jax.sharding import PartitionSpec as P

step_size = 0.5


def chirp_offsets(out_offset, in_offset, count_in, bin_scale):
    product = out_offset[:, None] * in_offset[None, :]
    fraction = (product % count_in).astype(jnp.float32) / count_in
    excess_angle = (bin_scale - 1.0) * (product.astype(jnp.float32) / count_in)
    phase_angle = -2.0 * math.pi * (fraction + excess_angle)
    normalizer = 1.0 / math.sqrt(count_in)
    real_part = jnp.cos(phase_angle) * normalizer
    imag_part = jnp.sin(phase_angle) * normalizer
    block_matrix = jnp.stack(
        [jnp.stack([real_part, -imag_part]), jnp.stack([imag_part, real_part])]
    )
    return jnp.transpose(block_matrix, (0, 2, 1, 3)).astype(jnp.bfloat16)


def chirp_matrix(count_out, count_in, bin_scale):
    out_offset = jnp.arange(count_out, dtype=jnp.int32) - count_out // 2
    in_offset = jnp.arange(count_in, dtype=jnp.int32) - count_in // 2
    return chirp_offsets(out_offset, in_offset, count_in, bin_scale)


def ratio_from(intensity, counts_rows):
    return 1.0 - jnp.sqrt(counts_rows.astype(jnp.float32) / jnp.maximum(intensity, 0.5))


def finish(amp_values, disp_values, mask_values, bragg_vector, sum_amp, sum_phase):
    new_amplitude = amp_values - step_size * (mask_values * sum_amp)
    grad_phase = -mask_values * amp_values * sum_phase
    new_displacement = (
        disp_values - step_size * bragg_vector[:, None, None, None] * grad_phase[None]
    ).astype(jnp.bfloat16)
    return (new_amplitude, new_displacement)


def per_device(amplitude, displacement, support, counts, bin_weights, bin_scales, bragg_vector):
    spec_count = lax.axis_size("spec")
    spec_index = lax.axis_index("spec")
    bins_total = bin_scales.shape[0]
    bins_local = bins_total // spec_count
    cells_z = amplitude.shape[2]
    rows_y = amplitude.shape[1]
    rows_x = counts.shape[0]
    frames = counts.shape[2]
    amp_values = amplitude.astype(jnp.float32)
    disp_values = displacement.astype(jnp.float32)
    mask_values = support.astype(jnp.float32)
    scales_local = lax.dynamic_slice_in_dim(bin_scales, spec_index * bins_local, bins_local)
    weights_local = lax.dynamic_slice_in_dim(bin_weights, spec_index * bins_local, bins_local)
    phase_field = (
        bragg_vector[0] * disp_values[0]
        + bragg_vector[1] * disp_values[1]
        + bragg_vector[2] * disp_values[2]
    )
    magnitude = mask_values * amp_values
    matrices = []
    section_list = []
    for member in range(bins_local):
        bin_scale = scales_local[member]
        bin_phase = bin_scale * phase_field
        mat_z = chirp_matrix(frames, cells_z, bin_scale)
        mat_y = chirp_matrix(rows_y, rows_y, bin_scale)
        mat_x = chirp_matrix(rows_x, rows_x, bin_scale)
        matrices.append((mat_z, mat_y, mat_x))
        exit_wave = jnp.stack(
            [magnitude * jnp.cos(bin_phase), magnitude * jnp.sin(bin_phase)]
        ).astype(jnp.bfloat16)
        section_one = jnp.einsum(
            "pxyn,okpn->oxyk", exit_wave, mat_z, preferred_element_type=jnp.float32
        ).astype(jnp.bfloat16)
        section_two = jnp.einsum(
            "pxnk,ojpn->oxjk", section_one, mat_y, preferred_element_type=jnp.float32
        ).astype(jnp.bfloat16)
        section_list.append(section_two)
    pencils = [
        lax.all_to_all(section, "slab", split_axis=2, concat_axis=1, tiled=True)
        for section in section_list
    ]
    far_list = []
    partial_value = None
    for member in range(bins_local):
        far_field = jnp.einsum(
            "pnjk,oipn->oijk",
            pencils[member],
            matrices[member][2],
            preferred_element_type=jnp.float32,
        )
        far_list.append(far_field)
        term = weights_local[member] * (far_field[0] * far_field[0] + far_field[1] * far_field[1])
        partial_value = term if partial_value is None else partial_value + term
    intensity = lax.psum(partial_value.astype(jnp.bfloat16), "spec").astype(jnp.float32)
    modulus_ratio = ratio_from(intensity, counts)
    back_list = []
    for member in range(bins_local):
        back_field = (weights_local[member] * modulus_ratio * far_list[member]).astype(jnp.bfloat16)
        back_one = jnp.einsum(
            "oijk,oipn->pnjk", back_field, matrices[member][2], preferred_element_type=jnp.float32
        ).astype(jnp.bfloat16)
        back_list.append(back_one)
    slabs = [
        lax.all_to_all(back_one, "slab", split_axis=1, concat_axis=2, tiled=True)
        for back_one in back_list
    ]
    part_amp = jnp.zeros(amplitude.shape, jnp.float32)
    part_phase = jnp.zeros(amplitude.shape, jnp.float32)
    for member in range(bins_local):
        bin_scale = scales_local[member]
        bin_phase = bin_scale * phase_field
        back_two = jnp.einsum(
            "oxjk,ojpn->pxnk",
            slabs[member],
            matrices[member][1],
            preferred_element_type=jnp.float32,
        ).astype(jnp.bfloat16)
        back_three = jnp.einsum(
            "oxyk,okpn->pxyn", back_two, matrices[member][0], preferred_element_type=jnp.float32
        )
        cosine = jnp.cos(bin_phase)
        sine_part = jnp.sin(bin_phase)
        part_amp = part_amp + (back_three[0] * cosine + back_three[1] * sine_part)
        part_phase = part_phase + bin_scale * (back_three[0] * sine_part - back_three[1] * cosine)
    summed = lax.psum(jnp.stack([part_amp, part_phase]).astype(jnp.bfloat16), "spec").astype(
        jnp.float32
    )
    return finish(amp_values, disp_values, mask_values, bragg_vector, summed[0], summed[1])


def solution(mesh):
    in_specs = (
        P("slab", None, None),
        P(None, "slab", None, None),
        P("slab", None, None),
        P(None, "slab", None),
        P(),
        P(),
        P(),
    )
    out_specs = (P("slab", None, None), P(None, "slab", None, None))
    return jax.shard_map(
        per_device, mesh=mesh, in_specs=in_specs, out_specs=out_specs, check_vma=False
    )
```

profile of v0, /device:TPU:1, one launch (start us, length us, event | category | flops | bytes accessed | tf_op | source)
XLA Modules:
  0.0 507.6 jit_solution(8900729084781085427)
XLA Ops:
  7.2 0.7 dynamic_slice.6
  7.9 0.6 fusion.111
  9.8 1.4 fusion.110
  11.3 0.0 copy-start.1
  11.3 4.4 convert_element_type.236
  15.7 0.0 copy-done.1
  15.7 0.2 copy-done.3
  15.9 18.6 %fusion.14 = (bf16[1,8,512,256]{3,2,0,1:T(8,128)(2,1)}, f32[1,8,512,256]{3,2,1,0:T(8,128)S(1)}) fusion(f32[]{:T(128)} %bitcast, bf16[8,512,256]{2,1,0:T(8,128)(2,1)S(1)} %copy-done.3, s32[8,512,256]{2,1,0:T(8,128)S(1)} %copy-done.1, f32[3,8,512,256]{3,2,1,0:T(8,128)S(1)} %convert_element_type.236, f32[]{:T(128)} %bitcast.18, f32[]{:T(128)} %bitcast.17, ...), kind=kLoop, calls=%fused_computation.54 | loop fusion | flops 11534336 | bytes 25165840 | tf_op jit(solution)/shard_map/stack | solution.py:73
  34.5 0.0 copy-start
  34.5 32.2 %fusion.15 = (bf16[1,8,512,256]{3,2,0,1:T(8,128)(2,1)}, bf16[1,8,512,256]{3,2,1,0:T(8,128)(2,1)}, bf16[1,8,512,256]{3,2,1,0:T(8,128)(2,1)}) fusion(f32[1,8,512,256]{3,2,1,0:T(8,128)S(1)} %get-tuple-element.7, f32[]{:T(128)} %bitcast, bf16[8,512,256]{2,1,0:T(8,128)(2,1)S(1)} %copy-done.3, s32[8,512,256]{2,1,0:T(8,128)S(1)} %copy-done.1, f32[]{:T(128)} %bitcast.40), kind=kLoop, calls=%fused_computation.55 | loop fusion | flops 11534336 | bytes 16777224 | tf_op jit(solution)/shard_map/stack | solution.py:73
  66.8 0.0 copy-done
  66.8 8.8 %negate_convert_fusion.1 = (bf16[1,512,512]{2,1,0:T(8,128)(2,1)S(1)}, bf16[1,512,512]{2,1,0:T(8,128)(2,1)S(1)}, bf16[1,512,512]{2,1,0:T(8,128)(2,1)S(1)}, bf16[1...) fusion(f32[]{:T(128)S(6)} %mul.631, s32[512]{0:T(512)S(1)} %iota_add_fusion, ...), kind=kLoop, calls=%fused_computation.120 | loop fusion | flops 8650752 | bytes 3147784 | tf_op jit(solution)/shard_map/convert.34
  75.6 1.3 negate_convert_fusion.3
  77.0 2.1 maximum_bitcast_fusion.5
  79.1 7.7 %fusion.58 = bf16[2,8,512,128]{3,2,1,0:T(8,128)(2,1)} fusion(bf16[1,2,512,512]{3,2,1,0:T(8,128)(2,1)} %get-tuple-element.18, bf16[1,2,512,512]{3,2,1,0:T(8,128)(2,1)} %get-tuple-element.17, bf16[1,8,512,256]{3,2,0,1:T(8,128)(2,1)} %get-tuple-element.12, bf16[1,8,512,256]{3,2,0,1:T(8,128)(2,1)} %get-tuple-element.6, ...), kind=kOutput, calls=%fused_computation.98 | convolution fusion | flops 3236429824 | bytes 8650752 | tf_op jit(solution)/shard_map/pxnk,ojpn->oxjk/dot_general | solution.py:79
  86.8 4.3 copy.65
  91.0 12.7 %all-to-all-start = ((bf16[2,8,512,128]{3,1,0,2:T(8,128)(2,1)}), bf16[2,8,512,128]{3,1,0,2:T(8,128)(2,1)}, u32[]{:S(2)}, u32[]{:S(2)}) async-start(bf16[2,8,512,128]{3,1,0,2:T(8,128)(2,1)} %copy.65), calls=%async_computation | async-start | bytes 4194304 | tf_op jit(solution)/shard_map/all_to_all | solution.py:84
  103.7 7.6 %fusion.63 = bf16[2,8,512,128]{3,2,1,0:T(8,128)(2,1)} fusion(bf16[1,2,512,512]{3,2,1,0:T(8,128)(2,1)} %get-tuple-element.44, bf16[1,2,512,512]{3,2,1,0:T(8,128)(2,1)} %get-tuple-element.45, bf16[1,2,128,256]{3,2,1,0:T(8,128)(2,1)S(1)} %get-tuple-element.46, bf16[1,2,128,256]{3,2,1,0:T(8,128)(2,1)S(1)} %get-tuple-element.47, ...), kind=kOutput, calls=%fused_computation.99 | convolution fusion | flops 3230138368 | bytes 8650752 | tf_op jit(solution)/shard_map/pxnk,ojpn->oxjk/dot_general | solution.py:79
  111.4 4.3 copy.69
  115.6 0.0 copy-start.10
  115.6 18.5 %all-to-all-done = bf16[2,8,512,128]{3,1,0,2:T(8,128)(2,1)} async-done(((bf16[2,8,512,128]{3,1,0,2:T(8,128)(2,1)}), bf16[2,8,512,128]{3,1,0,2:T(8,128)(2,1)}, u32[]{:S(2)}, u32[]{:S(2)}) %all-to-all-start) | async-done | bytes 2097184 | tf_op jit(solution)/shard_map/all_to_all | solution.py:84
  134.1 5.1 %all-to-all-start.1 = ((bf16[2,8,512,128]{3,1,0,2:T(8,128)(2,1)}), bf16[2,8,512,128]{3,1,0,2:T(8,128)(2,1)}, u32[]{:S(2)}, u32[]{:S(2)}) async-start(bf16[2,8,512,128]{3,1,0,2:T(8,128)(2,1)} %copy.69), calls=%async_computation.1 | async-start | bytes 4194304 | tf_op jit(solution)/shard_map/all_to_all | solution.py:84
  139.3 0.0 all-reduce.3.cloned.1.call-start
  139.3 0.0 copy-done.10
  139.3 0.1 dynamic_slice.7
  139.4 0.6 fusion.109
  140.0 6.6 %convolution_bitcast_fusion.3 = f32[2,512,8,128]{3,1,2,0:T(8,128)} fusion(bf16[2,8,64,8,128]{4,1,0,3,2:T(8,128)(2,1)} %bitcast.33, bf16[1,2,512,512]{3,2,1,0:T(8,128)(2,1)} %get-tuple-element.18, bf16[1,2,512,512]{3,2,1,0:T(8,128)(2,1)} %get-tuple-element.17), kind=kOutput, calls=%fused_computation.53 | convolution fusion | flops 2151677952 | bytes 8388608 | tf_op jit(solution)/shard_map/pnjk,oipn->oijk/dot_general | solution.py:90
  146.6 23.2 %all-to-all-done.1 = bf16[2,8,512,128]{3,1,0,2:T(8,128)(2,1)} async-done(((bf16[2,8,512,128]{3,1,0,2:T(8,128)(2,1)}), bf16[2,8,512,128]{3,1,0,2:T(8,128)(2,1)}, u32[]{:S(2)}, u32[]{:S(2)}) %all-to-all-start.1) | async-done | bytes 2097184 | tf_op jit(solution)/shard_map/all_to_all | solution.py:84
  169.7 4.7 convolution_bitcast_fusion.2
  174.4 0.0 copy-start.4
  174.5 2.0 copy-done.4
  176.5 0.0 copy-done.5
  176.5 2.9 fusion.77
  179.3 0.0 all-reduce.3.cloned.1.call-update
  179.3 42.4 %all-reduce.3.cloned.1.call-done = bf16[512,8,128]{2,0,1:T(8,128)(2,1)} async-done(((bf16[512,8,128]{2,0,1:T(8,128)(2,1)}), bf16[512,8,128]{2,0,1:T(8,128)(2,1)}) %all-reduce.3.cloned.1.call-update) | async-done | bytes 1048592 | tf_op jit(solution)/shard_map/psum | solution.py:99
  221.8 0.0 copy-start.6
  221.8 0.0 copy-start.7
  221.8 0.0 copy-start.8
  221.8 6.2 %broadcast_multiply_fusion.1 = (f32[512,8,128]{2,0,1:T(8,128)S(1)}, f32[512,8,128]{2,0,1:T(8,128)}) fusion(f32[]{:T(128)} %bitcast.10, bf16[512,8,128]{2,0,1:T(8,128)(2,1)} %all-reduce.3.cloned.1.call-done, s32[512,8,128]{2,1,0:T(8,128)} %param.10, f32[]{:T(128)} %bitcast.39), kind=kLoop, calls=%fused_computation.119 | loop fusion | flops 3670016 | bytes 7340040 | tf_op jit(solution)/shard_map/mul | solution.py:103
  228.0 0.0 copy-done.6
  228.0 0.0 copy-done.7
  228.0 0.0 copy-done.8
  228.0 2.4 bitcast_convert_fusion.3
  230.5 2.7 copy.73
  233.1 21.5 %all-to-all-start.2 = ((bf16[2,512,8,128]{3,2,0,1:T(8,128)(2,1)}), bf16[2,512,8,128]{3,2,0,1:T(8,128)(2,1)}, u32[]{:S(2)}, u32[]{:S(2)}) async-start(bf16[2,512,8,128]{3,2,0,1:T(8,128)(2,1)} %copy.73), calls=%async_computation.2 | async-start | bytes 4194304 | tf_op jit(solution)/shard_map/all_to_all | solution.py:109
  254.6 5.8 %bitcast_convert_fusion.2 = bf16[2,512,8,128]{3,1,2,0:T(8,128)(2,1)S(1)} fusion(bf16[1,2,512,512]{3,2,1,0:T(8,128)(2,1)} %get-tuple-element.44, bf16[1,2,512,512]{3,2,1,0:T(8,128)(2,1)} %get-tuple-element.45, f32[2,512,8,128]{3,1,2,0:T(8,128)} %copy-done.4, f32[512,8,128]{2,0,1:T(8,128)} %get-tuple-element.16), kind=kOutput, calls=%fused_computation.22 | convolution fusion | flops 2151677952 | bytes 10485760 | tf_op jit(solution)/shard_map/oijk,oipn->pnjk/dot_general | solution.py:104
  260.5 2.7 copy.82
  263.1 21.7 %all-to-all-done.2 = bf16[2,512,8,128]{3,2,0,1:T(8,128)(2,1)} async-done(((bf16[2,512,8,128]{3,2,0,1:T(8,128)(2,1)}), bf16[2,512,8,128]{3,2,0,1:T(8,128)(2,1)}, u32[]{:S(2)}, u32[]{:S(2)}) %all-to-all-start.2) | async-done | bytes 2097184 | tf_op jit(solution)/shard_map/all_to_all | solution.py:109
  284.8 5.1 %all-to-all-start.3 = ((bf16[2,512,8,128]{3,2,0,1:T(8,128)(2,1)}), bf16[2,512,8,128]{3,2,0,1:T(8,128)(2,1)}, u32[]{:S(2)}, u32[]{:S(2)}) async-start(bf16[2,512,8,128]{3,2,0,1:T(8,128)(2,1)} %copy.82), calls=%async_computation.3 | async-start | bytes 4194304 | tf_op jit(solution)/shard_map/all_to_all | solution.py:109
  290.0 0.0 all-reduce.5.cloned.1.call-start
  290.0 9.0 %convolution_bitcast_fusion.1 = f32[2,8,512,256]{3,2,1,0:T(8,128)} fusion(bf16[1,2,512,512]{3,2,1,0:T(8,128)(2,1)} %get-tuple-element.18, bf16[1,2,512,512]{3,2,1,0:T(8,128)(2,1)} %get-tuple-element.17, bf16[2,8,64,8,128]{4,3,0,1,2:T(8,128)(2,1)} %bitcast.76, bf16[1,2,128,256]{3,2,1,0:T(8,128)(2,1)S(1)} %get-tuple-element.22, ...), kind=kOutput, calls=%fused_computation.47 | convolution fusion | flops 3226599424 | bytes 12845056 | tf_op jit(solution)/shard_map/oxyk,okpn->pxyn/dot_general | solution.py:123
  299.0 21.5 %all-to-all-done.3 = bf16[2,512,8,128]{3,2,0,1:T(8,128)(2,1)} async-done(((bf16[2,512,8,128]{3,2,0,1:T(8,128)(2,1)}), bf16[2,512,8,128]{3,2,0,1:T(8,128)(2,1)}, u32[]{:S(2)}, u32[]{:S(2)}) %all-to-all-start.3) | async-done | bytes 2097184 | tf_op jit(solution)/shard_map/all_to_all | solution.py:109
  320.5 8.9 %convolution_bitcast_fusion = f32[2,8,512,256]{3,2,1,0:T(8,128)} fusion(bf16[1,2,512,512]{3,2,1,0:T(8,128)(2,1)} %get-tuple-element.44, bf16[1,2,512,512]{3,2,1,0:T(8,128)(2,1)} %get-tuple-element.45, bf16[2,8,64,8,128]{4,3,0,1,2:T(8,128)(2,1)} %bitcast.94, bf16[1,2,128,256]{3,2,1,0:T(8,128)(2,1)S(1)} %get-tuple-element.46, ...), kind=kOutput, calls=%fused_computation.46 | convolution fusion | flops 3226599424 | bytes 12845056 | tf_op jit(solution)/shard_map/oxyk,okpn->pxyn/dot_general | solution.py:123
  329.4 35.2 %add_convert_fusion.1 = (bf16[1,8,512,256]{3,2,1,0:T(8,128)(2,1)S(1)}, bf16[1,8,512,256]{3,2,1,0:T(8,128)(2,1)S(1)}) fusion(f32[2,8,512,256]{3,2,1,0:T(8,128)} %convolution_bitcast_fusion, f32[2,8,512,256]{3,2,1,0:T(8,128)} %convolution_bitcast_fusion.1, f32[1,8,512,256]{3,2,1,0:T(8,128)} %copy-done, f32[]{:T(128)} %bitcast.40, f32[]{:T(128)} %bitcast), kind=kLoop, calls=%fused_computation.39 | loop fusion | flops 20971520 | bytes 25165832 | tf_op jit(solution)/shard_map/convert
  364.6 2.4 pad_maximum_fusion
  367.0 0.0 copy-start.9
  367.0 0.0 all-reduce.5.cloned.1.call-update
  367.0 0.6 copy-done.9
  367.6 109.6 %all-reduce.5.cloned.1.call-done = bf16[2,8,512,256]{3,2,1,0:T(8,128)(2,1)} async-done(((bf16[2,8,512,256]{3,2,1,0:T(8,128)(2,1)}), bf16[2,8,512,256]{3,2,1,0:T(8,128)(2,1)}) %all-reduce.5.cloned.1.call-update) | async-done | bytes 4194320 | tf_op jit(solution)/shard_map/psum | solution.py:130
  477.3 0.0 copy-start.2
  477.3 6.5 %convert_element_type.256 = f32[2,8,512,256]{3,2,1,0:T(8,128)} convert(bf16[2,8,512,256]{3,2,1,0:T(8,128)(2,1)} %all-reduce.5.cloned.1.call-done) | non-fusion elementwise | flops 2097152 | bytes 12582912 | tf_op jit(solution)/shard_map/convert_element_type | solution.py:130
  483.8 0.0 copy-done.2
  483.8 8.2 %fusion = (f32[8,512,256]{2,1,0:T(8,128)}, f32[8,512,256]{2,1,0:T(8,128)}) fusion(bf16[8,512,256]{2,1,0:T(8,128)(2,1)S(1)} %copy-done.3, f32[2,8,512,256]{3,2,1,0:T(8,128)} %convert_element_type.256, s32[8,512,256]{2,1,0:T(8,128)S(1)} %copy-done.2), kind=kLoop, calls=%fused_computation.4 | loop fusion | flops 8388608 | bytes 23068672 | tf_op jit(solution)/shard_map/mul | solution.py:37
  492.0 8.6 %subtract_convert_fusion = bf16[3,8,512,256]{3,2,1,0:T(8,128)(2,1)} fusion(f32[8,512,256]{2,1,0:T(8,128)} %get-tuple-element.10, f32[3]{0:T(128)S(1)} %broadcast_multiply_fusion.2, bf16[3,8,512,256]{3,2,1,0:T(8,128)(2,1)} %param.8), kind=kLoop, calls=%fused_computation | loop fusion | flops 12582912 | bytes 16777228 | tf_op jit(solution)/shard_map/convert_element_type | solution.py:40
  (7 shorter events, 0.1 us)
Async XLA Ops:
  11.3 4.5 copy-start.1
  11.3 4.7 copy-start.3
  34.5 32.2 %copy-start = (f32[1,8,512,256]{3,2,1,0:T(8,128)}, f32[1,8,512,256]{3,2,1,0:T(8,128)S(1)}, u32[]{:S(2)}) copy-start(f32[1,8,512,256]{3,2,1,0:T(8,128)S(1)} %get-tuple-element.7) | copy-start | bytes 12582916
  91.0 43.1 %all-to-all-start = ((bf16[2,8,512,128]{3,1,0,2:T(8,128)(2,1)}), bf16[2,8,512,128]{3,1,0,2:T(8,128)(2,1)}, u32[]{:S(2)}, u32[]{:S(2)}) async-start(bf16[2,8,512,128]{3,1,0,2:T(8,128)(2,1)} %copy.65), calls=%async_computation | async-start | bytes 4194304 | tf_op jit(solution)/shard_map/all_to_all | solution.py:84
  115.6 23.7 %copy-start.10 = (f32[4]{0:T(128)S(1)}, f32[4]{0:T(128)}, u32[]{:S(2)}) copy-start(f32[4]{0:T(128)} %param.11) | copy-start | bytes 52
  134.1 35.6 %all-to-all-start.1 = ((bf16[2,8,512,128]{3,1,0,2:T(8,128)(2,1)}), bf16[2,8,512,128]{3,1,0,2:T(8,128)(2,1)}, u32[]{:S(2)}, u32[]{:S(2)}) async-start(bf16[2,8,512,128]{3,1,0,2:T(8,128)(2,1)} %copy.69), calls=%async_computation.1 | async-start | bytes 4194304 | tf_op jit(solution)/shard_map/all_to_all | solution.py:84
  139.3 82.5 %all-reduce.3.cloned.1.call-start = ((), (), s32[]{:S(2)}) async-start(), calls=%async_computation.4 | async-start | bytes 2097152 | tf_op jit(solution)/shard_map/psum | solution.py:99
  169.7 6.7 %copy-start.5 = (f32[2,512,8,128]{3,1,2,0:T(8,128)S(1)}, f32[2,512,8,128]{3,1,2,0:T(8,128)}, u32[]{:S(2)}) copy-start(f32[2,512,8,128]{3,1,2,0:T(8,128)} %convolution_bitcast_fusion.3) | copy-start | bytes 12582916
  174.4 2.0 copy-start.4
  221.8 6.2 %copy-start.6 = (f32[2,512,8,128]{3,1,2,0:T(8,128)S(1)}, f32[2,512,8,128]{3,1,2,0:T(8,128)}, u32[]{:S(2)}) copy-start(f32[2,512,8,128]{3,1,2,0:T(8,128)} %convolution_bitcast_fusion.3) | copy-start | bytes 12582916
  221.8 6.2 %copy-start.7 = (bf16[1,2,512,512]{3,2,1,0:T(8,128)(2,1)S(1)}, bf16[1,2,512,512]{3,2,1,0:T(8,128)(2,1)}, u32[]{:S(2)}) copy-start(bf16[1,2,512,512]{3,2,1,0:T(8,128)(2,1)} %get-tuple-element.17) | copy-start | bytes 3145732
  221.8 6.2 %copy-start.8 = (bf16[1,2,512,512]{3,2,1,0:T(8,128)(2,1)S(1)}, bf16[1,2,512,512]{3,2,1,0:T(8,128)(2,1)}, u32[]{:S(2)}) copy-start(bf16[1,2,512,512]{3,2,1,0:T(8,128)(2,1)} %get-tuple-element.18) | copy-start | bytes 3145732
  233.1 51.7 %all-to-all-start.2 = ((bf16[2,512,8,128]{3,2,0,1:T(8,128)(2,1)}), bf16[2,512,8,128]{3,2,0,1:T(8,128)(2,1)}, u32[]{:S(2)}, u32[]{:S(2)}) async-start(bf16[2,512,8,128]{3,2,0,1:T(8,128)(2,1)} %copy.73), calls=%async_computation.2 | async-start | bytes 4194304 | tf_op jit(solution)/shard_map/all_to_all | solution.py:109
  284.8 35.6 %all-to-all-start.3 = ((bf16[2,512,8,128]{3,2,0,1:T(8,128)(2,1)}), bf16[2,512,8,128]{3,2,0,1:T(8,128)(2,1)}, u32[]{:S(2)}, u32[]{:S(2)}) async-start(bf16[2,512,8,128]{3,2,0,1:T(8,128)(2,1)} %copy.82), calls=%async_computation.3 | async-start | bytes 4194304 | tf_op jit(solution)/shard_map/all_to_all | solution.py:109
  290.0 187.3 %all-reduce.5.cloned.1.call-start = ((), (), s32[]{:S(2)}) async-start(), calls=%async_computation.5 | async-start | bytes 8388608 | tf_op jit(solution)/shard_map/psum | solution.py:130
  367.0 0.7 copy-start.9
  477.3 6.5 %copy-start.2 = (s32[8,512,256]{2,1,0:T(8,128)S(1)}, s32[8,512,256]{2,1,0:T(8,128)}, u32[]{:S(2)}) copy-start(s32[8,512,256]{2,1,0:T(8,128)} %param.9) | copy-start | bytes 12582916
Sparse Core Ops, SparseCore 0:
  179.5 42.2 all-reduce.2
  367.1 110.1 all-reduce.4
where the time goes:
time: 511 us; the launch traced here: 508 us
  waiting for transfers between devices  237 us (46%)
  other arithmetic  138 us (27%)
  matrix products  52.8 us (10%)
  starting transfers between devices  44.5 us (9%)
  local copies, waits for them, and re-layouts  20.2 us (4%)
  between operations  15.7 us (3%)
    psum x1, waiting for transfers between devices, per_device(): lax.psum(jnp.stack([part_amp, part_phase]).astype(jnp.bfloat16), 'spec')  110 us
    another operation x2, other arithmetic, per_device(): jnp.stack([magnitude * jnp.cos(bin_phase), magnitude * jnp.sin(bin_phase)])  50.8 us
    another operation x3, other arithmetic  45.3 us
    all_to_all x2, waiting for transfers between devices, per_device(): lax.all_to_all(back_one, 'slab', split_axis=1, concat_axis=2, tiled=True)  43.2 us
    psum x1, waiting for transfers between devices, per_device(): lax.psum(partial_value.astype(jnp.bfloat16), 'spec').astype(jnp.float32)  42.4 us
    all_to_all x2, waiting for transfers between devices, per_device(): lax.all_to_all(section, 'slab', split_axis=2, concat_axis=1, tiled=True)  41.7 us
    all_to_all x2, starting transfers between devices, per_device(): lax.all_to_all(back_one, 'slab', split_axis=1, concat_axis=2, tiled=True)  26.6 us
    dot_general x2, matrix products, per_device(): jnp.einsum('oxyk,okpn->pxyn', back_two, matrices[member][0], preferred_el...  17.9 us
  transfers between devices with their start and end apart: 6, of which 6 were waited for; matrix products, arithmetic and copies ran while one was open for 7% of the time, Pallas kernels for 0%

commit v1 on v0

v1 whole, which is shorter than its diff:
```python
import functools
import math

import jax
import jax.numpy as jnp
from jax import lax
from jax.experimental import pallas as pl
from jax.experimental.pallas import tpu as pltpu
from jax.sharding import PartitionSpec as P

step_size = 0.5
both_axes = ("slab", "spec")
vmem_limit = 60 * 1024 * 1024
cos_terms = (
    0.9999992117703129, -19.738980419471183, 64.92865850463387,
    -85.27162830147759, 58.7905066287335, -21.071108461812614,
)
sin_terms = (
    6.283184916984337, -41.34158926418227, 81.59994386457431,
    -76.61447586037943, 41.342889429509576, -12.4712447471884,
)


def cos_sin_turns(turns):
    rest = turns - jnp.floor(turns + 0.5)
    square = rest * rest
    cosine = jnp.full_like(square, cos_terms[-1])
    sine = jnp.full_like(square, sin_terms[-1])
    for level in range(len(cos_terms) - 2, -1, -1):
        cosine = cosine * square + cos_terms[level]
        sine = sine * square + sin_terms[level]
    return cosine, sine * rest


def chirp_parts(out_index, in_index, count_out, count_in, bin_scale):
    product = (out_index - count_out // 2) * (in_index - count_in // 2)
    fraction = (product & (count_in - 1)).astype(jnp.float32) * (1.0 / count_in)
    excess = (bin_scale - 1.0) * (product.astype(jnp.float32) * (1.0 / count_in))
    cosine, sine = cos_sin_turns(fraction + excess)
    normalizer = 1.0 / math.sqrt(count_in)
    return cosine * normalizer, sine * -normalizer


def iota(shape, dim):
    return lax.broadcasted_iota(jnp.int32, shape, dim)


def dot(a, b):
    return jnp.dot(a, b, preferred_element_type=jnp.float32)


def params(limit=vmem_limit):
    return pltpu.CompilerParams(vmem_limit_bytes=limit)


def row_matrices_kernel(scales_ref, rows_ref, zf_ref, zb_ref, *, size, cells_z, frames):
    bin_scale = scales_ref[pl.program_id(0)]
    tile = 64

    def body(step, carry):
        start = step * tile
        out_index = start + iota((tile, size), 0)
        real, imag = chirp_parts(out_index, iota((tile, size), 1), size, size, bin_scale)
        real = real.reshape(tile // 8, 8, size)
        imag = imag.reshape(tile // 8, 8, size)
        low = iota(real.shape, 1) < 4

        def interleave(first, second):
            even = jnp.where(low, first, pltpu.roll(second, 4, 1))
            odd = jnp.where(low, pltpu.roll(first, 4, 1), second)
            return jnp.stack([even, odd], axis=1).reshape(2 * tile, size)

        at = pl.ds(pl.multiple_of(2 * start, 2 * tile), 2 * tile)
        rows_ref[0, at, 0:size] = interleave(real, imag).astype(jnp.bfloat16)
        rows_ref[0, at, size : 2 * size] = interleave(-imag, real).astype(jnp.bfloat16)
        return carry

    lax.fori_loop(0, size // tile, body, 0)
    real, imag = chirp_parts(
        iota((cells_z, frames), 1), iota((cells_z, frames), 0), frames, cells_z, bin_scale
    )
    zf_ref[0, 0:cells_z, 0:frames] = real.astype(jnp.bfloat16)
    zf_ref[0, 0:cells_z, frames : 2 * frames] = imag.astype(jnp.bfloat16)
    zf_ref[0, cells_z : 2 * cells_z, 0:frames] = (-imag).astype(jnp.bfloat16)
    zf_ref[0, cells_z : 2 * cells_z, frames : 2 * frames] = real.astype(jnp.bfloat16)
    real, imag = chirp_parts(
        iota((frames, cells_z), 0), iota((frames, cells_z), 1), frames, cells_z, bin_scale
    )
    zb_ref[0, 0:frames, 0:cells_z] = real.astype(jnp.bfloat16)
    zb_ref[0, 0:frames, cells_z : 2 * cells_z] = imag.astype(jnp.bfloat16)
    zb_ref[0, frames : 2 * frames, 0:cells_z] = (-imag).astype(jnp.bfloat16)
    zb_ref[0, frames : 2 * frames, cells_z : 2 * cells_z] = real.astype(jnp.bfloat16)


def row_matrices(bin_scales, size, cells_z, frames):
    bins = bin_scales.shape[0]
    return pl.pallas_call(
        functools.partial(row_matrices_kernel, size=size, cells_z=cells_z, frames=frames),
        grid=(bins,),
        in_specs=[pl.BlockSpec(memory_space=pltpu.SMEM)],
        out_specs=[
            pl.BlockSpec((1, 2 * size, 2 * size), lambda b: (b, 0, 0)),
            pl.BlockSpec((1, 2 * cells_z, 2 * frames), lambda b: (b, 0, 0)),
            pl.BlockSpec((1, 2 * frames, 2 * cells_z), lambda b: (b, 0, 0)),
        ],
        out_shape=[
            jax.ShapeDtypeStruct((bins, 2 * size, 2 * size), jnp.bfloat16),
            jax.ShapeDtypeStruct((bins, 2 * cells_z, 2 * frames), jnp.bfloat16),
            jax.ShapeDtypeStruct((bins, 2 * frames, 2 * cells_z), jnp.bfloat16),
        ],
        compiler_params=params(),
        name="row_matrices",
    )(bin_scales)


def column_matrices_kernel(scales_ref, cols_ref, *, size):
    bin_scale = scales_ref[pl.program_id(0)]
    tile = 64
    owners = size // 4

    def body(step, carry):
        start = step * tile
        out_index = start + iota((tile, size), 0)
        lane = iota((tile, size), 1)
        in_index = 4 * (lane % owners) + lane // owners
        real, imag = chirp_parts(out_index, in_index, size, size, bin_scale)
        at = pl.ds(pl.multiple_of(start, tile), tile)
        cols_ref[0, 0, at, 0:size] = real.astype(jnp.bfloat16)
        cols_ref[0, 0, at, size : 2 * size] = (-imag).astype(jnp.bfloat16)
        cols_ref[0, 1, at, 0:size] = imag.astype(jnp.bfloat16)
        cols_ref[0, 1, at, size : 2 * size] = real.astype(jnp.bfloat16)
        return carry

    lax.fori_loop(0, size // tile, body, 0)


def column_matrices(bin_scales, size):
    bins = bin_scales.shape[0]
    return pl.pallas_call(
        functools.partial(column_matrices_kernel, size=size),
        grid=(bins,),
        in_specs=[pl.BlockSpec(memory_space=pltpu.SMEM)],
        out_specs=pl.BlockSpec((1, 2, size, 2 * size), lambda b: (b, 0, 0, 0)),
        out_shape=jax.ShapeDtypeStruct((bins, 2, size, 2 * size), jnp.bfloat16),
        compiler_params=params(),
        cost_estimate=pl.CostEstimate(flops=8_000_000_000, bytes_accessed=8 << 20, transcendentals=0),
        name="column_matrices",
    )(bin_scales)


def forward_kernel(
    place_ref, bragg_ref, scales_ref, disp_ref, amp_ref, mask_ref, zf_ref, rows_ref,
    wave_ref, out_ref, section, *, first,
):
    step = pl.program_id(0)
    cells_y, cells_z = amp_ref.shape[1:]
    frames = zf_ref.shape[2] // 2

    @pl.when(step < 4)
    def _():
        phase = (
            bragg_ref[0] * disp_ref[0, 0].astype(jnp.float32)
            + bragg_ref[1] * disp_ref[1, 0].astype(jnp.float32)
            + bragg_ref[2] * disp_ref[2, 0].astype(jnp.float32)
        )
        magnitude = amp_ref[0].astype(jnp.float32) * mask_ref[0].astype(jnp.float32)
        for member in range(2):
            scale = scales_ref[first + member] * (0.5 / math.pi)
            cosine, sine = cos_sin_turns(scale * phase)
            wave_ref[member, 0, :, 0:cells_z] = (magnitude * cosine).astype(jnp.bfloat16)
            wave_ref[member, 0, :, cells_z : 2 * cells_z] = (magnitude * sine).astype(jnp.bfloat16)
            both = dot(wave_ref[member, 0], zf_ref[member]).astype(jnp.bfloat16)
            section[member, step, 0:cells_y, :] = both[:, 0:frames]
            section[member, step, cells_y : 2 * cells_y, :] = both[:, frames : 2 * frames]

    @pl.when(step >= 4)
    def _():
        parts = []
        for member in range(2):
            wide = jnp.concatenate([section[member, row] for row in range(4)], axis=1)
            value = dot(rows_ref[member], wide)
            parts.append(value.reshape(value.shape[0] // 8, 8, value.shape[1]))
        out_ref[...] = jnp.concatenate(parts, axis=1).astype(jnp.bfloat16)


def forward(place, bragg, scales, disp, amp, mask, zf, rows, first):
    _, _, cells_y, cells_z = disp.shape
    size = rows.shape[1]
    frames = zf.shape[2] // 2
    pair = first // 2
    tiles = 4
    row_tile = size // tiles
    owners = size // 8

    def at_row(step):
        return jnp.minimum(step, 3)

    def at_tile(step):
        return jnp.maximum(step - 4, 0)

    return pl.pallas_call(
        functools.partial(forward_kernel, first=first),
        grid_spec=pltpu.PrefetchScalarGridSpec(
            num_scalar_prefetch=3,
            grid=(4 + tiles,),
            in_specs=[
                pl.BlockSpec((3, 1, cells_y, cells_z), lambda t, p, *_: (0, 4 * p[0] + at_row(t), 0, 0)),
                pl.BlockSpec((1, cells_y, cells_z), lambda t, p, *_: (4 * p[0] + at_row(t), 0, 0)),
                pl.BlockSpec((1, cells_y, cells_z), lambda t, p, *_: (4 * p[0] + at_row(t), 0, 0)),
                pl.BlockSpec((2, 2 * cells_z, 2 * frames), lambda t, *_: (pair, 0, 0)),
                pl.BlockSpec((2, row_tile, size), lambda t, *_: (pair, at_tile(t), 0)),
            ],
            out_specs=[
                pl.BlockSpec((2, 1, cells_y, 2 * cells_z), lambda t, *_: (0, at_row(t), 0, 0)),
                pl.BlockSpec((owners // tiles, 16, 4 * frames), lambda t, *_: (at_tile(t), 0, 0)),
            ],
            scratch_shapes=[pltpu.VMEM((2, 4, 2 * cells_y, frames), jnp.bfloat16)],
        ),
        out_shape=[
            jax.ShapeDtypeStruct((2, 4, cells_y, 2 * cells_z), jnp.bfloat16),
            jax.ShapeDtypeStruct((owners, 16, 4 * frames), jnp.bfloat16),
        ],
        compiler_params=params(),
        cost_estimate=pl.CostEstimate(flops=3_300_000_000 * 2, bytes_accessed=20 << 20, transcendentals=0),
        name="forward_z_y",
    )(place, bragg, scales, disp, amp, mask, zf, rows)


def gather_columns(got_ref, wide, frames):
    owners = got_ref.shape[0]
    for lane_group in range(4):
        piece = got_ref[:, :, lane_group * frames : (lane_group + 1) * frames]
        turned = jnp.swapaxes(piece.astype(jnp.float32), 0, 1).astype(jnp.bfloat16)
        for member in range(2):
            for part in range(2):
                at = (4 * part + lane_group) * owners
                for row in range(4):
                    wide[member, at : at + owners, row * frames : (row + 1) * frames] = turned[
                        8 * member + 4 * part + row
                    ]


def far_kernel(got_ref, cols_ref, out_ref, wide, *, frames):
    step = pl.program_id(0)

    @pl.when(step == 0)
    def _():
        gather_columns(got_ref, wide, frames)

    for member in range(2):
        for part in range(2):
            out_ref[member, part] = dot(cols_ref[member, part], wide[member]).astype(out_ref.dtype)


def apply_columns(got, cols, first, out_dtype):
    owners, _, lanes = got.shape
    size = cols.shape[2]
    frames = lanes // 4
    tiles = 4
    pair = first // 2
    return pl.pallas_call(
        functools.partial(far_kernel, frames=frames),
        grid=(tiles,),
        in_specs=[
            pl.BlockSpec((owners, 16, lanes), lambda t: (0, 0, 0)),
            pl.BlockSpec((2, 2, size // tiles, 2 * size), lambda t: (pair, 0, t, 0)),
        ],
        out_specs=pl.BlockSpec((2, 2, size // tiles, lanes), lambda t: (0, 0, t, 0)),
        out_shape=jax.ShapeDtypeStruct((2, 2, size, lanes), out_dtype),
        scratch_shapes=[pltpu.VMEM((2, 2 * size, lanes), jnp.bfloat16)],
        compiler_params=params(),
        cost_estimate=pl.CostEstimate(flops=4_300_000_000, bytes_accessed=12 << 20, transcendentals=0),
        name="apply_columns",
    )(got, cols)


def ratio_kernel(weights_ref, low_ref, high_ref, counts_ref, back_low_ref, back_high_ref):
    intensity = None
    for member in range(4):
        field_ref = low_ref if member < 2 else high_ref
        real, imag = field_ref[member % 2, 0], field_ref[member % 2, 1]
        term = weights_ref[member] * (real * real + imag * imag)
        intensity = term if intensity is None else intensity + term
    ratio = 1.0 - jnp.sqrt(counts_ref[...].astype(jnp.float32) / jnp.maximum(intensity, 0.5))
    for member in range(4):
        field_ref = low_ref if member < 2 else high_ref
        back_ref = back_low_ref if member < 2 else back_high_ref
        factor = weights_ref[member] * ratio
        back_ref[member % 2, 0] = (factor * field_ref[member % 2, 0]).astype(jnp.bfloat16)
        back_ref[member % 2, 1] = (-factor * field_ref[member % 2, 1]).astype(jnp.bfloat16)


def back_fields(weights, low, high, counts):
    _, _, size, lanes = low.shape
    tiles = 8
    field = pl.BlockSpec((2, 2, size // tiles, lanes), lambda t: (0, 0, t, 0))
    return pl.pallas_call(
        ratio_kernel,
        grid=(tiles,),
        in_specs=[
            pl.BlockSpec(memory_space=pltpu.SMEM),
            field,
            field,
            pl.BlockSpec((size // tiles, lanes), lambda t: (t, 0)),
        ],
        out_specs=[field, field],
        out_shape=[jax.ShapeDtypeStruct(low.shape, jnp.bfloat16)] * 2,
        compiler_params=params(),
        name="back_fields",
    )(weights, low, high, counts)


def back_rows_kernel(field_ref, rows_ref, out_ref):
    parts = []
    for member in range(2):
        value = dot(rows_ref[member], field_ref[member])
        parts.append(value.reshape(value.shape[0] // 8, 8, value.shape[1]))
    out_ref[...] = jnp.concatenate(parts, axis=1).astype(jnp.bfloat16)


def back_rows(field, rows, first):
    size = rows.shape[1]
    lanes = field.shape[3]
    tiles = 4
    pair = first // 2
    owners = size // 8
    return pl.pallas_call(
        back_rows_kernel,
        grid=(tiles,),
        in_specs=[
            pl.BlockSpec((2, size, lanes), lambda t: (0, 0, 0)),
            pl.BlockSpec((2, size // tiles, size), lambda t: (pair, t, 0)),
        ],
        out_specs=pl.BlockSpec((owners // tiles, 16, lanes), lambda t: (t, 0, 0)),
        out_shape=jax.ShapeDtypeStruct((owners, 16, lanes), jnp.bfloat16),
        compiler_params=params(),
        cost_estimate=pl.CostEstimate(flops=4_300_000_000, bytes_accessed=8 << 20, transcendentals=0),
        name="back_rows",
    )(field.reshape(2, size, lanes), rows)


def gradient_kernel(place_ref, scales_ref, low_ref, high_ref, zb_ref, wave_low_ref, wave_high_ref, amp_ref, out_ref):
    cells_y, cells_z = amp_ref.shape[1:]
    sum_amp = None
    sum_phase = None
    for member in range(4):
        field_ref = low_ref if member < 2 else high_ref
        wave_ref = wave_low_ref if member < 2 else wave_high_ref
        field = jnp.concatenate([field_ref[member % 2, 0], field_ref[member % 2, 1]], axis=1)
        both = dot(field, zb_ref[member])
        back_real, back_imag = both[:, 0:cells_z], both[:, cells_z : 2 * cells_z]
        wave_real = wave_ref[member % 2, 0, :, 0:cells_z].astype(jnp.float32)
        wave_imag = wave_ref[member % 2, 0, :, cells_z : 2 * cells_z].astype(jnp.float32)
        term_amp = back_real * wave_real - back_imag * wave_imag
        term_phase = scales_ref[member] * (back_real * wave_imag + back_imag * wave_real)
        sum_amp = term_amp if sum_amp is None else sum_amp + term_amp
        sum_phase = term_phase if sum_phase is None else sum_phase + term_phase
    out_ref[0, 0] = (sum_amp / amp_ref[0].astype(jnp.float32)).astype(jnp.bfloat16)
    out_ref[0, 1] = sum_phase.astype(jnp.bfloat16)


def gradient(place, scales, low, high, zb, wave_low, wave_high, amp, first_row, rows):
    _, cells_y, cells_z = amp.shape
    frames = zb.shape[1] // 2
    size = low.shape[2]
    field = pl.BlockSpec((2, 2, size, frames), lambda t, *_: (0, 0, 0, first_row + t))
    wave = pl.BlockSpec((2, 1, cells_y, 2 * cells_z), lambda t, *_: (0, first_row + t, 0, 0))
    return pl.pallas_call(
        gradient_kernel,
        grid_spec=pltpu.PrefetchScalarGridSpec(
            num_scalar_prefetch=2,
            grid=(rows,),
            in_specs=[
                field,
                field,
                pl.BlockSpec(zb.shape, lambda t, *_: (0, 0, 0)),
                wave,
                wave,
                pl.BlockSpec((1, cells_y, cells_z), lambda t, p, *_: (4 * p[0] + first_row + t, 0, 0)),
            ],
            out_specs=pl.BlockSpec((1, 2, cells_y, cells_z), lambda t, *_: (t, 0, 0, 0)),
        ),
        out_shape=jax.ShapeDtypeStruct((rows, 2, cells_y, cells_z), jnp.bfloat16),
        compiler_params=params(),
        cost_estimate=pl.CostEstimate(flops=1_000_000_000 * rows, bytes_accessed=(6 << 20) * rows, transcendentals=0),
        name="gradient",
    )(place, scales, low, high, zb, wave_low, wave_high, amp)


def finish_kernel(place_ref, bragg_ref, sums_ref, amp_ref, disp_ref, *rest):
    new_amp_ref, new_disp_ref = rest[-2:]
    new_amp_ref[0] = amp_ref[0].astype(jnp.float32) - step_size * sums_ref[0, 0].astype(jnp.float32)
    sum_phase = sums_ref[0, 1].astype(jnp.float32)
    for axis in range(3):
        new_disp_ref[axis, 0] = (
            disp_ref[axis, 0].astype(jnp.float32) + (step_size * bragg_ref[axis]) * sum_phase
        ).astype(jnp.bfloat16)


def finish(place, bragg, sums, amp, disp, earlier, first_row, other):
    rows = sums.shape[0]
    _, cells_y, cells_z = amp.shape

    def row(t, p):
        half = 1 - p[0] if other else p[0]
        return 4 * half + first_row + t

    amp_spec = pl.BlockSpec((1, cells_y, cells_z), lambda t, p, *_: (row(t, p), 0, 0))
    disp_spec = pl.BlockSpec((3, 1, cells_y, cells_z), lambda t, p, *_: (0, row(t, p), 0, 0))
    kept = [] if earlier is None else list(earlier)
    return pl.pallas_call(
        finish_kernel,
        grid_spec=pltpu.PrefetchScalarGridSpec(
            num_scalar_prefetch=2,
            grid=(rows,),
            in_specs=[
                pl.BlockSpec((1, 2, cells_y, cells_z), lambda t, *_: (t, 0, 0, 0)),
                amp_spec,
                disp_spec,
            ]
            + [pl.BlockSpec(memory_space=pl.ANY)] * len(kept),
            out_specs=[amp_spec, disp_spec],
        ),
        out_shape=[
            jax.ShapeDtypeStruct(amp.shape, jnp.float32),
            jax.ShapeDtypeStruct(disp.shape, jnp.bfloat16),
        ],
        input_output_aliases={} if earlier is None else {5: 0, 6: 1},
        compiler_params=params(),
        cost_estimate=pl.CostEstimate(flops=10_000_000, bytes_accessed=(3 << 20) * rows, transcendentals=0),
        name="finish",
    )(place, bragg, sums, amp, disp, *kept)


def exchange(blocks):
    return lax.all_to_all(blocks, both_axes, split_axis=0, concat_axis=0, tiled=True)


def swap(values):
    return lax.ppermute(values, "spec", [(0, 1), (1, 0)])


def per_device(amplitude, displacement, support, counts, bin_weights, bin_scales, bragg_vector):
    place = lax.axis_index("spec").reshape(1).astype(jnp.int32)
    size, rows_y, frames = counts.shape
    cells_z = amplitude.shape[2]
    rows, zf, zb = row_matrices(bin_scales, size, cells_z, frames)
    waves, sent = [], []
    for first in (0, 2):
        wave, blocks = forward(
            place, bragg_vector, bin_scales, displacement, amplitude, support, zf, rows, first
        )
        waves.append(wave)
        sent.append(exchange(blocks))
    cols = column_matrices(bin_scales, size)
    my_counts = lax.dynamic_slice_in_dim(counts, place[0] * (rows_y // 2), rows_y // 2, axis=1)
    my_counts = my_counts.reshape(size, rows_y // 2 * frames)
    far = [apply_columns(sent[k], cols, 2 * k, jnp.float32) for k in range(2)]
    fields = back_fields(bin_weights, far[0], far[1], my_counts)
    returned = [exchange(back_rows(fields[k], rows, 2 * k)) for k in range(2)]
    back = [apply_columns(returned[k], cols, 2 * k, jnp.bfloat16) for k in range(2)]
    outs = None
    sums = []
    for first_row in (0, 2):
        part = gradient(
            place, bin_scales, back[0], back[1], zb, waves[0], waves[1], amplitude, first_row, 2
        )
        sums.append((part, swap(part)))
    for other in (False, True):
        for k in range(2):
            outs = finish(
                place, bragg_vector, sums[k][other], amplitude, displacement, outs, 2 * k, other
            )
    return tuple(outs)


def solution(mesh):
    in_specs = (
        P("slab", None, None),
        P(None, "slab", None, None),
        P("slab", None, None),
        P(None, "slab", None),
        P(),
        P(),
        P(),
    )
    out_specs = (P("slab", None, None), P(None, "slab", None, None))
    return jax.shard_map(
        per_device, mesh=mesh, in_specs=in_specs, out_specs=out_specs, check_vma=False
    )
```

time: 511 us -> 263 us (0.51)
  other arithmetic: 138 us -> 0 us
  waiting for transfers between devices: 237 us -> 105 us
  Pallas kernels: 0 us -> 125 us
  matrix products: 52.8 us -> 0 us
  starting transfers between devices: 44.5 us -> 26.7 us
  local copies, waits for them, and re-layouts: 20.2 us -> 3.86 us
  between operations: 15.7 us -> 0.73 us
    psum x2 -> x0, waiting for transfers between devices: 152 us -> none  [the longest x1 110 us: per_device(): lax.psum(jnp.stack([part_amp, part_phase]).astype(jnp.bfloat16), 'spec')]
    pallas_call x0 -> x17, Pallas kernels: none -> 125 us  [the longest x4 31.4 us: apply_columns(): pl.pallas_call(functools.partial(far_kernel, frames=frames), grid=(tiles,...]
    another operation x8 -> x0, other arithmetic: 101 us -> none  [the longest x2 50.8 us: per_device(): jnp.stack([magnitude * jnp.cos(bin_phase), magnitude * jnp.sin(bin_phase)])]
    dot_general x8 -> x0, matrix products: 52.8 us -> none  [the longest x2 17.9 us: per_device(): jnp.einsum('oxyk,okpn->pxyn', back_two, matrices[member][0], preferred_el...]
    ppermute x0 -> x2, waiting for transfers between devices: none -> 27.7 us  [swap(): return lax.ppermute(values, 'spec', [(0, 1), (1, 0)])]
    convert_element_type x3 -> x0, other arithmetic: 19.5 us -> none  [the longest x1 8.57 us: finish(): new_displacement = (disp_values - step_size * bragg_vector[:, None, None,...]
    all_to_all x4, starting transfers between devices: 44.4 us -> 25.3 us  [exchange(): lax.all_to_all(blocks, both_axes, split_axis=0, concat_axis=0, tiled=True)]
    mul x3 -> x0, other arithmetic: 14.5 us -> none  [the longest x1 8.24 us: finish(): grad_phase = -mask_values * amp_values * sum_phase]
  transfers between devices with their start and end apart: 6 -> 6, of which waited for: 6 -> 6; matrix products, arithmetic and copies ran while one was open for 7% -> 1% of each run, Pallas kernels for 0% -> 23%
where the time goes in v1:
time: 263 us; the launch traced here: 262 us
  Pallas kernels  125 us (48%)
  waiting for transfers between devices  105 us (40%)
  starting transfers between devices  26.7 us (10%)
  local copies, waits for them, and re-layouts  3.86 us (1%)
    all_to_all x4, waiting for transfers between devices, exchange(): lax.all_to_all(blocks, both_axes, split_axis=0, concat_axis=0, tiled=True)  77.7 us
    pallas_call x4, Pallas kernels, apply_columns(): pl.pallas_call(functools.partial(far_kernel, frames=frames), grid=(tiles,...  31.4 us
    pallas_call x2, Pallas kernels, forward(): pl.pallas_call(functools.partial(forward_kernel, first=first), grid_spec=...  27.8 us
    ppermute x2, waiting for transfers between devices, swap(): return lax.ppermute(values, 'spec', [(0, 1), (1, 0)])  27.7 us
    all_to_all x4, starting transfers between devices, exchange(): lax.all_to_all(blocks, both_axes, split_axis=0, concat_axis=0, tiled=True)  25.3 us
    pallas_call x4, Pallas kernels, finish(): pl.pallas_call(finish_kernel, grid_spec=pltpu.PrefetchScalarGridSpec(num_...  15.2 us
    pallas_call x2, Pallas kernels, back_rows(): pl.pallas_call(back_rows_kernel, grid=(tiles,), in_specs=[pl.BlockSpec((2...  12.8 us
    pallas_call x2, Pallas kernels, gradient(): pl.pallas_call(gradient_kernel, grid_spec=pltpu.PrefetchScalarGridSpec(nu...  11.7 us
  transfers between devices with their start and end apart: 6, of which 6 were waited for; matrix products, arithmetic and copies ran while one was open for 1% of the time, Pallas kernels for 23%

profile of v1, /device:TPU:1, one launch (start us, length us, event | category | flops | bytes accessed | tf_op | source)
XLA Modules:
  0.0 261.8 jit_solution(10155270086387642706)
XLA Ops:
  0.6 0.0 copy-start
  0.7 10.2 %row_matrices.1 = (bf16[4,1024,1024]{2,1,0:T(8,128)(2,1)}, bf16[4,512,256]{2,1,0:T(8,128)(2,1)}, bf16[4,256,512]{2,1,0:T(8,128)(2,1)}) custom-call(f32[4]{0:T(128)} %scales_ref.11), custom_call_target="tpu_custom_call" | custom-call | tf_op jit(solution)/shard_map/row_matrices/pallas_call | solution.py:97
  10.8 13.9 %forward_z_y.3 = (bf16[2,4,512,512]{3,2,1,0:T(8,128)(2,1)}, bf16[128,16,512]{2,1,0:T(8,128)(2,1)}) custom-call(s32[1]{0:T(128)} %bitcast.place_ref, f32[3]{0:T(128)} %bragg_ref.11, f32[4]{0:T(128)} %scales_ref.11, bf16[3,8,512,256]{3,2,1,0:T(8,128)(2,1)} %disp_ref.11, bf16[8,512,256]{2,1,0:T(8,128)(2,1)} %amp_ref.15, s32[8,512,256]{2,1,0:T(8,128)} %mask_ref.3, ...), custom_call_target="tpu_custom_call" | custom-call | flops 6600000000 | bytes 20971520 | tf_op jit(solution)/shard_map/forward_z_y/pallas_call | solution.py:201
  24.7 12.0 %all-to-all-start.1 = ((bf16[128,16,512]{2,1,0:T(8,128)(2,1)}), bf16[128,16,512]{2,1,0:T(8,128)(2,1)}, u32[]{:S(2)}, u32[]{:S(2)}) async-start(bf16[128,16,512]{2,1,0:T(8,128)(2,1)} %get-tuple-element.20), calls=%async_computation.1 | async-start | bytes 4194304 | tf_op jit(solution)/shard_map/all_to_all | solution.py:436
  36.7 13.9 %forward_z_y.2 = (bf16[2,4,512,512]{3,2,1,0:T(8,128)(2,1)}, bf16[128,16,512]{2,1,0:T(8,128)(2,1)}) custom-call(s32[1]{0:T(128)} %bitcast.place_ref, f32[3]{0:T(128)} %bragg_ref.11, f32[4]{0:T(128)} %scales_ref.11, bf16[3,8,512,256]{3,2,1,0:T(8,128)(2,1)} %disp_ref.11, bf16[8,512,256]{2,1,0:T(8,128)(2,1)} %amp_ref.15, s32[8,512,256]{2,1,0:T(8,128)} %mask_ref.3, ...), custom_call_target="tpu_custom_call" | custom-call | flops 6600000000 | bytes 20971520 | tf_op jit(solution)/shard_map/forward_z_y/pallas_call | solution.py:201
  50.6 16.7 %all-to-all-done.1.got_ref = bf16[128,16,512]{2,1,0:T(8,128)(2,1)} async-done(((bf16[128,16,512]{2,1,0:T(8,128)(2,1)}), bf16[128,16,512]{2,1,0:T(8,128)(2,1)}, u32[]{:S(2)}, u32[]{:S(2)}) %all-to-all-start.1) | async-done | bytes 2097184 | tf_op jit(solution)/shard_map/all_to_all | solution.py:436
  67.3 4.7 %all-to-all-start = ((bf16[128,16,512]{2,1,0:T(8,128)(2,1)}), bf16[128,16,512]{2,1,0:T(8,128)(2,1)}, u32[]{:S(2)}, u32[]{:S(2)}) async-start(bf16[128,16,512]{2,1,0:T(8,128)(2,1)} %get-tuple-element.19), calls=%async_computation | async-start | bytes 4194304 | tf_op jit(solution)/shard_map/all_to_all | solution.py:436
  72.1 0.0 copy-done
  72.1 0.2 constant_dynamic-slice_fusion
  72.3 0.4 copy.17
  72.7 1.3 copy.16.counts_ref
  74.0 7.8 %column_matrices.1.cols_ref = bf16[4,2,512,1024]{3,2,1,0:T(8,128)(2,1)} custom-call(f32[4]{0:T(128)} %scales_ref.11), custom_call_target="tpu_custom_call" | custom-call | flops 8000000000 | bytes 8388608 | tf_op jit(solution)/shard_map/column_matrices/pallas_call | solution.py:139
  81.7 8.0 %apply_columns.5.high_ref = f32[2,2,512,512]{3,2,1,0:T(8,128)} custom-call(bf16[128,16,512]{2,1,0:T(8,128)(2,1)} %all-to-all-done.1.got_ref, bf16[4,2,512,1024]{3,2,1,0:T(8,128)(2,1)} %column_matrices.1.cols_ref), custom_call_target="tpu_custom_call" | custom-call | flops 4300000256 | bytes 12582912 | tf_op jit(solution)/shard_map/apply_columns/pallas_call | solution.py:261
  89.8 13.1 %all-to-all-done.got_ref = bf16[128,16,512]{2,1,0:T(8,128)(2,1)} async-done(((bf16[128,16,512]{2,1,0:T(8,128)(2,1)}), bf16[128,16,512]{2,1,0:T(8,128)(2,1)}, u32[]{:S(2)}, u32[]{:S(2)}) %all-to-all-start) | async-done | bytes 2097184 | tf_op jit(solution)/shard_map/all_to_all | solution.py:436
  102.9 8.0 %apply_columns.4.low_ref = f32[2,2,512,512]{3,2,1,0:T(8,128)} custom-call(bf16[128,16,512]{2,1,0:T(8,128)(2,1)} %all-to-all-done.got_ref, bf16[4,2,512,1024]{3,2,1,0:T(8,128)(2,1)} %column_matrices.1.cols_ref), custom_call_target="tpu_custom_call" | custom-call | flops 4300000256 | bytes 12582912 | tf_op jit(solution)/shard_map/apply_columns/pallas_call | solution.py:261
  110.9 8.3 %back_fields.1 = (bf16[2,2,512,512]{3,2,1,0:T(8,128)(2,1)}, bf16[2,2,512,512]{3,2,1,0:T(8,128)(2,1)}) custom-call(f32[4]{0:T(128)} %weights_ref.1, f32[2,2,512,512]{3,2,1,0:T(8,128)} %apply_columns.4.low_ref, f32[2,2,512,512]{3,2,1,0:T(8,128)} %apply_columns.5.high_ref, s32[512,512]{1,0:T(8,128)} %copy.16.counts_ref), custom_call_target="tpu_custom_call" | custom-call | tf_op jit(solution)/shard_map/back_fields/pallas_call | solution.py:297
  119.2 6.4 %back_rows.3 = bf16[128,16,512]{2,1,0:T(8,128)(2,1)} custom-call(bf16[2,1024,512]{2,1,0:T(8,128)(2,1)} %bitcast.6, bf16[4,1024,1024]{2,1,0:T(8,128)(2,1)} %get-tuple-element.18.rows_ref), custom_call_target="tpu_custom_call" | custom-call | flops 4300000256 | bytes 8388608 | tf_op jit(solution)/shard_map/back_rows/pallas_call | solution.py:327
  125.6 3.8 %all-to-all-start.3 = ((bf16[128,16,512]{2,1,0:T(8,128)(2,1)}), bf16[128,16,512]{2,1,0:T(8,128)(2,1)S(1)}, u32[]{:S(2)}, u32[]{:S(2)}) async-start(bf16[128,16,512]{2,1,0:T(8,128)(2,1)} %back_rows.3), calls=%async_computation.3 | async-start | bytes 4194304 | tf_op jit(solution)/shard_map/all_to_all | solution.py:436
  129.4 6.4 %back_rows.2 = bf16[128,16,512]{2,1,0:T(8,128)(2,1)} custom-call(bf16[2,1024,512]{2,1,0:T(8,128)(2,1)} %bitcast.5, bf16[4,1024,1024]{2,1,0:T(8,128)(2,1)} %get-tuple-element.18.rows_ref), custom_call_target="tpu_custom_call" | custom-call | flops 4300000256 | bytes 8388608 | tf_op jit(solution)/shard_map/back_rows/pallas_call | solution.py:327
  135.8 24.8 %all-to-all-done.3.got_ref = bf16[128,16,512]{2,1,0:T(8,128)(2,1)S(1)} async-done(((bf16[128,16,512]{2,1,0:T(8,128)(2,1)}), bf16[128,16,512]{2,1,0:T(8,128)(2,1)S(1)}, u32[]{:S(2)}, u32[]{:S(2)}) %all-to-all-start.3) | async-done | bytes 2097184 | tf_op jit(solution)/shard_map/all_to_all | solution.py:436
  160.6 0.0 copy-start.2
  160.6 4.8 %all-to-all-start.2 = ((bf16[128,16,512]{2,1,0:T(8,128)(2,1)}), bf16[128,16,512]{2,1,0:T(8,128)(2,1)}, u32[]{:S(2)}, u32[]{:S(2)}) async-start(bf16[128,16,512]{2,1,0:T(8,128)(2,1)} %back_rows.2), calls=%async_computation.2 | async-start | bytes 4194304 | tf_op jit(solution)/shard_map/all_to_all | solution.py:436
  165.4 0.0 copy-done.2
  165.4 7.7 %apply_columns.7.high_ref = bf16[2,2,512,512]{3,2,1,0:T(8,128)(2,1)} custom-call(bf16[128,16,512]{2,1,0:T(8,128)(2,1)} %copy-done.2, bf16[4,2,512,1024]{3,2,1,0:T(8,128)(2,1)} %column_matrices.1.cols_ref), custom_call_target="tpu_custom_call" | custom-call | flops 4300000256 | bytes 12582912 | tf_op jit(solution)/shard_map/apply_columns/pallas_call | solution.py:261
  173.1 23.1 %all-to-all-done.2.got_ref = bf16[128,16,512]{2,1,0:T(8,128)(2,1)} async-done(((bf16[128,16,512]{2,1,0:T(8,128)(2,1)}), bf16[128,16,512]{2,1,0:T(8,128)(2,1)}, u32[]{:S(2)}, u32[]{:S(2)}) %all-to-all-start.2) | async-done | bytes 2097184 | tf_op jit(solution)/shard_map/all_to_all | solution.py:436
  196.2 7.7 %apply_columns.6.low_ref = bf16[2,2,512,512]{3,2,1,0:T(8,128)(2,1)} custom-call(bf16[128,16,512]{2,1,0:T(8,128)(2,1)} %all-to-all-done.2.got_ref, bf16[4,2,512,1024]{3,2,1,0:T(8,128)(2,1)} %column_matrices.1.cols_ref), custom_call_target="tpu_custom_call" | custom-call | flops 4300000256 | bytes 12582912 | tf_op jit(solution)/shard_map/apply_columns/pallas_call | solution.py:261
  203.8 5.9 %gradient.3.sums_ref = bf16[2,2,512,256]{3,2,1,0:T(8,128)(2,1)} custom-call(s32[1]{0:T(128)} %bitcast.place_ref, f32[4]{0:T(128)} %scales_ref.11, bf16[2,2,512,512]{3,2,1,0:T(8,128)(2,1)} %apply_columns.6.low_ref, bf16[2,2,512,512]{3,2,1,0:T(8,128)(2,1)} %apply_columns.7.high_ref, bf16[4,256,512]{2,1,0:T(8,128)(2,1)} %get-tuple-element.23.zb_ref, ...), custom_call_target="tpu_custom_call" | custom-call | flops 2000000000 | bytes 12582912 | tf_op jit(solution)/shard_map/gradient/pallas_call | solution.py:368
  209.7 0.4 collective-permute-start.1
  210.0 5.8 %gradient.2.sums_ref = bf16[2,2,512,256]{3,2,1,0:T(8,128)(2,1)} custom-call(s32[1]{0:T(128)} %bitcast.place_ref, f32[4]{0:T(128)} %scales_ref.11, bf16[2,2,512,512]{3,2,1,0:T(8,128)(2,1)} %apply_columns.6.low_ref, bf16[2,2,512,512]{3,2,1,0:T(8,128)(2,1)} %apply_columns.7.high_ref, bf16[4,256,512]{2,1,0:T(8,128)(2,1)} %get-tuple-element.23.zb_ref, ...), custom_call_target="tpu_custom_call" | custom-call | flops 2000000000 | bytes 12582912 | tf_op jit(solution)/shard_map/gradient/pallas_call | solution.py:368
  215.9 1.1 collective-permute-start
  217.0 3.8 %finish.4 = (f32[8,512,256]{2,1,0:T(8,128)}, bf16[3,8,512,256]{3,2,1,0:T(8,128)(2,1)}) custom-call(s32[1]{0:T(128)} %bitcast.place_ref, f32[3]{0:T(128)} %bragg_ref.11, bf16[2,2,512,256]{3,2,1,0:T(8,128)(2,1)} %gradient.3.sums_ref, bf16[8,512,256]{2,1,0:T(8,128)(2,1)} %amp_ref.15, bf16[3,8,512,256]{3,2,1,0:T(8,128)(2,1)} %disp_ref.11), custom_call_target="tpu_custom_call" | custom-call | flops 10000000 | bytes 6291456 | tf_op jit(solution)/shard_map/finish/pallas_call | solution.py:411
  220.7 3.8 %finish.5 = (f32[8,512,256]{2,1,0:T(8,128)}, bf16[3,8,512,256]{3,2,1,0:T(8,128)(2,1)}) custom-call(s32[1]{0:T(128)} %bitcast.place_ref, f32[3]{0:T(128)} %bragg_ref.11, bf16[2,2,512,256]{3,2,1,0:T(8,128)(2,1)} %gradient.2.sums_ref, bf16[8,512,256]{2,1,0:T(8,128)(2,1)} %amp_ref.15, ...), custom_call_target="tpu_custom_call", output_to_operand_aliasing={{0}: (5, {}), {1}: (6, {})} | custom-call | flops 10000000 | bytes 6291456 | tf_op jit(solution)/shard_map/finish/pallas_call | solution.py:411
  224.5 9.9 %collective-permute-done.1.sums_ref = bf16[2,2,512,256]{3,2,1,0:T(8,128)(2,1)S(1)} collective-permute-done((bf16[2,2,512,256]{3,2,1,0:T(8,128)(2,1)}, bf16[2,2,512,256]{3,2,1,0:T(8,128)(2,1)S(1)}, u32[]{:S(2)}, u32[]{:S(2)}) %collective-permute-start.1) | collective-permute-done | bytes 1048608 | tf_op jit(solution)/shard_map/ppermute | solution.py:440
  234.4 0.0 copy-start.4
  234.4 1.0 copy-done.4
  235.4 3.8 %finish.6 = (f32[8,512,256]{2,1,0:T(8,128)}, bf16[3,8,512,256]{3,2,1,0:T(8,128)(2,1)}) custom-call(s32[1]{0:T(128)} %bitcast.place_ref, f32[3]{0:T(128)} %bragg_ref.11, bf16[2,2,512,256]{3,2,1,0:T(8,128)(2,1)} %copy-done.4, bf16[8,512,256]{2,1,0:T(8,128)(2,1)} %amp_ref.15, ...), custom_call_target="tpu_custom_call", output_to_operand_aliasing={{0}: (5, {}), {1}: (6, {})} | custom-call | flops 10000000 | bytes 6291456 | tf_op jit(solution)/shard_map/finish/pallas_call | solution.py:411
  239.2 17.7 %collective-permute-done.sums_ref = bf16[2,2,512,256]{3,2,1,0:T(8,128)(2,1)S(1)} collective-permute-done((bf16[2,2,512,256]{3,2,1,0:T(8,128)(2,1)}, bf16[2,2,512,256]{3,2,1,0:T(8,128)(2,1)S(1)}, u32[]{:S(2)}, u32[]{:S(2)}) %collective-permute-start) | collective-permute-done | bytes 1048608 | tf_op jit(solution)/shard_map/ppermute | solution.py:440
  256.9 0.0 copy-start.3
  256.9 1.0 copy-done.3
  257.9 0.0 copy-start.1
  257.9 3.9 %finish.7 = (f32[8,512,256]{2,1,0:T(8,128)}, bf16[3,8,512,256]{3,2,1,0:T(8,128)(2,1)}) custom-call(s32[1]{0:T(128)} %bitcast.place_ref, f32[3]{0:T(128)} %bragg_ref.11, bf16[2,2,512,256]{3,2,1,0:T(8,128)(2,1)} %copy-done.3, bf16[8,512,256]{2,1,0:T(8,128)(2,1)} %amp_ref.15, ...), custom_call_target="tpu_custom_call", output_to_operand_aliasing={{0}: (5, {}), {1}: (6, {})} | custom-call | flops 10000000 | bytes 6291456 | tf_op jit(solution)/shard_map/finish/pallas_call | solution.py:411
  261.8 0.0 copy-done.1
Async XLA Ops:
  0.6 71.5 %copy-start = (s32[512,8,128]{2,1,0:T(8,128)S(1)}, s32[512,8,128]{2,1,0:T(8,128)}, u32[]{:S(2)}) copy-start(s32[512,8,128]{2,1,0:T(8,128)} %param.10) | copy-start | bytes 6291460
  24.7 42.6 %all-to-all-start.1 = ((bf16[128,16,512]{2,1,0:T(8,128)(2,1)}), bf16[128,16,512]{2,1,0:T(8,128)(2,1)}, u32[]{:S(2)}, u32[]{:S(2)}) async-start(bf16[128,16,512]{2,1,0:T(8,128)(2,1)} %get-tuple-element.20), calls=%async_computation.1 | async-start | bytes 4194304 | tf_op jit(solution)/shard_map/all_to_all | solution.py:436
  67.3 35.5 %all-to-all-start = ((bf16[128,16,512]{2,1,0:T(8,128)(2,1)}), bf16[128,16,512]{2,1,0:T(8,128)(2,1)}, u32[]{:S(2)}, u32[]{:S(2)}) async-start(bf16[128,16,512]{2,1,0:T(8,128)(2,1)} %get-tuple-element.19), calls=%async_computation | async-start | bytes 4194304 | tf_op jit(solution)/shard_map/all_to_all | solution.py:436
  125.6 35.0 %all-to-all-start.3 = ((bf16[128,16,512]{2,1,0:T(8,128)(2,1)}), bf16[128,16,512]{2,1,0:T(8,128)(2,1)S(1)}, u32[]{:S(2)}, u32[]{:S(2)}) async-start(bf16[128,16,512]{2,1,0:T(8,128)(2,1)} %back_rows.3), calls=%async_computation.3 | async-start | bytes 4194304 | tf_op jit(solution)/shard_map/all_to_all | solution.py:436
  160.6 4.8 %copy-start.2 = (bf16[128,16,512]{2,1,0:T(8,128)(2,1)}, bf16[128,16,512]{2,1,0:T(8,128)(2,1)S(1)}, u32[]{:S(2)}) copy-start(bf16[128,16,512]{2,1,0:T(8,128)(2,1)S(1)} %all-to-all-done.3.got_ref) | copy-start | bytes 6291460
  160.6 35.6 %all-to-all-start.2 = ((bf16[128,16,512]{2,1,0:T(8,128)(2,1)}), bf16[128,16,512]{2,1,0:T(8,128)(2,1)}, u32[]{:S(2)}, u32[]{:S(2)}) async-start(bf16[128,16,512]{2,1,0:T(8,128)(2,1)} %back_rows.2), calls=%async_computation.2 | async-start | bytes 4194304 | tf_op jit(solution)/shard_map/all_to_all | solution.py:436
  209.7 24.8 %collective-permute-start.1 = (bf16[2,2,512,256]{3,2,1,0:T(8,128)(2,1)}, bf16[2,2,512,256]{3,2,1,0:T(8,128)(2,1)S(1)}, u32[]{:S(2)}, u32[]{:S(2)}) collective-permute-start(bf16[2,2,512,256]{3,2,1,0:T(8,128)(2,1)} %gradient.3.sums_ref), channel_id=1, source_target_pairs={{0,64},{64,0},{1,65},{65,1},{2,66},{66,2},{3,67},{67,3},{4,68},{68... | collective-permute-start | bytes 3145736 | tf_op jit(solution)/shard_map/ppermute | solution.py:440
  215.9 41.0 %collective-permute-start = (bf16[2,2,512,256]{3,2,1,0:T(8,128)(2,1)}, bf16[2,2,512,256]{3,2,1,0:T(8,128)(2,1)S(1)}, u32[]{:S(2)}, u32[]{:S(2)}) collective-permute-start(bf16[2,2,512,256]{3,2,1,0:T(8,128)(2,1)} %gradient.2.sums_ref), channel_id=1, source_target_pairs={{0,64},{64,0},{1,65},{65,1},{2,66},{66,2},{3,67},{67,3},{4,68},{68... | collective-permute-start | bytes 3145736 | tf_op jit(solution)/shard_map/ppermute | solution.py:440
  234.4 1.0 copy-start.4
  256.9 1.0 copy-start.3
  257.9 3.9 %copy-start.1 = (s32[512,8,128]{2,1,0:T(8,128)S(1)}, s32[512,8,128]{2,1,0:T(8,128)}, u32[]{:S(2)}) copy-start(s32[512,8,128]{2,1,0:T(8,128)} %param.10) | copy-start | bytes 6291460

commit v2 on v0

v2 whole, which is shorter than its diff:
```python
import functools
import math

import jax
import jax.numpy as jnp
from jax import lax
from jax.experimental import pallas as pl
from jax.experimental.pallas import tpu as pltpu
from jax.sharding import PartitionSpec as P

step_size = 0.5
both_axes = ("slab", "spec")
vmem_limit = 60 * 1024 * 1024
small_limit = 36 * 1024 * 1024
cos_terms = (
    0.9999992117703129, -19.738980419471183, 64.92865850463387,
    -85.27162830147759, 58.7905066287335, -21.071108461812614,
)
sin_terms = (
    6.283184916984337, -41.34158926418227, 81.59994386457431,
    -76.61447586037943, 41.342889429509576, -12.4712447471884,
)


wave_cos_terms = (
    0.9999590619701949, -19.73094403547976, 64.67145824268955,
    -82.39085380484792, 45.6210638400798,
)
wave_sin_terms = (
    6.283161153735962, -41.33683281238831, 81.44771611530231,
    -74.90944720114622, 33.548361462485595,
)


def cos_sin_turns(turns, cos_series=cos_terms, sin_series=sin_terms):
    rest = turns - jnp.floor(turns + 0.5)
    square = rest * rest
    cosine = jnp.full_like(square, cos_series[-1])
    sine = jnp.full_like(square, sin_series[-1])
    for level in range(len(cos_series) - 2, -1, -1):
        cosine = cosine * square + cos_series[level]
        sine = sine * square + sin_series[level]
    return cosine, sine * rest


def chirp_parts(out_index, in_index, count_out, count_in, bin_scale):
    product = (out_index - count_out // 2) * (in_index - count_in // 2)
    fraction = (product & (count_in - 1)).astype(jnp.float32) * (1.0 / count_in)
    excess = (bin_scale - 1.0) * (product.astype(jnp.float32) * (1.0 / count_in))
    cosine, sine = cos_sin_turns(fraction + excess)
    normalizer = 1.0 / math.sqrt(count_in)
    return cosine * normalizer, sine * -normalizer


def iota(shape, dim):
    return lax.broadcasted_iota(jnp.int32, shape, dim)


def dot(a, b):
    return jnp.dot(a, b, preferred_element_type=jnp.float32)


def params(limit=vmem_limit):
    return pltpu.CompilerParams(vmem_limit_bytes=limit)


def small_table(index, stride, others, size, bin_scale):
    product = stride * index * others
    fraction = (product & (size - 1)).astype(jnp.float32) * (1.0 / size)
    excess = (bin_scale - 1.0) * (product.astype(jnp.float32) * (1.0 / size))
    cosine, sine = cos_sin_turns(fraction + excess)
    return cosine, -sine


def fill_tables(big_real, big_imag, lane_index, size, bin_scale):
    others = lane_index - size // 2
    wide = (size // 8, size)
    real, imag = small_table(iota(wide, 0) - size // 16, 8, jnp.broadcast_to(others, wide), size, bin_scale)
    normalizer = 1.0 / math.sqrt(size)
    big_real[...] = real * normalizer
    big_imag[...] = imag * normalizer
    narrow = (8, size)
    return small_table(iota(narrow, 0), 1, jnp.broadcast_to(others, narrow), size, bin_scale)


def table_rows(big_real, big_imag, small, step):
    real = jnp.broadcast_to(big_real[pl.ds(step, 1), :], small[0].shape)
    imag = jnp.broadcast_to(big_imag[pl.ds(step, 1), :], small[0].shape)
    return real * small[0] - imag * small[1], real * small[1] + imag * small[0]


def fill_z(zf_ref, member, bin_scale, cells_z, frames):
    real, imag = chirp_parts(
        iota((cells_z, frames), 1), iota((cells_z, frames), 0), frames, cells_z, bin_scale
    )
    zf_ref[member, 0:cells_z, 0:frames] = real.astype(jnp.bfloat16)
    zf_ref[member, 0:cells_z, frames : 2 * frames] = imag.astype(jnp.bfloat16)
    zf_ref[member, cells_z : 2 * cells_z, 0:frames] = (-imag).astype(jnp.bfloat16)
    zf_ref[member, cells_z : 2 * cells_z, frames : 2 * frames] = real.astype(jnp.bfloat16)


def row_matrices_kernel(scales_ref, rows_ref, big_real, big_imag, *, size):
    bin_scale = scales_ref[pl.program_id(0)]
    small = fill_tables(big_real, big_imag, iota((1, size), 1), size, bin_scale)
    low = (iota((8, size), 0) & 2) == 0

    def body(step, carry):
        halves = [[[], []], [[], []]]
        for sub in range(2):
            real, imag = table_rows(big_real, big_imag, small, 2 * step + sub)
            for column, (first, second) in enumerate(((real, imag), (-imag, real))):
                halves[0][column].append(jnp.where(low, first, pltpu.roll(second, 2, 0)))
                halves[1][column].append(jnp.where(low, pltpu.roll(first, 6, 0), second))
        at = pl.ds(pl.multiple_of(16 * step, 16), 16)
        for half in range(2):
            for column in range(2):
                rows_ref[0, half, at, column * size : (column + 1) * size] = jnp.concatenate(
                    halves[half][column], axis=0
                ).astype(jnp.bfloat16)
        return carry

    lax.fori_loop(0, size // 16, body, 0)


def row_matrices(bin_scales, size):
    bins = bin_scales.shape[0]
    return pl.pallas_call(
        functools.partial(row_matrices_kernel, size=size),
        grid=(bins,),
        in_specs=[pl.BlockSpec(memory_space=pltpu.SMEM)],
        out_specs=pl.BlockSpec((1, 2, size, 2 * size), lambda b: (b, 0, 0, 0)),
        out_shape=jax.ShapeDtypeStruct((bins, 2, size, 2 * size), jnp.bfloat16),
        scratch_shapes=[pltpu.VMEM((size // 8, size), jnp.float32)] * 2,
        compiler_params=params(),
        cost_estimate=pl.CostEstimate(flops=4_000_000_000, bytes_accessed=8 << 20, transcendentals=0),
        name="row_matrices",
    )(bin_scales)


def column_matrices_kernel(scales_ref, cols_ref, zb_ref, big_real, big_imag, *, size, cells_z, frames):
    bin_scale = scales_ref[pl.program_id(0)]
    owners = size // 4
    lane = iota((1, size), 1)
    small = fill_tables(big_real, big_imag, 4 * (lane % owners) + lane // owners, size, bin_scale)
    wide = size // 2

    def body(step, carry):
        pairs = [table_rows(big_real, big_imag, small, 2 * step + sub) for sub in range(2)]
        real = jnp.concatenate([pair[0] for pair in pairs], axis=0)
        imag = jnp.concatenate([pair[1] for pair in pairs], axis=0)
        at = pl.ds(pl.multiple_of(16 * step, 16), 16)
        for part, (first, second) in enumerate(((real, -imag), (imag, real))):
            for half in range(2):
                lanes = slice(half * wide, (half + 1) * wide)
                cols_ref[0, part, at, 2 * half * wide : (2 * half + 1) * wide] = first[:, lanes].astype(jnp.bfloat16)
                cols_ref[0, part, at, (2 * half + 1) * wide : (2 * half + 2) * wide] = second[:, lanes].astype(jnp.bfloat16)
        return carry

    lax.fori_loop(0, size // 16, body, 0)
    real, imag = chirp_parts(
        iota((frames, cells_z), 0), iota((frames, cells_z), 1), frames, cells_z, bin_scale
    )
    zb_ref[0, 0:frames, 0:cells_z] = real.astype(jnp.bfloat16)
    zb_ref[0, 0:frames, cells_z : 2 * cells_z] = imag.astype(jnp.bfloat16)
    zb_ref[0, frames : 2 * frames, 0:cells_z] = (-imag).astype(jnp.bfloat16)
    zb_ref[0, frames : 2 * frames, cells_z : 2 * cells_z] = real.astype(jnp.bfloat16)


def column_matrices(bin_scales, size, cells_z, frames):
    bins = bin_scales.shape[0]
    return pl.pallas_call(
        functools.partial(column_matrices_kernel, size=size, cells_z=cells_z, frames=frames),
        grid=(bins,),
        in_specs=[pl.BlockSpec(memory_space=pltpu.SMEM)],
        out_specs=[
            pl.BlockSpec((1, 2, size, 2 * size), lambda b: (b, 0, 0, 0)),
            pl.BlockSpec((1, 2 * frames, 2 * cells_z), lambda b: (b, 0, 0)),
        ],
        out_shape=[
            jax.ShapeDtypeStruct((bins, 2, size, 2 * size), jnp.bfloat16),
            jax.ShapeDtypeStruct((bins, 2 * frames, 2 * cells_z), jnp.bfloat16),
        ],
        scratch_shapes=[pltpu.VMEM((size // 8, size), jnp.float32)] * 2,
        compiler_params=params(),
        cost_estimate=pl.CostEstimate(flops=4_000_000_000, bytes_accessed=8 << 20, transcendentals=0),
        name="column_matrices",
    )(bin_scales)


def pack_owners(values, out_ref, place):
    lanes = out_ref.shape[2]
    tile = 8

    def body(step, carry):
        at = pl.ds(pl.multiple_of(step * 4 * tile, 4 * tile), 4 * tile)
        rows = [values(member, at).reshape(tile // 2, 8, lanes) for member in range(4)]
        low = iota(rows[0].shape, 1) < 4
        even, odd = [], []
        for first, second in ((rows[0], rows[1]), (rows[2], rows[3])):
            even.append(jnp.where(low, first, pltpu.roll(second, 4, 1)))
            odd.append(jnp.where(low, pltpu.roll(first, 4, 1), second))
        even = jnp.concatenate(even, axis=1)
        odd = jnp.concatenate(odd, axis=1)
        both = jnp.stack([even, odd], axis=1).reshape(tile, 16, lanes)
        out_ref[pl.ds(step * tile, tile), pl.ds(place, 16), :] = both.astype(jnp.bfloat16)
        return carry

    lax.fori_loop(0, out_ref.shape[0] // tile, body, 0)


def wave_chunk(bragg_ref, scales_ref, disp_ref, amp_ref, mask_ref, row, at, use):
    phase = (
        bragg_ref[0] * disp_ref[0, row, at, :].astype(jnp.float32)
        + bragg_ref[1] * disp_ref[1, row, at, :].astype(jnp.float32)
        + bragg_ref[2] * disp_ref[2, row, at, :].astype(jnp.float32)
    )
    magnitude = amp_ref[row, at, :].astype(jnp.float32) * mask_ref[row, at, :].astype(jnp.float32)
    for member in range(4):
        cosine, sine = cos_sin_turns(
            (scales_ref[member] * (0.5 / math.pi)) * phase, wave_cos_terms, wave_sin_terms
        )
        use(
            member,
            jnp.concatenate(
                [(magnitude * cosine).astype(jnp.bfloat16), (magnitude * sine).astype(jnp.bfloat16)], axis=1
            ),
        )


def wave_kernel(place_ref, bragg_ref, scales_ref, disp_ref, amp_ref, mask_ref, wave_ref):
    tile = 64

    def body(step, carry):
        at = pl.ds(pl.multiple_of(step * tile, tile), tile)

        def use(member, wave):
            wave_ref[member, 0, at, :] = wave

        wave_chunk(bragg_ref, scales_ref, disp_ref, amp_ref, mask_ref, 0, at, use)
        return carry

    lax.fori_loop(0, amp_ref.shape[1] // tile, body, 0)


def volume_specs(cells_y, cells_z, at_row):
    return [
        pl.BlockSpec((3, 1, cells_y, cells_z), lambda t, p, *_: (0, 4 * p[0] + at_row(t), 0, 0)),
        pl.BlockSpec((1, cells_y, cells_z), lambda t, p, *_: (4 * p[0] + at_row(t), 0, 0)),
        pl.BlockSpec((1, cells_y, cells_z), lambda t, p, *_: (4 * p[0] + at_row(t), 0, 0)),
    ]


def waves(place, bragg, scales, disp, amp, mask):
    _, _, cells_y, cells_z = disp.shape
    return pl.pallas_call(
        wave_kernel,
        grid_spec=pltpu.PrefetchScalarGridSpec(
            num_scalar_prefetch=3,
            grid=(4,),
            in_specs=volume_specs(cells_y, cells_z, lambda t: t),
            out_specs=pl.BlockSpec((4, 1, cells_y, 2 * cells_z), lambda t, *_: (0, t, 0, 0)),
        ),
        out_shape=jax.ShapeDtypeStruct((4, 4, cells_y, 2 * cells_z), jnp.bfloat16),
        compiler_params=params(),
        cost_estimate=pl.CostEstimate(flops=10_000_000_000, bytes_accessed=24 << 20, transcendentals=0),
        name="waves",
    )(place, bragg, scales, disp, amp, mask)


def first_kernel(
    place_ref, bragg_ref, scales_ref, disp_ref, amp_ref, mask_ref,
    section_ref, out_ref, section, held, zf, matrix, big_real, big_imag,
):
    step = pl.program_id(0)
    cells_y, cells_z = amp_ref.shape[1:]
    frames = zf.shape[2] // 2
    size = matrix.shape[0]

    @pl.when(step == 0)
    def _():
        for member in range(4):
            fill_z(zf, member, scales_ref[member], cells_z, frames)

    @pl.when(step < 4)
    def _():
        lanes = pl.ds(pl.multiple_of(step * frames, frames), frames)
        tile = 256

        def body(turn, carry):
            at = pl.ds(pl.multiple_of(turn * tile, tile), tile)
            low = pl.ds(pl.multiple_of(cells_y + turn * tile, tile), tile)

            def use(member, wave):
                both = dot(wave, zf[member]).astype(jnp.bfloat16)
                section[member, at, lanes] = both[:, 0:frames]
                section[member, low, lanes] = both[:, frames : 2 * frames]

            wave_chunk(bragg_ref, scales_ref, disp_ref, amp_ref, mask_ref, 0, at, use)
            return carry

        lax.fori_loop(0, cells_y // tile, body, 0)

    @pl.when(step >= 4)
    def _():
        small = fill_tables(big_real, big_imag, iota((1, size), 1), size, scales_ref[step - 4])
        low = (iota((8, size), 0) & 2) == 0

        def body(turn, carry):
            columns = [[], []]
            for sub in range(2):
                real, imag = table_rows(big_real, big_imag, small, 2 * turn + sub)
                columns[0].append(jnp.where(low, real, pltpu.roll(imag, 2, 0)))
                columns[1].append(jnp.where(low, -imag, pltpu.roll(real, 2, 0)))
            at = pl.ds(pl.multiple_of(16 * turn, 16), 16)
            for column in range(2):
                matrix[at, column * size : (column + 1) * size] = jnp.concatenate(
                    columns[column], axis=0
                ).astype(jnp.bfloat16)
            return carry

        lax.fori_loop(0, size // 16, body, 0)
        section_ref[0] = section[step - 4]
        held[step - 4] = dot(matrix[...], section[step - 4])

    @pl.when(step == 7)
    def _():
        pack_owners(lambda member, at: held[member, at, :], out_ref, 0)


def first_half(place, bragg, scales, disp, amp, mask, size, frames):
    _, _, cells_y, cells_z = disp.shape
    owners = size // 4
    return pl.pallas_call(
        first_kernel,
        grid_spec=pltpu.PrefetchScalarGridSpec(
            num_scalar_prefetch=3,
            grid=(8,),
            in_specs=volume_specs(cells_y, cells_z, lambda t: jnp.minimum(t, 3)),
            out_specs=[
                pl.BlockSpec((1, 2 * cells_y, 4 * frames), lambda t, *_: (jnp.maximum(t - 4, 0), 0, 0)),
                pl.BlockSpec((owners, 16, 4 * frames), lambda t, *_: (0, 0, 0)),
            ],
            scratch_shapes=[
                pltpu.VMEM((4, 2 * cells_y, 4 * frames), jnp.bfloat16),
                pltpu.VMEM((4, size, 4 * frames), jnp.float32),
                pltpu.VMEM((4, 2 * cells_z, 2 * frames), jnp.bfloat16),
                pltpu.VMEM((size, 2 * size), jnp.bfloat16),
                pltpu.VMEM((size // 8, size), jnp.float32),
                pltpu.VMEM((size // 8, size), jnp.float32),
            ],
        ),
        out_shape=[
            jax.ShapeDtypeStruct((4, 2 * cells_y, 4 * frames), jnp.bfloat16),
            jax.ShapeDtypeStruct((owners, 16, 4 * frames), jnp.bfloat16),
        ],
        compiler_params=params(),
        cost_estimate=pl.CostEstimate(flops=9_000_000_000, bytes_accessed=14 << 20, transcendentals=0),
        name="first_half",
    )(place, bragg, scales, disp, amp, mask)


def second_kernel(section_ref, rows_ref, out_ref, held):
    step = pl.program_id(0)
    held[step] = dot(rows_ref[0, 0], section_ref[0])

    @pl.when(step == 3)
    def _():
        pack_owners(lambda member, at: held[member, at, :], out_ref, 0)


def second_half(section, rows):
    size = rows.shape[2]
    lanes = section.shape[2]
    owners = size // 4
    return pl.pallas_call(
        second_kernel,
        grid=(4,),
        in_specs=[
            pl.BlockSpec((1, 2 * size, lanes), lambda t: (t, 0, 0)),
            pl.BlockSpec((1, 1, size, 2 * size), lambda t: (t, 1, 0, 0)),
        ],
        out_specs=pl.BlockSpec((owners, 16, lanes), lambda t: (0, 0, 0)),
        out_shape=jax.ShapeDtypeStruct((owners, 16, lanes), jnp.bfloat16),
        scratch_shapes=[pltpu.VMEM((4, size, lanes), jnp.float32)],
        compiler_params=params(),
        cost_estimate=pl.CostEstimate(flops=3_000_000_000, bytes_accessed=10 << 20, transcendentals=0),
        name="second_half",
    )(section, rows)


def middle_kernel(weights_ref, got_ref, counts_ref, cols_ref, rows_ref, *rest):
    out_refs, (wide, far, back, held) = rest[:-4], rest[-4:]
    step = pl.program_id(0)
    owners = got_ref.shape[0]
    size = far.shape[2]
    frames = got_ref.shape[2] // 4
    lanes = 2 * frames

    @pl.when(step == 0)
    def _():
        for group in range(4):
            piece = got_ref[:, :, group * frames : (group + 1) * frames].astype(jnp.float32)
            turned = jnp.swapaxes(piece, 0, 1).astype(jnp.bfloat16)
            for member in range(4):
                for part in range(2):
                    at = (4 * (group // 2) + 2 * part + group % 2) * owners
                    for row in range(2):
                        wide[member, at : at + owners, row * frames : (row + 1) * frames] = turned[
                            4 * member + 2 * part + row
                        ]

    @pl.when(step < 4)
    def _():
        for part in range(2):
            far[step, part] = dot(cols_ref[0, part], wide[step])

    @pl.when(step == 3)
    def _():
        def body(turn, carry):
            at = pl.ds(pl.multiple_of(turn * 16, 16), 16)
            fields = [(far[member, 0, at, :], far[member, 1, at, :]) for member in range(4)]
            intensity = None
            for member, (real, imag) in enumerate(fields):
                term = weights_ref[member] * (real * real + imag * imag)
                intensity = term if intensity is None else intensity + term
            ratio = 1.0 - jnp.sqrt(counts_ref[at, :].astype(jnp.float32) / jnp.maximum(intensity, 0.5))
            for member, (real, imag) in enumerate(fields):
                factor = weights_ref[member] * ratio
                back[member, at, :] = (factor * real).astype(jnp.bfloat16)
                low = pl.ds(pl.multiple_of(size + turn * 16, 16), 16)
                back[member, low, :] = (-factor * imag).astype(jnp.bfloat16)
            return carry

        lax.fori_loop(0, size // 16, body, 0)

    @pl.when(step >= 4)
    def _():
        for half in range(2):
            held[step - 4, half] = dot(rows_ref[0, half], back[step - 4])

    @pl.when(step == 7)
    def _():
        for half in range(2):
            out_ref, place = (out_refs[0], 16 * half) if len(out_refs) == 1 else (out_refs[half], 0)
            pack_owners(lambda member, at, half=half: held[member, half, at, :], out_ref, place)


def middle(weights, got, counts, cols, rows, split):
    owners, _, lanes4 = got.shape
    size = rows.shape[2]
    lanes = lanes4 // 2
    if split:
        shapes = [(owners, 16, lanes)] * 2
    else:
        shapes = [(owners, 32, lanes)]
    return pl.pallas_call(
        middle_kernel,
        grid=(8,),
        in_specs=[
            pl.BlockSpec(memory_space=pltpu.SMEM),
            pl.BlockSpec(got.shape, lambda t: (0, 0, 0)),
            pl.BlockSpec(counts.shape, lambda t: (0, 0)),
            pl.BlockSpec((1, 2, size, 2 * size), lambda t: (jnp.minimum(t, 3), 0, 0, 0)),
            pl.BlockSpec((1, 2, size, 2 * size), lambda t: (jnp.maximum(t - 4, 0), 0, 0, 0)),
        ],
        out_specs=[pl.BlockSpec(shape, lambda t: (0, 0, 0)) for shape in shapes],
        out_shape=[jax.ShapeDtypeStruct(shape, jnp.bfloat16) for shape in shapes],
        scratch_shapes=[
            pltpu.VMEM((4, 2 * size, lanes), jnp.bfloat16),
            pltpu.VMEM((4, 2, size, lanes), jnp.float32),
            pltpu.VMEM((4, 2 * size, lanes), jnp.bfloat16),
            pltpu.VMEM((4, 2, size, lanes), jnp.float32),
        ],
        compiler_params=params(),
        cost_estimate=pl.CostEstimate(flops=9_000_000_000, bytes_accessed=22 << 20, transcendentals=0),
        name="middle",
    )(weights, got, counts, cols, rows)


def turn_rows(got_ref, wide, group, frames, members, first_row, first_lane):
    owners = got_ref.shape[0]
    piece = got_ref[:, first_row : first_row + 16, group * frames : (group + 1) * frames]
    turned = jnp.swapaxes(piece.astype(jnp.float32), 0, 1).astype(jnp.bfloat16)
    for member in range(members):
        for part in range(2):
            at = (2 * part + group) * owners
            for row in range(2):
                lane = first_lane + row * frames
                wide[member, at : at + owners, lane : lane + frames] = turned[4 * member + 2 * part + row]


def early_kernel(got_ref, cols_ref, out_ref, wide):
    member = pl.program_id(0)
    frames = got_ref.shape[2] // 2

    @pl.when(member == 0)
    def _():
        for half in range(2):
            for group in range(2):
                turn_rows(got_ref, wide, group, frames, 4, 16 * half, 2 * half * frames)

    for part in range(2):
        out_ref[0, part] = dot(cols_ref[0, part], wide[member]).astype(jnp.bfloat16)


def early_part(got, cols):
    owners, rows, lanes = got.shape
    size = cols.shape[2]
    return pl.pallas_call(
        early_kernel,
        grid=(4,),
        in_specs=[
            pl.BlockSpec(got.shape, lambda t: (0, 0, 0)),
            pl.BlockSpec((1, 2, size, size), lambda t: (t, 0, 0, 0)),
        ],
        out_specs=pl.BlockSpec((1, 2, size, 2 * lanes), lambda t: (t, 0, 0, 0)),
        out_shape=jax.ShapeDtypeStruct((4, 2, size, 2 * lanes), jnp.bfloat16),
        scratch_shapes=[pltpu.VMEM((4, size, 2 * lanes), jnp.bfloat16)],
        compiler_params=params(),
        cost_estimate=pl.CostEstimate(flops=4_000_000_000, bytes_accessed=10 << 20, transcendentals=0),
        name="early_part",
    )(got, cols)


def last_kernel(
    place_ref, scales_ref, late_ref, real_cols_ref, imag_cols_ref, real_part_ref, imag_part_ref, zb_ref,
    wave_ref, amp_ref, *rest,
):
    out_refs, (wide, field, sum_amp, sum_phase) = rest[:-4], rest[-4:]
    member = pl.program_id(0)
    frames = late_ref.shape[2] // 2
    cells_y, cells_z = amp_ref.shape[1:]

    @pl.when(member == 0)
    def _():
        for group in range(2):
            turn_rows(late_ref, wide, group, frames, 4, 0, 0)
        sum_amp[...] = jnp.zeros_like(sum_amp)
        sum_phase[...] = jnp.zeros_like(sum_phase)

    columns = wide[member]
    real = (dot(real_cols_ref[0, 0], columns) + real_part_ref[0, 0].astype(jnp.float32)).astype(jnp.bfloat16)
    imag = (dot(imag_cols_ref[0, 0], columns) + imag_part_ref[0, 0].astype(jnp.float32)).astype(jnp.bfloat16)
    for row in range(2):
        lane = slice(row * frames, (row + 1) * frames)
        field[row, :, 0:frames] = real[:, lane]
        field[row, :, frames : 2 * frames] = imag[:, lane]
    scale = scales_ref[member]
    tile = 256

    def body(step, carry):
        at = pl.ds(pl.multiple_of(step * tile, tile), tile)
        for row in range(2):
            both = dot(field[row, at, :], zb_ref[0])
            back_real, back_imag = both[:, 0:cells_z], both[:, cells_z : 2 * cells_z]
            wave_real = wave_ref[0, row, at, 0:cells_z].astype(jnp.float32)
            wave_imag = wave_ref[0, row, at, cells_z : 2 * cells_z].astype(jnp.float32)
            sum_amp[row, at, :] += back_real * wave_real - back_imag * wave_imag
            sum_phase[row, at, :] += scale * (back_real * wave_imag + back_imag * wave_real)
        return carry

    lax.fori_loop(0, cells_y // tile, body, 0)

    @pl.when(member == 3)
    def _():
        def close(step, carry):
            at = pl.ds(pl.multiple_of(step * tile, tile), tile)
            for row in range(2):
                out_ref, place = (out_refs[0], row) if len(out_refs) == 1 else (out_refs[row], 0)
                total = sum_amp[row, at, :] / amp_ref[row, at, :].astype(jnp.float32)
                out_ref[place, 0, at, :] = total.astype(jnp.bfloat16)
                out_ref[place, 1, at, :] = sum_phase[row, at, :].astype(jnp.bfloat16)
            return carry

        lax.fori_loop(0, cells_y // tile, close, 0)


def last(place, scales, late, early, cols, zb, wave, amp, half, pieces):
    _, cells_y, cells_z = amp.shape
    owners, _, lanes = late.shape
    size = cols.shape[2]

    def of_part(part, at):
        return lambda t, *_: (t, part, 0, at)

    return pl.pallas_call(
        last_kernel,
        grid_spec=pltpu.PrefetchScalarGridSpec(
            num_scalar_prefetch=2,
            grid=(4,),
            in_specs=[
                pl.BlockSpec((owners, 16, lanes), lambda t, *_: (0, 0, 0)),
                pl.BlockSpec((1, 1, size, size), of_part(0, 1)),
                pl.BlockSpec((1, 1, size, size), of_part(1, 1)),
                pl.BlockSpec((1, 1, size, lanes), of_part(0, half)),
                pl.BlockSpec((1, 1, size, lanes), of_part(1, half)),
                pl.BlockSpec((1,) + zb.shape[1:], lambda t, *_: (t, 0, 0)),
                pl.BlockSpec((1, 2, cells_y, 2 * cells_z), lambda t, *_: (t, half, 0, 0)),
                pl.BlockSpec((2, cells_y, cells_z), lambda t, p, *_: (2 * p[0] + half, 0, 0)),
            ],
            out_specs=[pl.BlockSpec((2 // pieces, 2, cells_y, cells_z), lambda t, *_: (0, 0, 0, 0))] * pieces,
            scratch_shapes=[
                pltpu.VMEM((4, size, lanes), jnp.bfloat16),
                pltpu.VMEM((2, cells_y, lanes), jnp.bfloat16),
                pltpu.VMEM((2, cells_y, cells_z), jnp.float32),
                pltpu.VMEM((2, cells_y, cells_z), jnp.float32),
            ],
        ),
        out_shape=[jax.ShapeDtypeStruct((2 // pieces, 2, cells_y, cells_z), jnp.bfloat16)] * pieces,
        compiler_params=params(),
        cost_estimate=pl.CostEstimate(flops=4_000_000_000, bytes_accessed=16 << 20, transcendentals=0),
        name="last",
    )(place, scales, late, cols, cols, early, early, zb, wave, amp)


def finish_kernel(place_ref, bragg_ref, sums_ref, amp_ref, disp_ref, *rest):
    new_amp_ref, new_disp_ref = rest[-2:]
    new_amp_ref[0] = amp_ref[0].astype(jnp.float32) - step_size * sums_ref[0, 0].astype(jnp.float32)
    sum_phase = sums_ref[0, 1].astype(jnp.float32)
    for axis in range(3):
        new_disp_ref[axis, 0] = (
            disp_ref[axis, 0].astype(jnp.float32) + (step_size * bragg_ref[axis]) * sum_phase
        ).astype(jnp.bfloat16)


def finish(place, bragg, sums, amp, disp, earlier, first_row, other):
    rows = sums.shape[0]
    _, cells_y, cells_z = amp.shape

    def row(t, p):
        half = 1 - p[0] if other else p[0]
        return 4 * half + first_row + t

    amp_spec = pl.BlockSpec((1, cells_y, cells_z), lambda t, p, *_: (row(t, p), 0, 0))
    disp_spec = pl.BlockSpec((3, 1, cells_y, cells_z), lambda t, p, *_: (0, row(t, p), 0, 0))
    kept = [] if earlier is None else list(earlier)
    return pl.pallas_call(
        finish_kernel,
        grid_spec=pltpu.PrefetchScalarGridSpec(
            num_scalar_prefetch=2,
            grid=(rows,),
            in_specs=[
                pl.BlockSpec((1, 2, cells_y, cells_z), lambda t, *_: (t, 0, 0, 0)),
                amp_spec,
                disp_spec,
            ]
            + [pl.BlockSpec(memory_space=pl.ANY)] * len(kept),
            out_specs=[amp_spec, disp_spec],
        ),
        out_shape=[
            jax.ShapeDtypeStruct(amp.shape, jnp.float32),
            jax.ShapeDtypeStruct(disp.shape, jnp.bfloat16),
        ],
        input_output_aliases={} if earlier is None else {5: 0, 6: 1},
        compiler_params=params(small_limit),
        cost_estimate=pl.CostEstimate(flops=10_000_000, bytes_accessed=(3 << 20) * rows, transcendentals=0),
        name="finish",
    )(place, bragg, sums, amp, disp, *kept)


def exchange(blocks):
    return lax.all_to_all(blocks, both_axes, split_axis=0, concat_axis=0, tiled=True)


def swap(values):
    return lax.ppermute(values, "spec", [(0, 1), (1, 0)])


def nothing(*refs):
    pass


def after(values, *others):
    anywhere = pl.BlockSpec(memory_space=pl.ANY)
    return pl.pallas_call(
        nothing,
        in_specs=[anywhere] * (1 + len(others)),
        out_specs=anywhere,
        out_shape=jax.ShapeDtypeStruct(values.shape, values.dtype),
        input_output_aliases={0: 0},
        compiler_params=params(),
        name="after",
    )(values, *others)


def per_device(amplitude, displacement, support, counts, bin_weights, bin_scales, bragg_vector):
    place = lax.axis_index("spec").reshape(1).astype(jnp.int32)
    size, rows_y, frames = counts.shape
    cells_z = amplitude.shape[2]
    volume = (place, bragg_vector, bin_scales, displacement, amplitude, support)
    section, blocks = first_half(*volume, size, frames)
    sent_early = exchange(blocks)
    rows = row_matrices(bin_scales, size)
    wave = waves(*volume)
    sent_late = exchange(after(second_half(section, rows), sent_early, wave))
    cols, zb = column_matrices(bin_scales, size, cells_z, frames)
    mine = lax.dynamic_slice_in_dim(counts, place[0] * (rows_y // 2), rows_y // 2, axis=1)
    mine = mine.reshape(size, rows_y // 2 * frames)
    early_counts, late_counts = mine[:, 0 : 2 * frames], mine[:, 2 * frames : 4 * frames]
    (early,) = middle(bin_weights, sent_early, early_counts, cols, rows, False)
    early = exchange(after(early, sent_late))
    parts = middle(bin_weights, sent_late, late_counts, cols, rows, True)
    early_sum = early_part(early, cols)
    late = [exchange(after(parts[0], early))]
    late.append(exchange(after(parts[1], early_sum, late[0])))
    sums = []
    for half in range(2):
        parts = last(
            place, bin_scales, late[half], early_sum, cols, zb, wave, amplitude, half, 1 + half
        )
        for number, part in enumerate(parts):
            sums.append((2 * half + number, part, swap(part)))
    outs = None
    for other in (False, True):
        for row, mine, theirs in sums:
            outs = finish(
                place, bragg_vector, theirs if other else mine, amplitude, displacement, outs, row, other
            )
    return tuple(outs)


def solution(mesh):
    in_specs = (
        P("slab", None, None),
        P(None, "slab", None, None),
        P("slab", None, None),
        P(None, "slab", None),
        P(),
        P(),
        P(),
    )
    out_specs = (P("slab", None, None), P(None, "slab", None, None))
    return jax.shard_map(
        per_device, mesh=mesh, in_specs=in_specs, out_specs=out_specs, check_vma=False
    )
```

time: 511 us -> 226 us (0.44)
  waiting for transfers between devices: 237 us -> 59.6 us
  other arithmetic: 138 us -> 0 us
  Pallas kernels: 0 us -> 125 us
  matrix products: 52.8 us -> 0 us
  between operations: 15.7 us -> 0.76 us
  starting transfers between devices: 44.5 us -> 31.8 us
  local copies, waits for them, and re-layouts: 20.2 us -> 7.72 us
    psum x2 -> x0, waiting for transfers between devices: 152 us -> none  [the longest x1 110 us: per_device(): lax.psum(jnp.stack([part_amp, part_phase]).astype(jnp.bfloat16), 'spec')]
    pallas_call x0 -> x20, Pallas kernels: none -> 125 us  [the longest x2 32.1 us: middle(): pl.pallas_call(middle_kernel, grid=(8,), in_specs=[pl.BlockSpec(memory_sp...]
    another operation x8 -> x0, other arithmetic: 101 us -> none  [the longest x2 50.8 us: per_device(): jnp.stack([magnitude * jnp.cos(bin_phase), magnitude * jnp.sin(bin_phase)])]
    dot_general x8 -> x0, matrix products: 52.8 us -> none  [the longest x2 17.9 us: per_device(): jnp.einsum('oxyk,okpn->pxyn', back_two, matrices[member][0], preferred_el...]
    all_to_all x4 -> x5, waiting for transfers between devices: 84.9 us -> 46.3 us  [exchange(): lax.all_to_all(blocks, both_axes, split_axis=0, concat_axis=0, tiled=True)]
    convert_element_type x3 -> x0, other arithmetic: 19.5 us -> none  [the longest x1 8.57 us: finish(): new_displacement = (disp_values - step_size * bragg_vector[:, None, None,...]
    all_to_all x4 -> x5, starting transfers between devices: 44.4 us -> 28.8 us  [exchange(): lax.all_to_all(blocks, both_axes, split_axis=0, concat_axis=0, tiled=True)]
    mul x3 -> x0, other arithmetic: 14.5 us -> none  [the longest x1 8.24 us: finish(): grad_phase = -mask_values * amp_values * sum_phase]
  transfers between devices with their start and end apart: 6 -> 8, of which waited for: 6 -> 7; matrix products, arithmetic and copies ran while one was open for 7% -> 1% of each run, Pallas kernels for 0% -> 46%
where the time goes in v2:
time: 226 us; the launch traced here: 225 us
  Pallas kernels  125 us (55%)
  waiting for transfers between devices  59.6 us (26%)
  starting transfers between devices  31.8 us (14%)
  local copies, waits for them, and re-layouts  7.72 us (3%)
    all_to_all x5, waiting for transfers between devices, exchange(): lax.all_to_all(blocks, both_axes, split_axis=0, concat_axis=0, tiled=True)  46.3 us
    pallas_call x2, Pallas kernels, middle(): pl.pallas_call(middle_kernel, grid=(8,), in_specs=[pl.BlockSpec(memory_sp...  32.1 us
    all_to_all x5, starting transfers between devices, exchange(): lax.all_to_all(blocks, both_axes, split_axis=0, concat_axis=0, tiled=True)  28.8 us
    pallas_call x2, Pallas kernels, last(): pl.pallas_call(last_kernel, grid_spec=pltpu.PrefetchScalarGridSpec(num_sc...  21 us
    pallas_call x1, Pallas kernels, first_half(): pl.pallas_call(first_kernel, grid_spec=pltpu.PrefetchScalarGridSpec(num_s...  21 us
    ppermute x3, waiting for transfers between devices, swap(): return lax.ppermute(values, 'spec', [(0, 1), (1, 0)])  13.4 us
    pallas_call x6, Pallas kernels, finish(): pl.pallas_call(finish_kernel, grid_spec=pltpu.PrefetchScalarGridSpec(num_...  12.4 us
    pallas_call x1, Pallas kernels, waves(): pl.pallas_call(wave_kernel, grid_spec=pltpu.PrefetchScalarGridSpec(num_sc...  11.6 us
  transfers between devices with their start and end apart: 8, of which 7 were waited for; matrix products, arithmetic and copies ran while one was open for 1% of the time, Pallas kernels for 46%

profile of v2, /device:TPU:1, one launch (start us, length us, event | category | flops | bytes accessed | tf_op | source)
XLA Modules:
  0.0 225.4 jit_solution(11607230243533831638)
XLA Ops:
  0.6 0.0 copy-start
  0.7 21.0 %first_half.1 = (bf16[4,1024,512]{2,1,0:T(8,128)(2,1)}, bf16[128,16,512]{2,1,0:T(8,128)(2,1)}) custom-call(s32[1]{0:T(128)} %bitcast.place_ref, f32[3]{0:T(128)} %bragg_ref.15, f32[4]{0:T(128)} %scales_ref.11, bf16[3,8,512,256]{3,2,1,0:T(8,128)(2,1)} %disp_ref.15, bf16[8,512,256]{2,1,0:T(8,128)(2,1)} %amp_ref.19, s32[8,512,256]{2,1,0:T(8,128)} %mask_ref.3), custom_call_target="tpu_custom_call" | custom-call | flops 8999999488 | bytes 14680064 | tf_op jit(solution)/shard_map/first_half/pallas_call | solution.py:333
  21.6 12.0 %all-to-all-start = ((bf16[128,16,512]{2,1,0:T(8,128)(2,1)}), bf16[128,16,512]{2,1,0:T(8,128)(2,1)}, u32[]{:S(2)}, u32[]{:S(2)}) async-start(bf16[128,16,512]{2,1,0:T(8,128)(2,1)} %get-tuple-element.21), calls=%async_computation | async-start | bytes 4194304 | tf_op jit(solution)/shard_map/all_to_all | solution.py:662
  33.6 6.4 %row_matrices.1.rows_ref = bf16[4,2,512,1024]{3,2,1,0:T(8,128)(2,1)} custom-call(f32[4]{0:T(128)} %scales_ref.11), custom_call_target="tpu_custom_call" | custom-call | flops 4000000000 | bytes 8388608 | tf_op jit(solution)/shard_map/row_matrices/pallas_call | solution.py:127
  40.0 7.1 %second_half.1.refs_0_ = bf16[128,16,512]{2,1,0:T(8,128)(2,1)} custom-call(bf16[4,1024,512]{2,1,0:T(8,128)(2,1)} %get-tuple-element.20.section_ref, bf16[4,2,512,1024]{3,2,1,0:T(8,128)(2,1)} %row_matrices.1.rows_ref), custom_call_target="tpu_custom_call" | custom-call | flops 3000000000 | bytes 10485760 | tf_op jit(solution)/shard_map/second_half/pallas_call | solution.py:375
  47.1 11.6 %waves.1.refs_2_.wave_ref = bf16[4,4,512,512]{3,2,1,0:T(8,128)(2,1)} custom-call(s32[1]{0:T(128)} %bitcast.place_ref, f32[3]{0:T(128)} %bragg_ref.15, f32[4]{0:T(128)} %scales_ref.11, bf16[3,8,512,256]{3,2,1,0:T(8,128)(2,1)} %disp_ref.15, bf16[8,512,256]{2,1,0:T(8,128)(2,1)} %amp_ref.19, s32[8,512,256]{2,1,0:T(8,128)} %mask_ref.3), custom_call_target="tpu_custom_call" | custom-call | flops 10000000000 | bytes 25165824 | tf_op jit(solution)/shard_map/waves/pallas_call | solution.py:255
  58.6 5.6 %all-to-all-done.refs_1_.got_ref = bf16[128,16,512]{2,1,0:T(8,128)(2,1)} async-done(((bf16[128,16,512]{2,1,0:T(8,128)(2,1)}), bf16[128,16,512]{2,1,0:T(8,128)(2,1)}, u32[]{:S(2)}, u32[]{:S(2)}) %all-to-all-start) | async-done | bytes 2097184 | tf_op jit(solution)/shard_map/all_to_all | solution.py:662
  64.3 4.7 %all-to-all-start.1 = ((bf16[128,16,512]{2,1,0:T(8,128)(2,1)}), bf16[128,16,512]{2,1,0:T(8,128)(2,1)}, u32[]{:S(2)}, u32[]{:S(2)}) async-start(bf16[128,16,512]{2,1,0:T(8,128)(2,1)} %after.4), calls=%async_computation.1 | async-start | bytes 4194304 | tf_op jit(solution)/shard_map/all_to_all | solution.py:662
  69.0 0.0 copy-done
  69.0 0.2 constant_dynamic-slice_fusion
  69.2 0.4 copy.26
  69.6 0.1 fusion
  69.6 1.0 copy.28.counts_ref
  70.6 5.9 %column_matrices.1 = (bf16[4,2,512,1024]{3,2,1,0:T(8,128)(2,1)}, bf16[4,256,512]{2,1,0:T(8,128)(2,1)}) custom-call(f32[4]{0:T(128)} %scales_ref.11), custom_call_target="tpu_custom_call" | custom-call | flops 4000000000 | bytes 8388608 | tf_op jit(solution)/shard_map/column_matrices/pallas_call | solution.py:171
  76.5 16.1 %middle.3.refs_0_ = bf16[128,32,256]{2,1,0:T(8,128)(2,1)} custom-call(f32[4]{0:T(128)} %weights_ref.3, bf16[128,16,512]{2,1,0:T(8,128)(2,1)} %all-to-all-done.refs_1_.got_ref, s32[512,256]{1,0:T(8,128)} %copy.28.counts_ref, bf16[4,2,512,1024]{3,2,1,0:T(8,128)(2,1)} %get-tuple-element.22.cols_ref.real_cols_ref.imag_cols_ref, ...), custom_call_target="tpu_custom_call" | custom-call | flops 8999999488 | bytes 23068672 | tf_op jit(solution)/shard_map/middle/pallas_call | solution.py:456
  92.6 7.1 %all-to-all-done.1.got_ref.refs_1_ = bf16[128,16,512]{2,1,0:T(8,128)(2,1)} async-done(((bf16[128,16,512]{2,1,0:T(8,128)(2,1)}), bf16[128,16,512]{2,1,0:T(8,128)(2,1)}, u32[]{:S(2)}, u32[]{:S(2)}) %all-to-all-start.1) | async-done | bytes 2097184 | tf_op jit(solution)/shard_map/all_to_all | solution.py:662
  99.8 3.7 %all-to-all-start.2 = ((bf16[128,32,256]{2,1,0:T(8,128)(2,1)}), bf16[128,32,256]{2,1,0:T(8,128)(2,1)S(1)}, u32[]{:S(2)}, u32[]{:S(2)}) async-start(bf16[128,32,256]{2,1,0:T(8,128)(2,1)} %after.5), calls=%async_computation.2 | async-start | bytes 4194304 | tf_op jit(solution)/shard_map/all_to_all | solution.py:662
  103.4 1.0 copy.27.counts_ref
  104.4 16.1 %middle.2 = (bf16[128,16,256]{2,1,0:T(8,128)(2,1)}, bf16[128,16,256]{2,1,0:T(8,128)(2,1)}) custom-call(f32[4]{0:T(128)} %weights_ref.3, bf16[128,16,512]{2,1,0:T(8,128)(2,1)} %all-to-all-done.1.got_ref.refs_1_, s32[512,256]{1,0:T(8,128)} %copy.27.counts_ref, bf16[4,2,512,1024]{3,2,1,0:T(8,128)(2,1)} %get-tuple-element.22.cols_ref.real_cols_ref.imag_cols_ref, ...), custom_call_target="tpu_custom_call" | custom-call | flops 8999999488 | bytes 23068672 | tf_op jit(solution)/shard_map/middle/pallas_call | solution.py:456
  120.5 14.1 %all-to-all-done.2.got_ref.refs_1_ = bf16[128,32,256]{2,1,0:T(8,128)(2,1)S(1)} async-done(((bf16[128,32,256]{2,1,0:T(8,128)(2,1)}), bf16[128,32,256]{2,1,0:T(8,128)(2,1)S(1)}, u32[]{:S(2)}, u32[]{:S(2)}) %all-to-all-start.2) | async-done | bytes 2097184 | tf_op jit(solution)/shard_map/all_to_all | solution.py:662
  134.6 0.0 copy-start.10
  134.6 1.3 copy-done.10
  135.9 3.8 %all-to-all-start.3 = ((bf16[128,16,256]{2,1,0:T(8,128)(2,1)}), bf16[128,16,256]{2,1,0:T(8,128)(2,1)S(1)}, u32[]{:S(2)}, u32[]{:S(2)}) async-start(bf16[128,16,256]{2,1,0:T(8,128)(2,1)} %after.6), calls=%async_computation.3 | async-start | bytes 2097152 | tf_op jit(solution)/shard_map/all_to_all | solution.py:662
  139.7 8.0 %early_part.1.refs_1_.real_part_ref.imag_part_ref = bf16[4,2,512,512]{3,2,1,0:T(8,128)(2,1)} custom-call(bf16[128,32,256]{2,1,0:T(8,128)(2,1)} %copy-done.10, bf16[4,2,512,1024]{3,2,1,0:T(8,128)(2,1)} %get-tuple-element.22.cols_ref.real_cols_ref.imag_cols_ref), custom_call_target="tpu_custom_call" | custom-call | flops 4000000000 | bytes 10485760 | tf_op jit(solution)/shard_map/early_part/pallas_call | solution.py:509
  147.7 11.9 %all-to-all-done.3.refs_2_.late_ref = bf16[128,16,256]{2,1,0:T(8,128)(2,1)S(1)} async-done(((bf16[128,16,256]{2,1,0:T(8,128)(2,1)}), bf16[128,16,256]{2,1,0:T(8,128)(2,1)S(1)}, u32[]{:S(2)}, u32[]{:S(2)}) %all-to-all-start.3) | async-done | bytes 1048608 | tf_op jit(solution)/shard_map/all_to_all | solution.py:662
  159.7 0.0 copy-start.9
  159.7 1.0 copy-done.9
  160.6 4.7 %all-to-all-start.4 = ((bf16[128,16,256]{2,1,0:T(8,128)(2,1)}), bf16[128,16,256]{2,1,0:T(8,128)(2,1)}, u32[]{:S(2)}, u32[]{:S(2)}) async-start(bf16[128,16,256]{2,1,0:T(8,128)(2,1)} %after.7), calls=%async_computation.4 | async-start | bytes 2097152 | tf_op jit(solution)/shard_map/all_to_all | solution.py:662
  165.3 10.5 %last.3.sums_ref = bf16[2,2,512,256]{3,2,1,0:T(8,128)(2,1)} custom-call(s32[1]{0:T(128)} %bitcast.place_ref, f32[4]{0:T(128)} %scales_ref.11, bf16[128,16,256]{2,1,0:T(8,128)(2,1)} %copy-done.9, bf16[4,2,512,1024]{3,2,1,0:T(8,128)(2,1)} %get-tuple-element.22.cols_ref.real_cols_ref.imag_cols_ref, ...), custom_call_target="tpu_custom_call" | custom-call | flops 4000000000 | bytes 16777216 | tf_op jit(solution)/shard_map/last/pallas_call | solution.py:586
  175.8 0.0 copy-start.3
  175.8 0.0 copy-start.5
  175.8 0.0 copy-start.8
  175.8 1.5 collective-permute-start.2
  177.4 7.5 %all-to-all-done.4.late_ref = bf16[128,16,256]{2,1,0:T(8,128)(2,1)} async-done(((bf16[128,16,256]{2,1,0:T(8,128)(2,1)}), bf16[128,16,256]{2,1,0:T(8,128)(2,1)}, u32[]{:S(2)}, u32[]{:S(2)}) %all-to-all-start.4) | async-done | bytes 1048608 | tf_op jit(solution)/shard_map/all_to_all | solution.py:662
  184.8 10.5 %last.2 = (bf16[1,2,512,256]{3,2,1,0:T(8,128)(2,1)}, bf16[1,2,512,256]{3,2,1,0:T(8,128)(2,1)}) custom-call(s32[1]{0:T(128)} %bitcast.place_ref, f32[4]{0:T(128)} %scales_ref.11, bf16[128,16,256]{2,1,0:T(8,128)(2,1)} %all-to-all-done.4.late_ref, bf16[4,2,512,1024]{3,2,1,0:T(8,128)(2,1)} %get-tuple-element.22.cols_ref.real_cols_ref.imag_cols_ref, ...), custom_call_target="tpu_custom_call" | custom-call | flops 4000000000 | bytes 16777216 | tf_op jit(solution)/shard_map/last/pallas_call | solution.py:586
  195.3 0.4 collective-permute-start.1
  195.7 1.1 collective-permute-start
  196.8 0.0 copy-done.3
  196.8 0.0 copy-done.5
  196.8 0.0 copy-done.8
  196.8 0.0 copy-start.2
  196.8 2.8 %copy-done.2 = bf16[3,8,512,256]{3,2,1,0:T(8,128)(2,1)S(1)} copy-done((bf16[3,8,512,256]{3,2,1,0:T(8,128)(2,1)S(1)}, bf16[3,8,512,256]{3,2,1,0:T(8,128)(2,1)}, u32[]{:S(2)}) %copy-start.2) | copy-done | bytes 6291480
  199.6 0.0 copy-start.7
  199.6 2.3 %finish.6 = (f32[8,512,256]{2,1,0:T(8,128)}, bf16[3,8,512,256]{3,2,1,0:T(8,128)(2,1)}) custom-call(s32[1]{0:T(128)} %bitcast.place_ref, f32[3]{0:T(128)S(1)} %copy-done.8, bf16[2,2,512,256]{3,2,1,0:T(8,128)(2,1)S(1)} %copy-done.5, bf16[8,512,256]{2,1,0:T(8,128)(2,1)S(1)} %copy-done.3, bf16[3,8,512,256]{3,2,1,0:T(8,128)(2,1)S(1)} %copy-done.2), custom_call_target="tpu_custom_call" | custom-call | flops 10000000 | bytes 6291456 | tf_op jit(solution)/shard_map/finish/pallas_call | solution.py:637
  201.9 0.0 copy-done.7
  201.9 0.0 copy-start.6
  201.9 1.7 finish.7
  203.6 0.0 copy-done.6
  203.6 1.7 finish.8
  205.3 0.0 collective-permute-done.2.sums_ref
  205.3 3.2 %finish.9 = (f32[8,512,256]{2,1,0:T(8,128)}, bf16[3,8,512,256]{3,2,1,0:T(8,128)(2,1)}) custom-call(s32[1]{0:T(128)} %bitcast.place_ref, f32[3]{0:T(128)S(1)} %copy-done.8, bf16[2,2,512,256]{3,2,1,0:T(8,128)(2,1)} %collective-permute-done.2.sums_ref, bf16[8,512,256]{2,1,0:T(8,128)(2,1)S(1)} %copy-done.3, ...), custom_call_target="tpu_custom_call", output_to_operand_aliasing={{0}: (5, {}), {1}: (6, {})} | custom-call | flops 10000000 | bytes 6291456 | tf_op jit(solution)/shard_map/finish/pallas_call | solution.py:637
  208.6 3.8 %collective-permute-done.1.sums_ref = bf16[1,2,512,256]{3,2,1,0:T(8,128)(2,1)S(1)} collective-permute-done((bf16[1,2,512,256]{3,2,1,0:T(8,128)(2,1)}, bf16[1,2,512,256]{3,2,1,0:T(8,128)(2,1)S(1)}, u32[]{:S(2)}, u32[]{:S(2)}) %collective-permute-start.1) | collective-permute-done | bytes 524320 | tf_op jit(solution)/shard_map/ppermute | solution.py:666
  212.4 0.0 copy-start.4
  212.4 1.7 finish.10
  214.1 9.5 %collective-permute-done.sums_ref = bf16[1,2,512,256]{3,2,1,0:T(8,128)(2,1)S(1)} collective-permute-done((bf16[1,2,512,256]{3,2,1,0:T(8,128)(2,1)}, bf16[1,2,512,256]{3,2,1,0:T(8,128)(2,1)S(1)}, u32[]{:S(2)}, u32[]{:S(2)}) %collective-permute-start) | collective-permute-done | bytes 524320 | tf_op jit(solution)/shard_map/ppermute | solution.py:666
  223.6 0.0 copy-done.4
  223.6 0.0 copy-start.1
  223.7 1.7 finish.11
  225.4 0.0 copy-done.1
  (4 shorter events, 0.0 us)
Async XLA Ops:
  0.6 68.4 %copy-start = (s32[512,8,128]{2,1,0:T(8,128)S(1)}, s32[512,8,128]{2,1,0:T(8,128)}, u32[]{:S(2)}) copy-start(s32[512,8,128]{2,1,0:T(8,128)} %param.10) | copy-start | bytes 6291460
  21.6 42.6 %all-to-all-start = ((bf16[128,16,512]{2,1,0:T(8,128)(2,1)}), bf16[128,16,512]{2,1,0:T(8,128)(2,1)}, u32[]{:S(2)}, u32[]{:S(2)}) async-start(bf16[128,16,512]{2,1,0:T(8,128)(2,1)} %get-tuple-element.21), calls=%async_computation | async-start | bytes 4194304 | tf_op jit(solution)/shard_map/all_to_all | solution.py:662
  64.3 35.5 %all-to-all-start.1 = ((bf16[128,16,512]{2,1,0:T(8,128)(2,1)}), bf16[128,16,512]{2,1,0:T(8,128)(2,1)}, u32[]{:S(2)}, u32[]{:S(2)}) async-start(bf16[128,16,512]{2,1,0:T(8,128)(2,1)} %after.4), calls=%async_computation.1 | async-start | bytes 4194304 | tf_op jit(solution)/shard_map/all_to_all | solution.py:662
  99.8 34.8 %all-to-all-start.2 = ((bf16[128,32,256]{2,1,0:T(8,128)(2,1)}), bf16[128,32,256]{2,1,0:T(8,128)(2,1)S(1)}, u32[]{:S(2)}, u32[]{:S(2)}) async-start(bf16[128,32,256]{2,1,0:T(8,128)(2,1)} %after.5), calls=%async_computation.2 | async-start | bytes 4194304 | tf_op jit(solution)/shard_map/all_to_all | solution.py:662
  134.6 1.3 copy-start.10
  135.9 23.7 %all-to-all-start.3 = ((bf16[128,16,256]{2,1,0:T(8,128)(2,1)}), bf16[128,16,256]{2,1,0:T(8,128)(2,1)S(1)}, u32[]{:S(2)}, u32[]{:S(2)}) async-start(bf16[128,16,256]{2,1,0:T(8,128)(2,1)} %after.6), calls=%async_computation.3 | async-start | bytes 2097152 | tf_op jit(solution)/shard_map/all_to_all | solution.py:662
  159.7 1.0 copy-start.9
  160.6 24.2 %all-to-all-start.4 = ((bf16[128,16,256]{2,1,0:T(8,128)(2,1)}), bf16[128,16,256]{2,1,0:T(8,128)(2,1)}, u32[]{:S(2)}, u32[]{:S(2)}) async-start(bf16[128,16,256]{2,1,0:T(8,128)(2,1)} %after.7), calls=%async_computation.4 | async-start | bytes 2097152 | tf_op jit(solution)/shard_map/all_to_all | solution.py:662
  175.8 21.0 %copy-start.3 = (bf16[8,512,256]{2,1,0:T(8,128)(2,1)S(1)}, bf16[8,512,256]{2,1,0:T(8,128)(2,1)}, u32[]{:S(2)}) copy-start(bf16[8,512,256]{2,1,0:T(8,128)(2,1)} %amp_ref.19) | copy-start | bytes 6291460
  175.8 21.0 %copy-start.5 = (bf16[2,2,512,256]{3,2,1,0:T(8,128)(2,1)S(1)}, bf16[2,2,512,256]{3,2,1,0:T(8,128)(2,1)}, u32[]{:S(2)}) copy-start(bf16[2,2,512,256]{3,2,1,0:T(8,128)(2,1)} %last.3.sums_ref) | copy-start | bytes 3145732
  175.8 21.0 %copy-start.8 = (f32[3]{0:T(128)S(1)}, f32[3]{0:T(128)}, u32[]{:S(2)}) copy-start(f32[3]{0:T(128)} %bragg_ref.15) | copy-start | bytes 40
  175.8 29.5 %collective-permute-start.2 = (bf16[2,2,512,256]{3,2,1,0:T(8,128)(2,1)}, bf16[2,2,512,256]{3,2,1,0:T(8,128)(2,1)}, u32[]{:S(2)}, u32[]{:S(2)}) collective-permute-start(bf16[2,2,512,256]{3,2,1,0:T(8,128)(2,1)} %last.3.sums_ref), channel_id=1, source_target_pairs={{0,64},{64,0},{1,65},{65,1},{2,66},{66,2},{3,67},{67,3},{4,68},{68... | collective-permute-start | bytes 3145736 | tf_op jit(solution)/shard_map/ppermute | solution.py:666
  195.3 17.1 %collective-permute-start.1 = (bf16[1,2,512,256]{3,2,1,0:T(8,128)(2,1)}, bf16[1,2,512,256]{3,2,1,0:T(8,128)(2,1)S(1)}, u32[]{:S(2)}, u32[]{:S(2)}) collective-permute-start(bf16[1,2,512,256]{3,2,1,0:T(8,128)(2,1)} %get-tuple-element.27.sums_ref), channel_id=1, source_target_pairs={{0,64},{64,0},{1,65},{65,1},{2,66},{66,2},{3,67},{67,3},{4,68},{68... | collective-permute-start | bytes 1572872 | tf_op jit(solution)/shard_map/ppermute | solution.py:666
  195.7 28.0 %collective-permute-start = (bf16[1,2,512,256]{3,2,1,0:T(8,128)(2,1)}, bf16[1,2,512,256]{3,2,1,0:T(8,128)(2,1)S(1)}, u32[]{:S(2)}, u32[]{:S(2)}) collective-permute-start(bf16[1,2,512,256]{3,2,1,0:T(8,128)(2,1)} %get-tuple-element.26.sums_ref), channel_id=1, source_target_pairs={{0,64},{64,0},{1,65},{65,1},{2,66},{66,2},{3,67},{67,3},{4,68},{68... | collective-permute-start | bytes 1572872 | tf_op jit(solution)/shard_map/ppermute | solution.py:666
  196.8 2.8 %copy-start.2 = (bf16[3,8,512,256]{3,2,1,0:T(8,128)(2,1)S(1)}, bf16[3,8,512,256]{3,2,1,0:T(8,128)(2,1)}, u32[]{:S(2)}) copy-start(bf16[3,8,512,256]{3,2,1,0:T(8,128)(2,1)} %disp_ref.15) | copy-start | bytes 18874372
  199.6 2.3 %copy-start.7 = (bf16[1,2,512,256]{3,2,1,0:T(8,128)(2,1)S(1)}, bf16[1,2,512,256]{3,2,1,0:T(8,128)(2,1)}, u32[]{:S(2)}) copy-start(bf16[1,2,512,256]{3,2,1,0:T(8,128)(2,1)} %get-tuple-element.27.sums_ref) | copy-start | bytes 1572868
  201.9 1.7 copy-start.6
  212.4 11.2 %copy-start.4 = (bf16[8,512,256]{2,1,0:T(8,128)(2,1)S(1)}, bf16[8,512,256]{2,1,0:T(8,128)(2,1)}, u32[]{:S(2)}) copy-start(bf16[8,512,256]{2,1,0:T(8,128)(2,1)} %amp_ref.19) | copy-start | bytes 6291460
  223.6 1.7 copy-start.1

commit v3 on v2

--- a/solution.py
+++ b/solution.py
@@ -10,7 +10,7 @@
 
 step_size = 0.5
 both_axes = ("slab", "spec")
-vmem_limit = 60 * 1024 * 1024
+vmem_limit = 62 * 1024 * 1024
 small_limit = 36 * 1024 * 1024
 cos_terms = (
     0.9999992117703129, -19.738980419471183, 64.92865850463387,
@@ -284,7 +284,7 @@
     @pl.when(step < 4)
     def _():
         lanes = pl.ds(pl.multiple_of(step * frames, frames), frames)
-        tile = 256
+        tile = 512
 
         def body(turn, carry):
             at = pl.ds(pl.multiple_of(turn * tile, tile), tile)
@@ -307,18 +307,18 @@
 
         def body(turn, carry):
             columns = [[], []]
-            for sub in range(2):
-                real, imag = table_rows(big_real, big_imag, small, 2 * turn + sub)
+            for sub in range(8):
+                real, imag = table_rows(big_real, big_imag, small, 8 * turn + sub)
                 columns[0].append(jnp.where(low, real, pltpu.roll(imag, 2, 0)))
                 columns[1].append(jnp.where(low, -imag, pltpu.roll(real, 2, 0)))
-            at = pl.ds(pl.multiple_of(16 * turn, 16), 16)
+            at = pl.ds(pl.multiple_of(64 * turn, 64), 64)
             for column in range(2):
                 matrix[at, column * size : (column + 1) * size] = jnp.concatenate(
                     columns[column], axis=0
                 ).astype(jnp.bfloat16)
             return carry
 
-        lax.fori_loop(0, size // 16, body, 0)
+        lax.fori_loop(0, size // 64, body, 0)
         section_ref[0] = section[step - 4]
         held[step - 4] = dot(matrix[...], section[step - 4])
 

time: 226 us -> 224 us (level)
    unnamed x25 -> x19, local copies, waits for them, and re-layouts: 7.46 us -> 7.79 us
where the time goes in v3:
time: 224 us; the launch traced here: 223 us
  Pallas kernels  124 us (55%)
  waiting for transfers between devices  57.8 us (26%)
  starting transfers between devices  33 us (15%)
  local copies, waits for them, and re-layouts  8.04 us (4%)
    all_to_all x5, waiting for transfers between devices, exchange(): lax.all_to_all(blocks, both_axes, split_axis=0, concat_axis=0, tiled=True)  46 us
    pallas_call x2, Pallas kernels, middle(): pl.pallas_call(middle_kernel, grid=(8,), in_specs=[pl.BlockSpec(memory_sp...  32.1 us
    all_to_all x5, starting transfers between devices, exchange(): lax.all_to_all(blocks, both_axes, split_axis=0, concat_axis=0, tiled=True)  30 us
    pallas_call x2, Pallas kernels, last(): pl.pallas_call(last_kernel, grid_spec=pltpu.PrefetchScalarGridSpec(num_sc...  21 us
    pallas_call x1, Pallas kernels, first_half(): pl.pallas_call(first_kernel, grid_spec=pltpu.PrefetchScalarGridSpec(num_s...  19.6 us
    pallas_call x6, Pallas kernels, finish(): pl.pallas_call(finish_kernel, grid_spec=pltpu.PrefetchScalarGridSpec(num_...  12.4 us
    ppermute x3, waiting for transfers between devices, swap(): return lax.ppermute(values, 'spec', [(0, 1), (1, 0)])  11.8 us
    pallas_call x1, Pallas kernels, waves(): pl.pallas_call(wave_kernel, grid_spec=pltpu.PrefetchScalarGridSpec(num_sc...  11.5 us
  transfers between devices with their start and end apart: 8, of which 7 were waited for; matrix products, arithmetic and copies ran while one was open for 1% of the time, Pallas kernels for 46%

profile of v3, /device:TPU:1, one launch (start us, length us, event | category | flops | bytes accessed | tf_op | source)
XLA Modules:
  0.0 223.3 jit_solution(15770823401537995506)
XLA Ops:
  0.6 19.6 %first_half.1 = (bf16[4,1024,512]{2,1,0:T(8,128)(2,1)}, bf16[128,16,512]{2,1,0:T(8,128)(2,1)}) custom-call(s32[1]{0:T(128)} %bitcast.place_ref, f32[3]{0:T(128)} %bragg_ref.15, f32[4]{0:T(128)} %scales_ref.11, bf16[3,8,512,256]{3,2,1,0:T(8,128)(2,1)} %disp_ref.15, bf16[8,512,256]{2,1,0:T(8,128)(2,1)} %amp_ref.19, s32[8,512,256]{2,1,0:T(8,128)} %mask_ref.3), custom_call_target="tpu_custom_call" | custom-call | flops 8999999488 | bytes 14680064 | tf_op jit(solution)/shard_map/first_half/pallas_call | solution.py:333
  20.2 12.0 %all-to-all-start = ((bf16[128,16,512]{2,1,0:T(8,128)(2,1)}), bf16[128,16,512]{2,1,0:T(8,128)(2,1)}, u32[]{:S(2)}, u32[]{:S(2)}) async-start(bf16[128,16,512]{2,1,0:T(8,128)(2,1)} %get-tuple-element.21), calls=%async_computation | async-start | bytes 4194304 | tf_op jit(solution)/shard_map/all_to_all | solution.py:662
  32.2 6.4 %row_matrices.1.rows_ref = bf16[4,2,512,1024]{3,2,1,0:T(8,128)(2,1)} custom-call(f32[4]{0:T(128)} %scales_ref.11), custom_call_target="tpu_custom_call" | custom-call | flops 4000000000 | bytes 8388608 | tf_op jit(solution)/shard_map/row_matrices/pallas_call | solution.py:127
  38.5 7.1 %second_half.1.refs_0_ = bf16[128,16,512]{2,1,0:T(8,128)(2,1)} custom-call(bf16[4,1024,512]{2,1,0:T(8,128)(2,1)} %get-tuple-element.20.section_ref, bf16[4,2,512,1024]{3,2,1,0:T(8,128)(2,1)} %row_matrices.1.rows_ref), custom_call_target="tpu_custom_call" | custom-call | flops 3000000000 | bytes 10485760 | tf_op jit(solution)/shard_map/second_half/pallas_call | solution.py:375
  45.6 11.5 %waves.1.refs_2_.wave_ref = bf16[4,4,512,512]{3,2,1,0:T(8,128)(2,1)} custom-call(s32[1]{0:T(128)} %bitcast.place_ref, f32[3]{0:T(128)} %bragg_ref.15, f32[4]{0:T(128)} %scales_ref.11, bf16[3,8,512,256]{3,2,1,0:T(8,128)(2,1)} %disp_ref.15, bf16[8,512,256]{2,1,0:T(8,128)(2,1)} %amp_ref.19, s32[8,512,256]{2,1,0:T(8,128)} %mask_ref.3), custom_call_target="tpu_custom_call" | custom-call | flops 10000000000 | bytes 25165824 | tf_op jit(solution)/shard_map/waves/pallas_call | solution.py:255
  57.2 5.7 %all-to-all-done.refs_1_.got_ref = bf16[128,16,512]{2,1,0:T(8,128)(2,1)} async-done(((bf16[128,16,512]{2,1,0:T(8,128)(2,1)}), bf16[128,16,512]{2,1,0:T(8,128)(2,1)}, u32[]{:S(2)}, u32[]{:S(2)}) %all-to-all-start) | async-done | bytes 2097184 | tf_op jit(solution)/shard_map/all_to_all | solution.py:662
  62.8 0.0 copy-start.7
  62.8 4.9 %all-to-all-start.1 = ((bf16[128,16,512]{2,1,0:T(8,128)(2,1)}), bf16[128,16,512]{2,1,0:T(8,128)(2,1)}, u32[]{:S(2)}, u32[]{:S(2)}) async-start(bf16[128,16,512]{2,1,0:T(8,128)(2,1)} %after.4), calls=%async_computation.1 | async-start | bytes 4194304 | tf_op jit(solution)/shard_map/all_to_all | solution.py:662
  67.7 0.0 copy-done.7
  67.7 0.2 constant_dynamic-slice_fusion
  67.9 0.4 copy.26
  68.3 0.1 fusion
  68.4 1.0 copy.28.counts_ref
  69.4 5.7 %column_matrices.1 = (bf16[4,2,512,1024]{3,2,1,0:T(8,128)(2,1)}, bf16[4,256,512]{2,1,0:T(8,128)(2,1)}) custom-call(f32[4]{0:T(128)} %scales_ref.11), custom_call_target="tpu_custom_call" | custom-call | flops 4000000000 | bytes 8388608 | tf_op jit(solution)/shard_map/column_matrices/pallas_call | solution.py:171
  75.1 16.1 %middle.3.refs_0_ = bf16[128,32,256]{2,1,0:T(8,128)(2,1)} custom-call(f32[4]{0:T(128)} %weights_ref.3, bf16[128,16,512]{2,1,0:T(8,128)(2,1)} %all-to-all-done.refs_1_.got_ref, s32[512,256]{1,0:T(8,128)} %copy.28.counts_ref, bf16[4,2,512,1024]{3,2,1,0:T(8,128)(2,1)} %get-tuple-element.22.cols_ref.real_cols_ref.imag_cols_ref, ...), custom_call_target="tpu_custom_call" | custom-call | flops 8999999488 | bytes 23068672 | tf_op jit(solution)/shard_map/middle/pallas_call | solution.py:456
  91.2 7.3 %all-to-all-done.1.got_ref.refs_1_ = bf16[128,16,512]{2,1,0:T(8,128)(2,1)} async-done(((bf16[128,16,512]{2,1,0:T(8,128)(2,1)}), bf16[128,16,512]{2,1,0:T(8,128)(2,1)}, u32[]{:S(2)}, u32[]{:S(2)}) %all-to-all-start.1) | async-done | bytes 2097184 | tf_op jit(solution)/shard_map/all_to_all | solution.py:662
  98.5 4.9 %all-to-all-start.2 = ((bf16[128,32,256]{2,1,0:T(8,128)(2,1)}), bf16[128,32,256]{2,1,0:T(8,128)(2,1)}, u32[]{:S(2)}, u32[]{:S(2)}) async-start(bf16[128,32,256]{2,1,0:T(8,128)(2,1)} %after.5), calls=%async_computation.2 | async-start | bytes 4194304 | tf_op jit(solution)/shard_map/all_to_all | solution.py:662
  103.4 1.0 copy.27.counts_ref
  104.4 16.0 %middle.2 = (bf16[128,16,256]{2,1,0:T(8,128)(2,1)}, bf16[128,16,256]{2,1,0:T(8,128)(2,1)}) custom-call(f32[4]{0:T(128)} %weights_ref.3, bf16[128,16,512]{2,1,0:T(8,128)(2,1)} %all-to-all-done.1.got_ref.refs_1_, s32[512,256]{1,0:T(8,128)} %copy.27.counts_ref, bf16[4,2,512,1024]{3,2,1,0:T(8,128)(2,1)} %get-tuple-element.22.cols_ref.real_cols_ref.imag_cols_ref, ...), custom_call_target="tpu_custom_call" | custom-call | flops 8999999488 | bytes 23068672 | tf_op jit(solution)/shard_map/middle/pallas_call | solution.py:456
  120.4 13.6 %all-to-all-done.2.got_ref.refs_1_ = bf16[128,32,256]{2,1,0:T(8,128)(2,1)} async-done(((bf16[128,32,256]{2,1,0:T(8,128)(2,1)}), bf16[128,32,256]{2,1,0:T(8,128)(2,1)}, u32[]{:S(2)}, u32[]{:S(2)}) %all-to-all-start.2) | async-done | bytes 2097184 | tf_op jit(solution)/shard_map/all_to_all | solution.py:662
  134.0 3.6 %all-to-all-start.3 = ((bf16[128,16,256]{2,1,0:T(8,128)(2,1)}), bf16[128,16,256]{2,1,0:T(8,128)(2,1)S(1)}, u32[]{:S(2)}, u32[]{:S(2)}) async-start(bf16[128,16,256]{2,1,0:T(8,128)(2,1)} %after.6), calls=%async_computation.3 | async-start | bytes 2097152 | tf_op jit(solution)/shard_map/all_to_all | solution.py:662
  137.7 8.0 %early_part.1.refs_1_.real_part_ref.imag_part_ref = bf16[4,2,512,512]{3,2,1,0:T(8,128)(2,1)} custom-call(bf16[128,32,256]{2,1,0:T(8,128)(2,1)} %all-to-all-done.2.got_ref.refs_1_, bf16[4,2,512,1024]{3,2,1,0:T(8,128)(2,1)} %get-tuple-element.22.cols_ref.real_cols_ref.imag_cols_ref), custom_call_target="tpu_custom_call" | custom-call | flops 4000000000 | bytes 10485760 | tf_op jit(solution)/shard_map/early_part/pallas_call | solution.py:509
  145.6 11.9 %all-to-all-done.3.refs_2_.late_ref = bf16[128,16,256]{2,1,0:T(8,128)(2,1)S(1)} async-done(((bf16[128,16,256]{2,1,0:T(8,128)(2,1)}), bf16[128,16,256]{2,1,0:T(8,128)(2,1)S(1)}, u32[]{:S(2)}, u32[]{:S(2)}) %all-to-all-start.3) | async-done | bytes 1048608 | tf_op jit(solution)/shard_map/all_to_all | solution.py:662
  157.6 0.0 copy-start.6
  157.6 1.0 copy-done.6
  158.6 4.7 %all-to-all-start.4 = ((bf16[128,16,256]{2,1,0:T(8,128)(2,1)}), bf16[128,16,256]{2,1,0:T(8,128)(2,1)}, u32[]{:S(2)}, u32[]{:S(2)}) async-start(bf16[128,16,256]{2,1,0:T(8,128)(2,1)} %after.7), calls=%async_computation.4 | async-start | bytes 2097152 | tf_op jit(solution)/shard_map/all_to_all | solution.py:662
  163.3 10.5 %last.3.sums_ref = bf16[2,2,512,256]{3,2,1,0:T(8,128)(2,1)} custom-call(s32[1]{0:T(128)} %bitcast.place_ref, f32[4]{0:T(128)} %scales_ref.11, bf16[128,16,256]{2,1,0:T(8,128)(2,1)} %copy-done.6, bf16[4,2,512,1024]{3,2,1,0:T(8,128)(2,1)} %get-tuple-element.22.cols_ref.real_cols_ref.imag_cols_ref, ...), custom_call_target="tpu_custom_call" | custom-call | flops 4000000000 | bytes 16777216 | tf_op jit(solution)/shard_map/last/pallas_call | solution.py:586
  173.8 0.0 copy-start.2
  173.8 0.0 copy-start.5
  173.8 1.5 collective-permute-start.2
  175.2 7.5 %all-to-all-done.4.late_ref = bf16[128,16,256]{2,1,0:T(8,128)(2,1)} async-done(((bf16[128,16,256]{2,1,0:T(8,128)(2,1)}), bf16[128,16,256]{2,1,0:T(8,128)(2,1)}, u32[]{:S(2)}, u32[]{:S(2)}) %all-to-all-start.4) | async-done | bytes 1048608 | tf_op jit(solution)/shard_map/all_to_all | solution.py:662
  182.8 10.5 %last.2 = (bf16[1,2,512,256]{3,2,1,0:T(8,128)(2,1)}, bf16[1,2,512,256]{3,2,1,0:T(8,128)(2,1)}) custom-call(s32[1]{0:T(128)} %bitcast.place_ref, f32[4]{0:T(128)} %scales_ref.11, bf16[128,16,256]{2,1,0:T(8,128)(2,1)} %all-to-all-done.4.late_ref, bf16[4,2,512,1024]{3,2,1,0:T(8,128)(2,1)} %get-tuple-element.22.cols_ref.real_cols_ref.imag_cols_ref, ...), custom_call_target="tpu_custom_call" | custom-call | flops 4000000000 | bytes 16777216 | tf_op jit(solution)/shard_map/last/pallas_call | solution.py:586
  193.3 0.4 collective-permute-start.1
  193.6 1.1 collective-permute-start
  194.7 0.0 copy-done.2
  194.7 0.0 copy-done.5
  194.7 0.0 copy-start
  194.7 2.8 %copy-done = bf16[3,8,512,256]{3,2,1,0:T(8,128)(2,1)S(1)} copy-done((bf16[3,8,512,256]{3,2,1,0:T(8,128)(2,1)S(1)}, bf16[3,8,512,256]{3,2,1,0:T(8,128)(2,1)}, u32[]{:S(2)}) %copy-start) | copy-done | bytes 6291480
  197.5 0.0 copy-start.1
  197.5 1.6 copy-done.1
  199.1 0.0 copy-start.4
  199.1 2.3 %finish.6 = (f32[8,512,256]{2,1,0:T(8,128)}, bf16[3,8,512,256]{3,2,1,0:T(8,128)(2,1)}) custom-call(s32[1]{0:T(128)} %bitcast.place_ref, f32[3]{0:T(128)S(1)} %copy-done.5, bf16[2,2,512,256]{3,2,1,0:T(8,128)(2,1)S(1)} %copy-done.2, bf16[8,512,256]{2,1,0:T(8,128)(2,1)S(1)} %copy-done.1, bf16[3,8,512,256]{3,2,1,0:T(8,128)(2,1)S(1)} %copy-done), custom_call_target="tpu_custom_call" | custom-call | flops 10000000 | bytes 6291456 | tf_op jit(solution)/shard_map/finish/pallas_call | solution.py:637
  201.5 0.0 copy-done.4
  201.5 0.0 copy-start.3
  201.5 1.7 finish.7
  203.1 0.0 copy-done.3
  203.1 1.7 finish.8
  204.8 0.0 collective-permute-done.2.sums_ref
  204.8 3.2 %finish.9 = (f32[8,512,256]{2,1,0:T(8,128)}, bf16[3,8,512,256]{3,2,1,0:T(8,128)(2,1)}) custom-call(s32[1]{0:T(128)} %bitcast.place_ref, f32[3]{0:T(128)S(1)} %copy-done.5, bf16[2,2,512,256]{3,2,1,0:T(8,128)(2,1)} %collective-permute-done.2.sums_ref, bf16[8,512,256]{2,1,0:T(8,128)(2,1)S(1)} %copy-done.1, ...), custom_call_target="tpu_custom_call", output_to_operand_aliasing={{0}: (5, {}), {1}: (6, {})} | custom-call | flops 10000000 | bytes 6291456 | tf_op jit(solution)/shard_map/finish/pallas_call | solution.py:637
  208.1 2.3 %collective-permute-done.1.sums_ref = bf16[1,2,512,256]{3,2,1,0:T(8,128)(2,1)S(1)} collective-permute-done((bf16[1,2,512,256]{3,2,1,0:T(8,128)(2,1)}, bf16[1,2,512,256]{3,2,1,0:T(8,128)(2,1)S(1)}, u32[]{:S(2)}, u32[]{:S(2)}) %collective-permute-start.1) | collective-permute-done | bytes 524320 | tf_op jit(solution)/shard_map/ppermute | solution.py:666
  210.4 1.7 finish.10
  212.1 9.5 %collective-permute-done.sums_ref = bf16[1,2,512,256]{3,2,1,0:T(8,128)(2,1)S(1)} collective-permute-done((bf16[1,2,512,256]{3,2,1,0:T(8,128)(2,1)}, bf16[1,2,512,256]{3,2,1,0:T(8,128)(2,1)S(1)}, u32[]{:S(2)}, u32[]{:S(2)}) %collective-permute-start) | collective-permute-done | bytes 524320 | tf_op jit(solution)/shard_map/ppermute | solution.py:666
  221.6 1.7 finish.11
  (4 shorter events, 0.0 us)
Async XLA Ops:
  20.2 42.6 %all-to-all-start = ((bf16[128,16,512]{2,1,0:T(8,128)(2,1)}), bf16[128,16,512]{2,1,0:T(8,128)(2,1)}, u32[]{:S(2)}, u32[]{:S(2)}) async-start(bf16[128,16,512]{2,1,0:T(8,128)(2,1)} %get-tuple-element.21), calls=%async_computation | async-start | bytes 4194304 | tf_op jit(solution)/shard_map/all_to_all | solution.py:662
  62.8 4.9 %copy-start.7 = (s32[512,8,128]{2,1,0:T(8,128)S(1)}, s32[512,8,128]{2,1,0:T(8,128)}, u32[]{:S(2)}) copy-start(s32[512,8,128]{2,1,0:T(8,128)} %param.10) | copy-start | bytes 6291460
  62.8 35.6 %all-to-all-start.1 = ((bf16[128,16,512]{2,1,0:T(8,128)(2,1)}), bf16[128,16,512]{2,1,0:T(8,128)(2,1)}, u32[]{:S(2)}, u32[]{:S(2)}) async-start(bf16[128,16,512]{2,1,0:T(8,128)(2,1)} %after.4), calls=%async_computation.1 | async-start | bytes 4194304 | tf_op jit(solution)/shard_map/all_to_all | solution.py:662
  98.5 35.5 %all-to-all-start.2 = ((bf16[128,32,256]{2,1,0:T(8,128)(2,1)}), bf16[128,32,256]{2,1,0:T(8,128)(2,1)}, u32[]{:S(2)}, u32[]{:S(2)}) async-start(bf16[128,32,256]{2,1,0:T(8,128)(2,1)} %after.5), calls=%async_computation.2 | async-start | bytes 4194304 | tf_op jit(solution)/shard_map/all_to_all | solution.py:662
  134.0 23.6 %all-to-all-start.3 = ((bf16[128,16,256]{2,1,0:T(8,128)(2,1)}), bf16[128,16,256]{2,1,0:T(8,128)(2,1)S(1)}, u32[]{:S(2)}, u32[]{:S(2)}) async-start(bf16[128,16,256]{2,1,0:T(8,128)(2,1)} %after.6), calls=%async_computation.3 | async-start | bytes 2097152 | tf_op jit(solution)/shard_map/all_to_all | solution.py:662
  157.6 1.0 copy-start.6
  158.6 24.2 %all-to-all-start.4 = ((bf16[128,16,256]{2,1,0:T(8,128)(2,1)}), bf16[128,16,256]{2,1,0:T(8,128)(2,1)}, u32[]{:S(2)}, u32[]{:S(2)}) async-start(bf16[128,16,256]{2,1,0:T(8,128)(2,1)} %after.7), calls=%async_computation.4 | async-start | bytes 2097152 | tf_op jit(solution)/shard_map/all_to_all | solution.py:662
  173.8 21.0 %copy-start.2 = (bf16[2,2,512,256]{3,2,1,0:T(8,128)(2,1)S(1)}, bf16[2,2,512,256]{3,2,1,0:T(8,128)(2,1)}, u32[]{:S(2)}) copy-start(bf16[2,2,512,256]{3,2,1,0:T(8,128)(2,1)} %last.3.sums_ref) | copy-start | bytes 3145732
  173.8 21.0 %copy-start.5 = (f32[3]{0:T(128)S(1)}, f32[3]{0:T(128)}, u32[]{:S(2)}) copy-start(f32[3]{0:T(128)} %bragg_ref.15) | copy-start | bytes 40
  173.8 31.1 %collective-permute-start.2 = (bf16[2,2,512,256]{3,2,1,0:T(8,128)(2,1)}, bf16[2,2,512,256]{3,2,1,0:T(8,128)(2,1)}, u32[]{:S(2)}, u32[]{:S(2)}) collective-permute-start(bf16[2,2,512,256]{3,2,1,0:T(8,128)(2,1)} %last.3.sums_ref), channel_id=1, source_target_pairs={{0,64},{64,0},{1,65},{65,1},{2,66},{66,2},{3,67},{67,3},{4,68},{68... | collective-permute-start | bytes 3145736 | tf_op jit(solution)/shard_map/ppermute | solution.py:666
  193.3 17.1 %collective-permute-start.1 = (bf16[1,2,512,256]{3,2,1,0:T(8,128)(2,1)}, bf16[1,2,512,256]{3,2,1,0:T(8,128)(2,1)S(1)}, u32[]{:S(2)}, u32[]{:S(2)}) collective-permute-start(bf16[1,2,512,256]{3,2,1,0:T(8,128)(2,1)} %get-tuple-element.27.sums_ref), channel_id=1, source_target_pairs={{0,64},{64,0},{1,65},{65,1},{2,66},{66,2},{3,67},{67,3},{4,68},{68... | collective-permute-start | bytes 1572872 | tf_op jit(solution)/shard_map/ppermute | solution.py:666
  193.6 28.0 %collective-permute-start = (bf16[1,2,512,256]{3,2,1,0:T(8,128)(2,1)}, bf16[1,2,512,256]{3,2,1,0:T(8,128)(2,1)S(1)}, u32[]{:S(2)}, u32[]{:S(2)}) collective-permute-start(bf16[1,2,512,256]{3,2,1,0:T(8,128)(2,1)} %get-tuple-element.26.sums_ref), channel_id=1, source_target_pairs={{0,64},{64,0},{1,65},{65,1},{2,66},{66,2},{3,67},{67,3},{4,68},{68... | collective-permute-start | bytes 1572872 | tf_op jit(solution)/shard_map/ppermute | solution.py:666
  194.7 2.8 %copy-start = (bf16[3,8,512,256]{3,2,1,0:T(8,128)(2,1)S(1)}, bf16[3,8,512,256]{3,2,1,0:T(8,128)(2,1)}, u32[]{:S(2)}) copy-start(bf16[3,8,512,256]{3,2,1,0:T(8,128)(2,1)} %disp_ref.15) | copy-start | bytes 18874372
  197.5 1.6 copy-start.1
  199.1 2.3 %copy-start.4 = (bf16[1,2,512,256]{3,2,1,0:T(8,128)(2,1)S(1)}, bf16[1,2,512,256]{3,2,1,0:T(8,128)(2,1)}, u32[]{:S(2)}) copy-start(bf16[1,2,512,256]{3,2,1,0:T(8,128)(2,1)} %get-tuple-element.27.sums_ref) | copy-start | bytes 1572868
  201.5 1.7 copy-start.3

commit v4 on v3

--- a/solution.py
+++ b/solution.py
@@ -33,7 +33,7 @@
 
 
 def cos_sin_turns(turns, cos_series=cos_terms, sin_series=sin_terms):
-    rest = turns - jnp.floor(turns + 0.5)
+    rest = turns - jnp.round(turns)
     square = rest * rest
     cosine = jnp.full_like(square, cos_series[-1])
     sine = jnp.full_like(square, sin_series[-1])
@@ -284,43 +284,35 @@
     @pl.when(step < 4)
     def _():
         lanes = pl.ds(pl.multiple_of(step * frames, frames), frames)
-        tile = 512
-
-        def body(turn, carry):
-            at = pl.ds(pl.multiple_of(turn * tile, tile), tile)
-            low = pl.ds(pl.multiple_of(cells_y + turn * tile, tile), tile)
-
-            def use(member, wave):
+        tile = cells_y // 2
+        for turn in range(2):
+            at = slice(turn * tile, (turn + 1) * tile)
+            low = slice(cells_y + turn * tile, cells_y + (turn + 1) * tile)
+
+            def use(member, wave, at=at, low=low):
                 both = dot(wave, zf[member]).astype(jnp.bfloat16)
                 section[member, at, lanes] = both[:, 0:frames]
                 section[member, low, lanes] = both[:, frames : 2 * frames]
 
             wave_chunk(bragg_ref, scales_ref, disp_ref, amp_ref, mask_ref, 0, at, use)
-            return carry
-
-        lax.fori_loop(0, cells_y // tile, body, 0)
 
     @pl.when(step >= 4)
     def _():
         small = fill_tables(big_real, big_imag, iota((1, size), 1), size, scales_ref[step - 4])
         low = (iota((8, size), 0) & 2) == 0
 
-        def body(turn, carry):
+        section_ref[0] = section[step - 4]
+        chunk = size // 2
+        for piece in range(2):
             columns = [[], []]
-            for sub in range(8):
-                real, imag = table_rows(big_real, big_imag, small, 8 * turn + sub)
+            for turn in range(piece * chunk // 8, (piece + 1) * chunk // 8):
+                real, imag = table_rows(big_real, big_imag, small, turn)
                 columns[0].append(jnp.where(low, real, pltpu.roll(imag, 2, 0)))
                 columns[1].append(jnp.where(low, -imag, pltpu.roll(real, 2, 0)))
-            at = pl.ds(pl.multiple_of(64 * turn, 64), 64)
-            for column in range(2):
-                matrix[at, column * size : (column + 1) * size] = jnp.concatenate(
-                    columns[column], axis=0
-                ).astype(jnp.bfloat16)
-            return carry
-
-        lax.fori_loop(0, size // 64, body, 0)
-        section_ref[0] = section[step - 4]
-        held[step - 4] = dot(matrix[...], section[step - 4])
+            both = [jnp.concatenate(column, axis=0).astype(jnp.bfloat16) for column in columns]
+            held[step - 4, piece * chunk : (piece + 1) * chunk, :] = dot(
+                jnp.concatenate(both, axis=1), section[step - 4]
+            )
 
     @pl.when(step == 7)
     def _():

time: 224 us -> 222 us (level)
  Pallas kernels: 124 us -> 121 us
where the time goes in v4:
time: 222 us; the launch traced here: 221 us
  Pallas kernels  121 us (55%)
  waiting for transfers between devices  58 us (26%)
  starting transfers between devices  33 us (15%)
  local copies, waits for them, and re-layouts  8.04 us (4%)
    all_to_all x5, waiting for transfers between devices, exchange(): lax.all_to_all(blocks, both_axes, split_axis=0, concat_axis=0, tiled=True)  46.2 us
    pallas_call x2, Pallas kernels, middle(): pl.pallas_call(middle_kernel, grid=(8,), in_specs=[pl.BlockSpec(memory_sp...  32.1 us
    all_to_all x5, starting transfers between devices, exchange(): lax.all_to_all(blocks, both_axes, split_axis=0, concat_axis=0, tiled=True)  30 us
    pallas_call x2, Pallas kernels, last(): pl.pallas_call(last_kernel, grid_spec=pltpu.PrefetchScalarGridSpec(num_sc...  21 us
    pallas_call x1, Pallas kernels, first_half(): pl.pallas_call(first_kernel, grid_spec=pltpu.PrefetchScalarGridSpec(num_s...  17.4 us
    pallas_call x6, Pallas kernels, finish(): pl.pallas_call(finish_kernel, grid_spec=pltpu.PrefetchScalarGridSpec(num_...  12.4 us
    ppermute x3, waiting for transfers between devices, swap(): return lax.ppermute(values, 'spec', [(0, 1), (1, 0)])  11.8 us
    pallas_call x1, Pallas kernels, waves(): pl.pallas_call(wave_kernel, grid_spec=pltpu.PrefetchScalarGridSpec(num_sc...  11.3 us
  transfers between devices with their start and end apart: 8, of which 7 were waited for; matrix products, arithmetic and copies ran while one was open for 1% of the time, Pallas kernels for 46%

profile of v4, /device:TPU:1, one launch (start us, length us, event | category | flops | bytes accessed | tf_op | source)
XLA Modules:
  0.0 221.2 jit_solution(4812362645738917541)
XLA Ops:
  0.6 17.4 %first_half.1 = (bf16[4,1024,512]{2,1,0:T(8,128)(2,1)}, bf16[128,16,512]{2,1,0:T(8,128)(2,1)}) custom-call(s32[1]{0:T(128)} %bitcast.place_ref, f32[3]{0:T(128)} %bragg_ref.15, f32[4]{0:T(128)} %scales_ref.11, bf16[3,8,512,256]{3,2,1,0:T(8,128)(2,1)} %disp_ref.15, bf16[8,512,256]{2,1,0:T(8,128)(2,1)} %amp_ref.19, s32[8,512,256]{2,1,0:T(8,128)} %mask_ref.3), custom_call_target="tpu_custom_call" | custom-call | flops 8999999488 | bytes 14680064 | tf_op jit(solution)/shard_map/first_half/pallas_call | solution.py:325
  18.1 11.9 %all-to-all-start = ((bf16[128,16,512]{2,1,0:T(8,128)(2,1)}), bf16[128,16,512]{2,1,0:T(8,128)(2,1)}, u32[]{:S(2)}, u32[]{:S(2)}) async-start(bf16[128,16,512]{2,1,0:T(8,128)(2,1)} %get-tuple-element.21), calls=%async_computation | async-start | bytes 4194304 | tf_op jit(solution)/shard_map/all_to_all | solution.py:654
  30.0 6.3 %row_matrices.1.rows_ref = bf16[4,2,512,1024]{3,2,1,0:T(8,128)(2,1)} custom-call(f32[4]{0:T(128)} %scales_ref.11), custom_call_target="tpu_custom_call" | custom-call | flops 4000000000 | bytes 8388608 | tf_op jit(solution)/shard_map/row_matrices/pallas_call | solution.py:127
  36.4 7.1 %second_half.1.refs_0_ = bf16[128,16,512]{2,1,0:T(8,128)(2,1)} custom-call(bf16[4,1024,512]{2,1,0:T(8,128)(2,1)} %get-tuple-element.20.section_ref, bf16[4,2,512,1024]{3,2,1,0:T(8,128)(2,1)} %row_matrices.1.rows_ref), custom_call_target="tpu_custom_call" | custom-call | flops 3000000000 | bytes 10485760 | tf_op jit(solution)/shard_map/second_half/pallas_call | solution.py:367
  43.5 11.3 %waves.1.refs_2_.wave_ref = bf16[4,4,512,512]{3,2,1,0:T(8,128)(2,1)} custom-call(s32[1]{0:T(128)} %bitcast.place_ref, f32[3]{0:T(128)} %bragg_ref.15, f32[4]{0:T(128)} %scales_ref.11, bf16[3,8,512,256]{3,2,1,0:T(8,128)(2,1)} %disp_ref.15, bf16[8,512,256]{2,1,0:T(8,128)(2,1)} %amp_ref.19, s32[8,512,256]{2,1,0:T(8,128)} %mask_ref.3), custom_call_target="tpu_custom_call" | custom-call | flops 10000000000 | bytes 25165824 | tf_op jit(solution)/shard_map/waves/pallas_call | solution.py:255
  54.8 5.9 %all-to-all-done.refs_1_.got_ref = bf16[128,16,512]{2,1,0:T(8,128)(2,1)} async-done(((bf16[128,16,512]{2,1,0:T(8,128)(2,1)}), bf16[128,16,512]{2,1,0:T(8,128)(2,1)}, u32[]{:S(2)}, u32[]{:S(2)}) %all-to-all-start) | async-done | bytes 2097184 | tf_op jit(solution)/shard_map/all_to_all | solution.py:654
  60.7 0.0 copy-start.7
  60.7 4.9 %all-to-all-start.1 = ((bf16[128,16,512]{2,1,0:T(8,128)(2,1)}), bf16[128,16,512]{2,1,0:T(8,128)(2,1)}, u32[]{:S(2)}, u32[]{:S(2)}) async-start(bf16[128,16,512]{2,1,0:T(8,128)(2,1)} %after.4), calls=%async_computation.1 | async-start | bytes 4194304 | tf_op jit(solution)/shard_map/all_to_all | solution.py:654
  65.5 0.0 copy-done.7
  65.6 0.2 constant_dynamic-slice_fusion
  65.7 0.4 copy.26
  66.1 0.1 fusion
  66.2 1.0 copy.28.counts_ref
  67.2 5.7 %column_matrices.1 = (bf16[4,2,512,1024]{3,2,1,0:T(8,128)(2,1)}, bf16[4,256,512]{2,1,0:T(8,128)(2,1)}) custom-call(f32[4]{0:T(128)} %scales_ref.11), custom_call_target="tpu_custom_call" | custom-call | flops 4000000000 | bytes 8388608 | tf_op jit(solution)/shard_map/column_matrices/pallas_call | solution.py:171
  72.9 16.1 %middle.3.refs_0_ = bf16[128,32,256]{2,1,0:T(8,128)(2,1)} custom-call(f32[4]{0:T(128)} %weights_ref.3, bf16[128,16,512]{2,1,0:T(8,128)(2,1)} %all-to-all-done.refs_1_.got_ref, s32[512,256]{1,0:T(8,128)} %copy.28.counts_ref, bf16[4,2,512,1024]{3,2,1,0:T(8,128)(2,1)} %get-tuple-element.22.cols_ref.real_cols_ref.imag_cols_ref, ...), custom_call_target="tpu_custom_call" | custom-call | flops 8999999488 | bytes 23068672 | tf_op jit(solution)/shard_map/middle/pallas_call | solution.py:448
  89.0 7.3 %all-to-all-done.1.got_ref.refs_1_ = bf16[128,16,512]{2,1,0:T(8,128)(2,1)} async-done(((bf16[128,16,512]{2,1,0:T(8,128)(2,1)}), bf16[128,16,512]{2,1,0:T(8,128)(2,1)}, u32[]{:S(2)}, u32[]{:S(2)}) %all-to-all-start.1) | async-done | bytes 2097184 | tf_op jit(solution)/shard_map/all_to_all | solution.py:654
  96.3 4.9 %all-to-all-start.2 = ((bf16[128,32,256]{2,1,0:T(8,128)(2,1)}), bf16[128,32,256]{2,1,0:T(8,128)(2,1)}, u32[]{:S(2)}, u32[]{:S(2)}) async-start(bf16[128,32,256]{2,1,0:T(8,128)(2,1)} %after.5), calls=%async_computation.2 | async-start | bytes 4194304 | tf_op jit(solution)/shard_map/all_to_all | solution.py:654
  101.2 1.0 copy.27.counts_ref
  102.3 16.0 %middle.2 = (bf16[128,16,256]{2,1,0:T(8,128)(2,1)}, bf16[128,16,256]{2,1,0:T(8,128)(2,1)}) custom-call(f32[4]{0:T(128)} %weights_ref.3, bf16[128,16,512]{2,1,0:T(8,128)(2,1)} %all-to-all-done.1.got_ref.refs_1_, s32[512,256]{1,0:T(8,128)} %copy.27.counts_ref, bf16[4,2,512,1024]{3,2,1,0:T(8,128)(2,1)} %get-tuple-element.22.cols_ref.real_cols_ref.imag_cols_ref, ...), custom_call_target="tpu_custom_call" | custom-call | flops 8999999488 | bytes 23068672 | tf_op jit(solution)/shard_map/middle/pallas_call | solution.py:448
  118.3 13.6 %all-to-all-done.2.got_ref.refs_1_ = bf16[128,32,256]{2,1,0:T(8,128)(2,1)} async-done(((bf16[128,32,256]{2,1,0:T(8,128)(2,1)}), bf16[128,32,256]{2,1,0:T(8,128)(2,1)}, u32[]{:S(2)}, u32[]{:S(2)}) %all-to-all-start.2) | async-done | bytes 2097184 | tf_op jit(solution)/shard_map/all_to_all | solution.py:654
  131.9 3.6 %all-to-all-start.3 = ((bf16[128,16,256]{2,1,0:T(8,128)(2,1)}), bf16[128,16,256]{2,1,0:T(8,128)(2,1)S(1)}, u32[]{:S(2)}, u32[]{:S(2)}) async-start(bf16[128,16,256]{2,1,0:T(8,128)(2,1)} %after.6), calls=%async_computation.3 | async-start | bytes 2097152 | tf_op jit(solution)/shard_map/all_to_all | solution.py:654
  135.5 8.0 %early_part.1.refs_1_.real_part_ref.imag_part_ref = bf16[4,2,512,512]{3,2,1,0:T(8,128)(2,1)} custom-call(bf16[128,32,256]{2,1,0:T(8,128)(2,1)} %all-to-all-done.2.got_ref.refs_1_, bf16[4,2,512,1024]{3,2,1,0:T(8,128)(2,1)} %get-tuple-element.22.cols_ref.real_cols_ref.imag_cols_ref), custom_call_target="tpu_custom_call" | custom-call | flops 4000000000 | bytes 10485760 | tf_op jit(solution)/shard_map/early_part/pallas_call | solution.py:501
  143.5 11.9 %all-to-all-done.3.refs_2_.late_ref = bf16[128,16,256]{2,1,0:T(8,128)(2,1)S(1)} async-done(((bf16[128,16,256]{2,1,0:T(8,128)(2,1)}), bf16[128,16,256]{2,1,0:T(8,128)(2,1)S(1)}, u32[]{:S(2)}, u32[]{:S(2)}) %all-to-all-start.3) | async-done | bytes 1048608 | tf_op jit(solution)/shard_map/all_to_all | solution.py:654
  155.4 0.0 copy-start.6
  155.4 1.0 copy-done.6
  156.4 4.7 %all-to-all-start.4 = ((bf16[128,16,256]{2,1,0:T(8,128)(2,1)}), bf16[128,16,256]{2,1,0:T(8,128)(2,1)}, u32[]{:S(2)}, u32[]{:S(2)}) async-start(bf16[128,16,256]{2,1,0:T(8,128)(2,1)} %after.7), calls=%async_computation.4 | async-start | bytes 2097152 | tf_op jit(solution)/shard_map/all_to_all | solution.py:654
  161.1 10.5 %last.3.sums_ref = bf16[2,2,512,256]{3,2,1,0:T(8,128)(2,1)} custom-call(s32[1]{0:T(128)} %bitcast.place_ref, f32[4]{0:T(128)} %scales_ref.11, bf16[128,16,256]{2,1,0:T(8,128)(2,1)} %copy-done.6, bf16[4,2,512,1024]{3,2,1,0:T(8,128)(2,1)} %get-tuple-element.22.cols_ref.real_cols_ref.imag_cols_ref, ...), custom_call_target="tpu_custom_call" | custom-call | flops 4000000000 | bytes 16777216 | tf_op jit(solution)/shard_map/last/pallas_call | solution.py:578
  171.6 0.0 copy-start.2
  171.6 0.0 copy-start.5
  171.6 1.5 collective-permute-start.2
  173.1 7.5 %all-to-all-done.4.late_ref = bf16[128,16,256]{2,1,0:T(8,128)(2,1)} async-done(((bf16[128,16,256]{2,1,0:T(8,128)(2,1)}), bf16[128,16,256]{2,1,0:T(8,128)(2,1)}, u32[]{:S(2)}, u32[]{:S(2)}) %all-to-all-start.4) | async-done | bytes 1048608 | tf_op jit(solution)/shard_map/all_to_all | solution.py:654
  180.6 10.5 %last.2 = (bf16[1,2,512,256]{3,2,1,0:T(8,128)(2,1)}, bf16[1,2,512,256]{3,2,1,0:T(8,128)(2,1)}) custom-call(s32[1]{0:T(128)} %bitcast.place_ref, f32[4]{0:T(128)} %scales_ref.11, bf16[128,16,256]{2,1,0:T(8,128)(2,1)} %all-to-all-done.4.late_ref, bf16[4,2,512,1024]{3,2,1,0:T(8,128)(2,1)} %get-tuple-element.22.cols_ref.real_cols_ref.imag_cols_ref, ...), custom_call_target="tpu_custom_call" | custom-call | flops 4000000000 | bytes 16777216 | tf_op jit(solution)/shard_map/last/pallas_call | solution.py:578
  191.1 0.4 collective-permute-start.1
  191.5 1.1 collective-permute-start
  192.6 0.0 copy-done.2
  192.6 0.0 copy-done.5
  192.6 0.0 copy-start
  192.6 2.8 %copy-done = bf16[3,8,512,256]{3,2,1,0:T(8,128)(2,1)S(1)} copy-done((bf16[3,8,512,256]{3,2,1,0:T(8,128)(2,1)S(1)}, bf16[3,8,512,256]{3,2,1,0:T(8,128)(2,1)}, u32[]{:S(2)}) %copy-start) | copy-done | bytes 6291480
  195.4 0.0 copy-start.1
  195.4 1.6 copy-done.1
  197.0 0.0 copy-start.4
  197.0 2.3 %finish.6 = (f32[8,512,256]{2,1,0:T(8,128)}, bf16[3,8,512,256]{3,2,1,0:T(8,128)(2,1)}) custom-call(s32[1]{0:T(128)} %bitcast.place_ref, f32[3]{0:T(128)S(1)} %copy-done.5, bf16[2,2,512,256]{3,2,1,0:T(8,128)(2,1)S(1)} %copy-done.2, bf16[8,512,256]{2,1,0:T(8,128)(2,1)S(1)} %copy-done.1, bf16[3,8,512,256]{3,2,1,0:T(8,128)(2,1)S(1)} %copy-done), custom_call_target="tpu_custom_call" | custom-call | flops 10000000 | bytes 6291456 | tf_op jit(solution)/shard_map/finish/pallas_call | solution.py:629
  199.3 0.0 copy-done.4
  199.3 0.0 copy-start.3
  199.3 1.7 finish.7
  201.0 0.0 copy-done.3
  201.0 1.7 finish.8
  202.7 0.0 collective-permute-done.2.sums_ref
  202.7 3.2 %finish.9 = (f32[8,512,256]{2,1,0:T(8,128)}, bf16[3,8,512,256]{3,2,1,0:T(8,128)(2,1)}) custom-call(s32[1]{0:T(128)} %bitcast.place_ref, f32[3]{0:T(128)S(1)} %copy-done.5, bf16[2,2,512,256]{3,2,1,0:T(8,128)(2,1)} %collective-permute-done.2.sums_ref, bf16[8,512,256]{2,1,0:T(8,128)(2,1)S(1)} %copy-done.1, ...), custom_call_target="tpu_custom_call", output_to_operand_aliasing={{0}: (5, {}), {1}: (6, {})} | custom-call | flops 10000000 | bytes 6291456 | tf_op jit(solution)/shard_map/finish/pallas_call | solution.py:629
  205.9 2.3 %collective-permute-done.1.sums_ref = bf16[1,2,512,256]{3,2,1,0:T(8,128)(2,1)S(1)} collective-permute-done((bf16[1,2,512,256]{3,2,1,0:T(8,128)(2,1)}, bf16[1,2,512,256]{3,2,1,0:T(8,128)(2,1)S(1)}, u32[]{:S(2)}, u32[]{:S(2)}) %collective-permute-start.1) | collective-permute-done | bytes 524320 | tf_op jit(solution)/shard_map/ppermute | solution.py:658
  208.2 1.7 finish.10
  209.9 9.5 %collective-permute-done.sums_ref = bf16[1,2,512,256]{3,2,1,0:T(8,128)(2,1)S(1)} collective-permute-done((bf16[1,2,512,256]{3,2,1,0:T(8,128)(2,1)}, bf16[1,2,512,256]{3,2,1,0:T(8,128)(2,1)S(1)}, u32[]{:S(2)}, u32[]{:S(2)}) %collective-permute-start) | collective-permute-done | bytes 524320 | tf_op jit(solution)/shard_map/ppermute | solution.py:658
  219.4 1.7 finish.11
  (4 shorter events, 0.0 us)
Async XLA Ops:
  18.1 42.6 %all-to-all-start = ((bf16[128,16,512]{2,1,0:T(8,128)(2,1)}), bf16[128,16,512]{2,1,0:T(8,128)(2,1)}, u32[]{:S(2)}, u32[]{:S(2)}) async-start(bf16[128,16,512]{2,1,0:T(8,128)(2,1)} %get-tuple-element.21), calls=%async_computation | async-start | bytes 4194304 | tf_op jit(solution)/shard_map/all_to_all | solution.py:654
  60.7 4.9 %copy-start.7 = (s32[512,8,128]{2,1,0:T(8,128)S(1)}, s32[512,8,128]{2,1,0:T(8,128)}, u32[]{:S(2)}) copy-start(s32[512,8,128]{2,1,0:T(8,128)} %param.10) | copy-start | bytes 6291460
  60.7 35.6 %all-to-all-start.1 = ((bf16[128,16,512]{2,1,0:T(8,128)(2,1)}), bf16[128,16,512]{2,1,0:T(8,128)(2,1)}, u32[]{:S(2)}, u32[]{:S(2)}) async-start(bf16[128,16,512]{2,1,0:T(8,128)(2,1)} %after.4), calls=%async_computation.1 | async-start | bytes 4194304 | tf_op jit(solution)/shard_map/all_to_all | solution.py:654
  96.3 35.5 %all-to-all-start.2 = ((bf16[128,32,256]{2,1,0:T(8,128)(2,1)}), bf16[128,32,256]{2,1,0:T(8,128)(2,1)}, u32[]{:S(2)}, u32[]{:S(2)}) async-start(bf16[128,32,256]{2,1,0:T(8,128)(2,1)} %after.5), calls=%async_computation.2 | async-start | bytes 4194304 | tf_op jit(solution)/shard_map/all_to_all | solution.py:654
  131.9 23.6 %all-to-all-start.3 = ((bf16[128,16,256]{2,1,0:T(8,128)(2,1)}), bf16[128,16,256]{2,1,0:T(8,128)(2,1)S(1)}, u32[]{:S(2)}, u32[]{:S(2)}) async-start(bf16[128,16,256]{2,1,0:T(8,128)(2,1)} %after.6), calls=%async_computation.3 | async-start | bytes 2097152 | tf_op jit(solution)/shard_map/all_to_all | solution.py:654
  155.4 1.0 copy-start.6
  156.4 24.2 %all-to-all-start.4 = ((bf16[128,16,256]{2,1,0:T(8,128)(2,1)}), bf16[128,16,256]{2,1,0:T(8,128)(2,1)}, u32[]{:S(2)}, u32[]{:S(2)}) async-start(bf16[128,16,256]{2,1,0:T(8,128)(2,1)} %after.7), calls=%async_computation.4 | async-start | bytes 2097152 | tf_op jit(solution)/shard_map/all_to_all | solution.py:654
  171.6 21.0 %copy-start.2 = (bf16[2,2,512,256]{3,2,1,0:T(8,128)(2,1)S(1)}, bf16[2,2,512,256]{3,2,1,0:T(8,128)(2,1)}, u32[]{:S(2)}) copy-start(bf16[2,2,512,256]{3,2,1,0:T(8,128)(2,1)} %last.3.sums_ref) | copy-start | bytes 3145732
  171.6 21.0 %copy-start.5 = (f32[3]{0:T(128)S(1)}, f32[3]{0:T(128)}, u32[]{:S(2)}) copy-start(f32[3]{0:T(128)} %bragg_ref.15) | copy-start | bytes 40
  171.6 31.1 %collective-permute-start.2 = (bf16[2,2,512,256]{3,2,1,0:T(8,128)(2,1)}, bf16[2,2,512,256]{3,2,1,0:T(8,128)(2,1)}, u32[]{:S(2)}, u32[]{:S(2)}) collective-permute-start(bf16[2,2,512,256]{3,2,1,0:T(8,128)(2,1)} %last.3.sums_ref), channel_id=1, source_target_pairs={{0,64},{64,0},{1,65},{65,1},{2,66},{66,2},{3,67},{67,3},{4,68},{68... | collective-permute-start | bytes 3145736 | tf_op jit(solution)/shard_map/ppermute | solution.py:658
  191.1 17.1 %collective-permute-start.1 = (bf16[1,2,512,256]{3,2,1,0:T(8,128)(2,1)}, bf16[1,2,512,256]{3,2,1,0:T(8,128)(2,1)S(1)}, u32[]{:S(2)}, u32[]{:S(2)}) collective-permute-start(bf16[1,2,512,256]{3,2,1,0:T(8,128)(2,1)} %get-tuple-element.27.sums_ref), channel_id=1, source_target_pairs={{0,64},{64,0},{1,65},{65,1},{2,66},{66,2},{3,67},{67,3},{4,68},{68... | collective-permute-start | bytes 1572872 | tf_op jit(solution)/shard_map/ppermute | solution.py:658
  191.5 28.0 %collective-permute-start = (bf16[1,2,512,256]{3,2,1,0:T(8,128)(2,1)}, bf16[1,2,512,256]{3,2,1,0:T(8,128)(2,1)S(1)}, u32[]{:S(2)}, u32[]{:S(2)}) collective-permute-start(bf16[1,2,512,256]{3,2,1,0:T(8,128)(2,1)} %get-tuple-element.26.sums_ref), channel_id=1, source_target_pairs={{0,64},{64,0},{1,65},{65,1},{2,66},{66,2},{3,67},{67,3},{4,68},{68... | collective-permute-start | bytes 1572872 | tf_op jit(solution)/shard_map/ppermute | solution.py:658
  192.6 2.8 %copy-start = (bf16[3,8,512,256]{3,2,1,0:T(8,128)(2,1)S(1)}, bf16[3,8,512,256]{3,2,1,0:T(8,128)(2,1)}, u32[]{:S(2)}) copy-start(bf16[3,8,512,256]{3,2,1,0:T(8,128)(2,1)} %disp_ref.15) | copy-start | bytes 18874372
  195.4 1.6 copy-start.1
  197.0 2.3 %copy-start.4 = (bf16[1,2,512,256]{3,2,1,0:T(8,128)(2,1)S(1)}, bf16[1,2,512,256]{3,2,1,0:T(8,128)(2,1)}, u32[]{:S(2)}) copy-start(bf16[1,2,512,256]{3,2,1,0:T(8,128)(2,1)} %get-tuple-element.27.sums_ref) | copy-start | bytes 1572868
  199.3 1.7 copy-start.3

commit v5 on v4

--- a/solution.py
+++ b/solution.py
@@ -10,7 +10,7 @@
 
 step_size = 0.5
 both_axes = ("slab", "spec")
-vmem_limit = 62 * 1024 * 1024
+vmem_limit = 63 * 1024 * 1024
 small_limit = 36 * 1024 * 1024
 cos_terms = (
     0.9999992117703129, -19.738980419471183, 64.92865850463387,
@@ -22,14 +22,23 @@
 )
 
 
-wave_cos_terms = (
-    0.9999590619701949, -19.73094403547976, 64.67145824268955,
-    -82.39085380484792, 45.6210638400798,
-)
-wave_sin_terms = (
-    6.283161153735962, -41.33683281238831, 81.44771611530231,
-    -74.90944720114622, 33.548361462485595,
-)
+half_cos_terms = (1.4142040219808052, -6.977637477680364,
+    5.71518850637918, -1.728213959543254)
+half_sin_terms = (4.442879570076877, -7.307816738835657,
+    3.597774399705265, -0.7911994115558773)
+
+
+def scaled_cos_sin(turns, magnitude):
+    rest = turns - jnp.round(turns)
+    square = rest * rest
+    cosine = half_cos_terms[3] * square + half_cos_terms[2]
+    sine = half_sin_terms[3] * square + half_sin_terms[2]
+    for level in (1, 0):
+        cosine = cosine * square + half_cos_terms[level]
+        sine = sine * square + half_sin_terms[level]
+    sine = sine * rest
+    scaled = magnitude * sine
+    return magnitude - scaled * sine, scaled * cosine
 
 
 def cos_sin_turns(turns, cos_series=cos_terms, sin_series=sin_terms):
@@ -216,13 +225,11 @@
     )
     magnitude = amp_ref[row, at, :].astype(jnp.float32) * mask_ref[row, at, :].astype(jnp.float32)
     for member in range(4):
-        cosine, sine = cos_sin_turns(
-            (scales_ref[member] * (0.5 / math.pi)) * phase, wave_cos_terms, wave_sin_terms
-        )
+        real, imag = scaled_cos_sin((scales_ref[member] * (0.5 / math.pi)) * phase, magnitude)
         use(
             member,
             jnp.concatenate(
-                [(magnitude * cosine).astype(jnp.bfloat16), (magnitude * sine).astype(jnp.bfloat16)], axis=1
+                [real.astype(jnp.bfloat16), imag.astype(jnp.bfloat16)], axis=1
             ),
         )
 

time: 222 us -> 222 us (level)
    unnamed x19 -> x17, local copies, waits for them, and re-layouts: 7.79 us -> 7.99 us
where the time goes in v5:
time: 222 us; the launch traced here: 220 us
  Pallas kernels  120 us (54%)
  waiting for transfers between devices  57 us (26%)
  starting transfers between devices  34 us (15%)
  local copies, waits for them, and re-layouts  8.25 us (4%)
    all_to_all x5, waiting for transfers between devices, exchange(): lax.all_to_all(blocks, both_axes, split_axis=0, concat_axis=0, tiled=True)  46.4 us
    pallas_call x2, Pallas kernels, middle(): pl.pallas_call(middle_kernel, grid=(8,), in_specs=[pl.BlockSpec(memory_sp...  32.1 us
    all_to_all x5, starting transfers between devices, exchange(): lax.all_to_all(blocks, both_axes, split_axis=0, concat_axis=0, tiled=True)  31.1 us
    pallas_call x2, Pallas kernels, last(): pl.pallas_call(last_kernel, grid_spec=pltpu.PrefetchScalarGridSpec(num_sc...  21 us
    pallas_call x1, Pallas kernels, first_half(): pl.pallas_call(first_kernel, grid_spec=pltpu.PrefetchScalarGridSpec(num_s...  17 us
    pallas_call x6, Pallas kernels, finish(): pl.pallas_call(finish_kernel, grid_spec=pltpu.PrefetchScalarGridSpec(num_...  12.4 us
    pallas_call x1, Pallas kernels, waves(): pl.pallas_call(wave_kernel, grid_spec=pltpu.PrefetchScalarGridSpec(num_sc...  10.9 us
    ppermute x3, waiting for transfers between devices, swap(): return lax.ppermute(values, 'spec', [(0, 1), (1, 0)])  10.6 us
  transfers between devices with their start and end apart: 8, of which 7 were waited for; matrix products, arithmetic and copies ran while one was open for 1% of the time, Pallas kernels for 46%

profile of v5, /device:TPU:1, one launch (start us, length us, event | category | flops | bytes accessed | tf_op | source)
XLA Modules:
  0.0 220.5 jit_solution(3611977314436810907)
XLA Ops:
  0.6 17.0 %first_half.1 = (bf16[4,1024,512]{2,1,0:T(8,128)(2,1)}, bf16[128,16,512]{2,1,0:T(8,128)(2,1)}) custom-call(s32[1]{0:T(128)} %bitcast.place_ref, f32[3]{0:T(128)} %bragg_ref.15, f32[4]{0:T(128)} %scales_ref.11, bf16[3,8,512,256]{3,2,1,0:T(8,128)(2,1)} %disp_ref.15, bf16[8,512,256]{2,1,0:T(8,128)(2,1)} %amp_ref.19, s32[8,512,256]{2,1,0:T(8,128)} %mask_ref.3), custom_call_target="tpu_custom_call" | custom-call | flops 8999999488 | bytes 14680064 | tf_op jit(solution)/shard_map/first_half/pallas_call | solution.py:332
  17.6 12.0 %all-to-all-start = ((bf16[128,16,512]{2,1,0:T(8,128)(2,1)}), bf16[128,16,512]{2,1,0:T(8,128)(2,1)}, u32[]{:S(2)}, u32[]{:S(2)}) async-start(bf16[128,16,512]{2,1,0:T(8,128)(2,1)} %get-tuple-element.21), calls=%async_computation | async-start | bytes 4194304 | tf_op jit(solution)/shard_map/all_to_all | solution.py:661
  29.6 6.3 %row_matrices.1.rows_ref = bf16[4,2,512,1024]{3,2,1,0:T(8,128)(2,1)} custom-call(f32[4]{0:T(128)} %scales_ref.11), custom_call_target="tpu_custom_call" | custom-call | flops 4000000000 | bytes 8388608 | tf_op jit(solution)/shard_map/row_matrices/pallas_call | solution.py:136
  35.9 7.1 %second_half.1.refs_0_ = bf16[128,16,512]{2,1,0:T(8,128)(2,1)} custom-call(bf16[4,1024,512]{2,1,0:T(8,128)(2,1)} %get-tuple-element.20.section_ref, bf16[4,2,512,1024]{3,2,1,0:T(8,128)(2,1)} %row_matrices.1.rows_ref), custom_call_target="tpu_custom_call" | custom-call | flops 3000000000 | bytes 10485760 | tf_op jit(solution)/shard_map/second_half/pallas_call | solution.py:374
  43.0 10.9 %waves.1.refs_2_.wave_ref = bf16[4,4,512,512]{3,2,1,0:T(8,128)(2,1)} custom-call(s32[1]{0:T(128)} %bitcast.place_ref, f32[3]{0:T(128)} %bragg_ref.15, f32[4]{0:T(128)} %scales_ref.11, bf16[3,8,512,256]{3,2,1,0:T(8,128)(2,1)} %disp_ref.15, bf16[8,512,256]{2,1,0:T(8,128)(2,1)} %amp_ref.19, s32[8,512,256]{2,1,0:T(8,128)} %mask_ref.3), custom_call_target="tpu_custom_call" | custom-call | flops 10000000000 | bytes 25165824 | tf_op jit(solution)/shard_map/waves/pallas_call | solution.py:262
  53.9 6.3 %all-to-all-done.refs_1_.got_ref = bf16[128,16,512]{2,1,0:T(8,128)(2,1)} async-done(((bf16[128,16,512]{2,1,0:T(8,128)(2,1)}), bf16[128,16,512]{2,1,0:T(8,128)(2,1)}, u32[]{:S(2)}, u32[]{:S(2)}) %all-to-all-start) | async-done | bytes 2097184 | tf_op jit(solution)/shard_map/all_to_all | solution.py:661
  60.2 0.0 copy-start.6
  60.2 4.9 %all-to-all-start.1 = ((bf16[128,16,512]{2,1,0:T(8,128)(2,1)}), bf16[128,16,512]{2,1,0:T(8,128)(2,1)}, u32[]{:S(2)}, u32[]{:S(2)}) async-start(bf16[128,16,512]{2,1,0:T(8,128)(2,1)} %after.4), calls=%async_computation.1 | async-start | bytes 4194304 | tf_op jit(solution)/shard_map/all_to_all | solution.py:661
  65.1 0.0 copy-done.6
  65.1 0.2 constant_dynamic-slice_fusion
  65.3 0.4 copy.26
  65.7 0.1 fusion
  65.7 1.0 copy.28.counts_ref
  66.7 5.7 %column_matrices.1 = (bf16[4,2,512,1024]{3,2,1,0:T(8,128)(2,1)}, bf16[4,256,512]{2,1,0:T(8,128)(2,1)}) custom-call(f32[4]{0:T(128)} %scales_ref.11), custom_call_target="tpu_custom_call" | custom-call | flops 4000000000 | bytes 8388608 | tf_op jit(solution)/shard_map/column_matrices/pallas_call | solution.py:180
  72.5 16.1 %middle.3.refs_0_ = bf16[128,32,256]{2,1,0:T(8,128)(2,1)} custom-call(f32[4]{0:T(128)} %weights_ref.3, bf16[128,16,512]{2,1,0:T(8,128)(2,1)} %all-to-all-done.refs_1_.got_ref, s32[512,256]{1,0:T(8,128)} %copy.28.counts_ref, bf16[4,2,512,1024]{3,2,1,0:T(8,128)(2,1)} %get-tuple-element.22.cols_ref.real_cols_ref.imag_cols_ref, ...), custom_call_target="tpu_custom_call" | custom-call | flops 8999999488 | bytes 23068672 | tf_op jit(solution)/shard_map/middle/pallas_call | solution.py:455
  88.6 7.3 %all-to-all-done.1.got_ref.refs_1_ = bf16[128,16,512]{2,1,0:T(8,128)(2,1)} async-done(((bf16[128,16,512]{2,1,0:T(8,128)(2,1)}), bf16[128,16,512]{2,1,0:T(8,128)(2,1)}, u32[]{:S(2)}, u32[]{:S(2)}) %all-to-all-start.1) | async-done | bytes 2097184 | tf_op jit(solution)/shard_map/all_to_all | solution.py:661
  95.9 4.9 %all-to-all-start.2 = ((bf16[128,32,256]{2,1,0:T(8,128)(2,1)}), bf16[128,32,256]{2,1,0:T(8,128)(2,1)}, u32[]{:S(2)}, u32[]{:S(2)}) async-start(bf16[128,32,256]{2,1,0:T(8,128)(2,1)} %after.5), calls=%async_computation.2 | async-start | bytes 4194304 | tf_op jit(solution)/shard_map/all_to_all | solution.py:661
  100.8 1.0 copy.27.counts_ref
  101.8 16.0 %middle.2 = (bf16[128,16,256]{2,1,0:T(8,128)(2,1)}, bf16[128,16,256]{2,1,0:T(8,128)(2,1)}) custom-call(f32[4]{0:T(128)} %weights_ref.3, bf16[128,16,512]{2,1,0:T(8,128)(2,1)} %all-to-all-done.1.got_ref.refs_1_, s32[512,256]{1,0:T(8,128)} %copy.27.counts_ref, bf16[4,2,512,1024]{3,2,1,0:T(8,128)(2,1)} %get-tuple-element.22.cols_ref.real_cols_ref.imag_cols_ref, ...), custom_call_target="tpu_custom_call" | custom-call | flops 8999999488 | bytes 23068672 | tf_op jit(solution)/shard_map/middle/pallas_call | solution.py:455
  117.8 13.6 %all-to-all-done.2.got_ref.refs_1_ = bf16[128,32,256]{2,1,0:T(8,128)(2,1)} async-done(((bf16[128,32,256]{2,1,0:T(8,128)(2,1)}), bf16[128,32,256]{2,1,0:T(8,128)(2,1)}, u32[]{:S(2)}, u32[]{:S(2)}) %all-to-all-start.2) | async-done | bytes 2097184 | tf_op jit(solution)/shard_map/all_to_all | solution.py:661
  131.4 4.7 %all-to-all-start.3 = ((bf16[128,16,256]{2,1,0:T(8,128)(2,1)}), bf16[128,16,256]{2,1,0:T(8,128)(2,1)}, u32[]{:S(2)}, u32[]{:S(2)}) async-start(bf16[128,16,256]{2,1,0:T(8,128)(2,1)} %after.6), calls=%async_computation.3 | async-start | bytes 2097152 | tf_op jit(solution)/shard_map/all_to_all | solution.py:661
  136.1 8.0 %early_part.1.refs_1_.real_part_ref.imag_part_ref = bf16[4,2,512,512]{3,2,1,0:T(8,128)(2,1)} custom-call(bf16[128,32,256]{2,1,0:T(8,128)(2,1)} %all-to-all-done.2.got_ref.refs_1_, bf16[4,2,512,1024]{3,2,1,0:T(8,128)(2,1)} %get-tuple-element.22.cols_ref.real_cols_ref.imag_cols_ref), custom_call_target="tpu_custom_call" | custom-call | flops 4000000000 | bytes 10485760 | tf_op jit(solution)/shard_map/early_part/pallas_call | solution.py:508
  144.1 11.6 %all-to-all-done.3.refs_2_.late_ref = bf16[128,16,256]{2,1,0:T(8,128)(2,1)} async-done(((bf16[128,16,256]{2,1,0:T(8,128)(2,1)}), bf16[128,16,256]{2,1,0:T(8,128)(2,1)}, u32[]{:S(2)}, u32[]{:S(2)}) %all-to-all-start.3) | async-done | bytes 1048608 | tf_op jit(solution)/shard_map/all_to_all | solution.py:661
  155.7 4.7 %all-to-all-start.4 = ((bf16[128,16,256]{2,1,0:T(8,128)(2,1)}), bf16[128,16,256]{2,1,0:T(8,128)(2,1)}, u32[]{:S(2)}, u32[]{:S(2)}) async-start(bf16[128,16,256]{2,1,0:T(8,128)(2,1)} %after.7), calls=%async_computation.4 | async-start | bytes 2097152 | tf_op jit(solution)/shard_map/all_to_all | solution.py:661
  160.4 10.5 %last.3.sums_ref = bf16[2,2,512,256]{3,2,1,0:T(8,128)(2,1)} custom-call(s32[1]{0:T(128)} %bitcast.place_ref, f32[4]{0:T(128)} %scales_ref.11, bf16[128,16,256]{2,1,0:T(8,128)(2,1)} %all-to-all-done.3.refs_2_.late_ref, bf16[4,2,512,1024]{3,2,1,0:T(8,128)(2,1)} %get-tuple-element.22.cols_ref.real_cols_ref.imag_cols_ref, ...), custom_call_target="tpu_custom_call" | custom-call | flops 4000000000 | bytes 16777216 | tf_op jit(solution)/shard_map/last/pallas_call | solution.py:585
  170.8 0.0 copy-start.5
  170.8 1.4 collective-permute-start.2
  172.2 7.6 %all-to-all-done.4.late_ref = bf16[128,16,256]{2,1,0:T(8,128)(2,1)} async-done(((bf16[128,16,256]{2,1,0:T(8,128)(2,1)}), bf16[128,16,256]{2,1,0:T(8,128)(2,1)}, u32[]{:S(2)}, u32[]{:S(2)}) %all-to-all-start.4) | async-done | bytes 1048608 | tf_op jit(solution)/shard_map/all_to_all | solution.py:661
  179.9 10.5 %last.2 = (bf16[1,2,512,256]{3,2,1,0:T(8,128)(2,1)}, bf16[1,2,512,256]{3,2,1,0:T(8,128)(2,1)}) custom-call(s32[1]{0:T(128)} %bitcast.place_ref, f32[4]{0:T(128)} %scales_ref.11, bf16[128,16,256]{2,1,0:T(8,128)(2,1)} %all-to-all-done.4.late_ref, bf16[4,2,512,1024]{3,2,1,0:T(8,128)(2,1)} %get-tuple-element.22.cols_ref.real_cols_ref.imag_cols_ref, ...), custom_call_target="tpu_custom_call" | custom-call | flops 4000000000 | bytes 16777216 | tf_op jit(solution)/shard_map/last/pallas_call | solution.py:585
  190.4 0.4 collective-permute-start.1
  190.7 1.1 collective-permute-start
  191.8 0.0 copy-done.5
  191.8 0.0 copy-start
  191.8 2.8 %copy-done = bf16[3,8,512,256]{3,2,1,0:T(8,128)(2,1)S(1)} copy-done((bf16[3,8,512,256]{3,2,1,0:T(8,128)(2,1)S(1)}, bf16[3,8,512,256]{3,2,1,0:T(8,128)(2,1)}, u32[]{:S(2)}) %copy-start) | copy-done | bytes 6291480
  194.6 0.0 copy-start.1
  194.6 1.6 copy-done.1
  196.2 0.0 copy-start.2
  196.2 1.2 copy-done.2
  197.4 0.0 copy-start.4
  197.4 2.3 %finish.6 = (f32[8,512,256]{2,1,0:T(8,128)}, bf16[3,8,512,256]{3,2,1,0:T(8,128)(2,1)}) custom-call(s32[1]{0:T(128)} %bitcast.place_ref, f32[3]{0:T(128)S(1)} %copy-done.5, bf16[2,2,512,256]{3,2,1,0:T(8,128)(2,1)S(1)} %copy-done.2, bf16[8,512,256]{2,1,0:T(8,128)(2,1)S(1)} %copy-done.1, bf16[3,8,512,256]{3,2,1,0:T(8,128)(2,1)S(1)} %copy-done), custom_call_target="tpu_custom_call" | custom-call | flops 10000000 | bytes 6291456 | tf_op jit(solution)/shard_map/finish/pallas_call | solution.py:636
  199.8 0.0 copy-done.4
  199.8 0.0 copy-start.3
  199.8 1.7 finish.7
  201.5 0.0 copy-done.3
  201.5 1.7 finish.8
  203.2 0.0 collective-permute-done.2.sums_ref
  203.2 3.2 %finish.9 = (f32[8,512,256]{2,1,0:T(8,128)}, bf16[3,8,512,256]{3,2,1,0:T(8,128)(2,1)}) custom-call(s32[1]{0:T(128)} %bitcast.place_ref, f32[3]{0:T(128)S(1)} %copy-done.5, bf16[2,2,512,256]{3,2,1,0:T(8,128)(2,1)} %collective-permute-done.2.sums_ref, bf16[8,512,256]{2,1,0:T(8,128)(2,1)S(1)} %copy-done.1, ...), custom_call_target="tpu_custom_call", output_to_operand_aliasing={{0}: (5, {}), {1}: (6, {})} | custom-call | flops 10000000 | bytes 6291456 | tf_op jit(solution)/shard_map/finish/pallas_call | solution.py:636
  206.4 1.1 collective-permute-done.1.sums_ref
  207.5 1.7 finish.10
  209.2 9.5 %collective-permute-done.sums_ref = bf16[1,2,512,256]{3,2,1,0:T(8,128)(2,1)S(1)} collective-permute-done((bf16[1,2,512,256]{3,2,1,0:T(8,128)(2,1)}, bf16[1,2,512,256]{3,2,1,0:T(8,128)(2,1)S(1)}, u32[]{:S(2)}, u32[]{:S(2)}) %collective-permute-start) | collective-permute-done | bytes 524320 | tf_op jit(solution)/shard_map/ppermute | solution.py:665
  218.7 1.7 finish.11
  (4 shorter events, 0.0 us)
Async XLA Ops:
  17.6 42.6 %all-to-all-start = ((bf16[128,16,512]{2,1,0:T(8,128)(2,1)}), bf16[128,16,512]{2,1,0:T(8,128)(2,1)}, u32[]{:S(2)}, u32[]{:S(2)}) async-start(bf16[128,16,512]{2,1,0:T(8,128)(2,1)} %get-tuple-element.21), calls=%async_computation | async-start | bytes 4194304 | tf_op jit(solution)/shard_map/all_to_all | solution.py:661
  60.2 4.9 %copy-start.6 = (s32[512,8,128]{2,1,0:T(8,128)S(1)}, s32[512,8,128]{2,1,0:T(8,128)}, u32[]{:S(2)}) copy-start(s32[512,8,128]{2,1,0:T(8,128)} %param.10) | copy-start | bytes 6291460
  60.2 35.7 %all-to-all-start.1 = ((bf16[128,16,512]{2,1,0:T(8,128)(2,1)}), bf16[128,16,512]{2,1,0:T(8,128)(2,1)}, u32[]{:S(2)}, u32[]{:S(2)}) async-start(bf16[128,16,512]{2,1,0:T(8,128)(2,1)} %after.4), calls=%async_computation.1 | async-start | bytes 4194304 | tf_op jit(solution)/shard_map/all_to_all | solution.py:661
  95.9 35.5 %all-to-all-start.2 = ((bf16[128,32,256]{2,1,0:T(8,128)(2,1)}), bf16[128,32,256]{2,1,0:T(8,128)(2,1)}, u32[]{:S(2)}, u32[]{:S(2)}) async-start(bf16[128,32,256]{2,1,0:T(8,128)(2,1)} %after.5), calls=%async_computation.2 | async-start | bytes 4194304 | tf_op jit(solution)/shard_map/all_to_all | solution.py:661
  131.4 24.3 %all-to-all-start.3 = ((bf16[128,16,256]{2,1,0:T(8,128)(2,1)}), bf16[128,16,256]{2,1,0:T(8,128)(2,1)}, u32[]{:S(2)}, u32[]{:S(2)}) async-start(bf16[128,16,256]{2,1,0:T(8,128)(2,1)} %after.6), calls=%async_computation.3 | async-start | bytes 2097152 | tf_op jit(solution)/shard_map/all_to_all | solution.py:661
  155.7 24.2 %all-to-all-start.4 = ((bf16[128,16,256]{2,1,0:T(8,128)(2,1)}), bf16[128,16,256]{2,1,0:T(8,128)(2,1)}, u32[]{:S(2)}, u32[]{:S(2)}) async-start(bf16[128,16,256]{2,1,0:T(8,128)(2,1)} %after.7), calls=%async_computation.4 | async-start | bytes 2097152 | tf_op jit(solution)/shard_map/all_to_all | solution.py:661
  170.8 21.0 %copy-start.5 = (f32[3]{0:T(128)S(1)}, f32[3]{0:T(128)}, u32[]{:S(2)}) copy-start(f32[3]{0:T(128)} %bragg_ref.15) | copy-start | bytes 40
  170.8 32.3 %collective-permute-start.2 = (bf16[2,2,512,256]{3,2,1,0:T(8,128)(2,1)}, bf16[2,2,512,256]{3,2,1,0:T(8,128)(2,1)}, u32[]{:S(2)}, u32[]{:S(2)}) collective-permute-start(bf16[2,2,512,256]{3,2,1,0:T(8,128)(2,1)} %last.3.sums_ref), channel_id=1, source_target_pairs={{0,64},{64,0},{1,65},{65,1},{2,66},{66,2},{3,67},{67,3},{4,68},{68... | collective-permute-start | bytes 3145736 | tf_op jit(solution)/shard_map/ppermute | solution.py:665
  190.4 17.1 %collective-permute-start.1 = (bf16[1,2,512,256]{3,2,1,0:T(8,128)(2,1)}, bf16[1,2,512,256]{3,2,1,0:T(8,128)(2,1)S(1)}, u32[]{:S(2)}, u32[]{:S(2)}) collective-permute-start(bf16[1,2,512,256]{3,2,1,0:T(8,128)(2,1)} %get-tuple-element.27.sums_ref), channel_id=1, source_target_pairs={{0,64},{64,0},{1,65},{65,1},{2,66},{66,2},{3,67},{67,3},{4,68},{68... | collective-permute-start | bytes 1572872 | tf_op jit(solution)/shard_map/ppermute | solution.py:665
  190.7 28.0 %collective-permute-start = (bf16[1,2,512,256]{3,2,1,0:T(8,128)(2,1)}, bf16[1,2,512,256]{3,2,1,0:T(8,128)(2,1)S(1)}, u32[]{:S(2)}, u32[]{:S(2)}) collective-permute-start(bf16[1,2,512,256]{3,2,1,0:T(8,128)(2,1)} %get-tuple-element.26.sums_ref), channel_id=1, source_target_pairs={{0,64},{64,0},{1,65},{65,1},{2,66},{66,2},{3,67},{67,3},{4,68},{68... | collective-permute-start | bytes 1572872 | tf_op jit(solution)/shard_map/ppermute | solution.py:665
  191.8 2.8 %copy-start = (bf16[3,8,512,256]{3,2,1,0:T(8,128)(2,1)S(1)}, bf16[3,8,512,256]{3,2,1,0:T(8,128)(2,1)}, u32[]{:S(2)}) copy-start(bf16[3,8,512,256]{3,2,1,0:T(8,128)(2,1)} %disp_ref.15) | copy-start | bytes 18874372
  194.6 1.6 copy-start.1
  196.2 1.2 copy-start.2
  197.4 2.3 %copy-start.4 = (bf16[1,2,512,256]{3,2,1,0:T(8,128)(2,1)S(1)}, bf16[1,2,512,256]{3,2,1,0:T(8,128)(2,1)}, u32[]{:S(2)}) copy-start(bf16[1,2,512,256]{3,2,1,0:T(8,128)(2,1)} %get-tuple-element.27.sums_ref) | copy-start | bytes 1572868
  199.8 1.7 copy-start.3

commit v6 on v5

--- a/solution.py
+++ b/solution.py
@@ -99,9 +99,16 @@
 
 
 def fill_z(zf_ref, member, bin_scale, cells_z, frames):
-    real, imag = chirp_parts(
-        iota((cells_z, frames), 1), iota((cells_z, frames), 0), frames, cells_z, bin_scale
+    others = iota((1, frames), 1) - frames // 2
+    wide, narrow = (cells_z // 8, frames), (8, frames)
+    big_real, big_imag = small_table(
+        iota(wide, 0) - cells_z // 16, 8, jnp.broadcast_to(others, wide), cells_z, bin_scale
     )
+    low_real, low_imag = small_table(iota(narrow, 0), 1, jnp.broadcast_to(others, narrow), cells_z, bin_scale)
+    normalizer = 1.0 / math.sqrt(cells_z)
+    big_real, big_imag = (big_real * normalizer)[:, None, :], (big_imag * normalizer)[:, None, :]
+    real = (big_real * low_real[None] - big_imag * low_imag[None]).reshape(cells_z, frames)
+    imag = (big_real * low_imag[None] + big_imag * low_real[None]).reshape(cells_z, frames)
     zf_ref[member, 0:cells_z, 0:frames] = real.astype(jnp.bfloat16)
     zf_ref[member, 0:cells_z, frames : 2 * frames] = imag.astype(jnp.bfloat16)
     zf_ref[member, cells_z : 2 * cells_z, 0:frames] = (-imag).astype(jnp.bfloat16)

time: 222 us -> 221 us (level)
  no operation moved by 1% of the time
where the time goes in v6:
time: 221 us; the launch traced here: 220 us
  Pallas kernels  120 us (54%)
  waiting for transfers between devices  57 us (26%)
  starting transfers between devices  33.9 us (15%)
  local copies, waits for them, and re-layouts  8.25 us (4%)
    all_to_all x5, waiting for transfers between devices, exchange(): lax.all_to_all(blocks, both_axes, split_axis=0, concat_axis=0, tiled=True)  46.4 us
    pallas_call x2, Pallas kernels, middle(): pl.pallas_call(middle_kernel, grid=(8,), in_specs=[pl.BlockSpec(memory_sp...  32.1 us
    all_to_all x5, starting transfers between devices, exchange(): lax.all_to_all(blocks, both_axes, split_axis=0, concat_axis=0, tiled=True)  31.1 us
    pallas_call x2, Pallas kernels, last(): pl.pallas_call(last_kernel, grid_spec=pltpu.PrefetchScalarGridSpec(num_sc...  21 us
    pallas_call x1, Pallas kernels, first_half(): pl.pallas_call(first_kernel, grid_spec=pltpu.PrefetchScalarGridSpec(num_s...  16.8 us
    pallas_call x6, Pallas kernels, finish(): pl.pallas_call(finish_kernel, grid_spec=pltpu.PrefetchScalarGridSpec(num_...  12.4 us
    pallas_call x1, Pallas kernels, waves(): pl.pallas_call(wave_kernel, grid_spec=pltpu.PrefetchScalarGridSpec(num_sc...  10.9 us
    ppermute x3, waiting for transfers between devices, swap(): return lax.ppermute(values, 'spec', [(0, 1), (1, 0)])  10.6 us
  transfers between devices with their start and end apart: 8, of which 7 were waited for; matrix products, arithmetic and copies ran while one was open for 1% of the time, Pallas kernels for 46%

profile of v6, /device:TPU:1, one launch (start us, length us, event | category | flops | bytes accessed | tf_op | source)
XLA Modules:
  0.0 220.3 jit_solution(10764188852593455732)
XLA Ops:
  0.6 16.8 %first_half.1 = (bf16[4,1024,512]{2,1,0:T(8,128)(2,1)}, bf16[128,16,512]{2,1,0:T(8,128)(2,1)}) custom-call(s32[1]{0:T(128)} %bitcast.place_ref, f32[3]{0:T(128)} %bragg_ref.15, f32[4]{0:T(128)} %scales_ref.11, bf16[3,8,512,256]{3,2,1,0:T(8,128)(2,1)} %disp_ref.15, bf16[8,512,256]{2,1,0:T(8,128)(2,1)} %amp_ref.19, s32[8,512,256]{2,1,0:T(8,128)} %mask_ref.3), custom_call_target="tpu_custom_call" | custom-call | flops 8999999488 | bytes 14680064 | tf_op jit(solution)/shard_map/first_half/pallas_call | solution.py:339
  17.4 12.0 %all-to-all-start = ((bf16[128,16,512]{2,1,0:T(8,128)(2,1)}), bf16[128,16,512]{2,1,0:T(8,128)(2,1)}, u32[]{:S(2)}, u32[]{:S(2)}) async-start(bf16[128,16,512]{2,1,0:T(8,128)(2,1)} %get-tuple-element.21), calls=%async_computation | async-start | bytes 4194304 | tf_op jit(solution)/shard_map/all_to_all | solution.py:668
  29.4 6.3 %row_matrices.1.rows_ref = bf16[4,2,512,1024]{3,2,1,0:T(8,128)(2,1)} custom-call(f32[4]{0:T(128)} %scales_ref.11), custom_call_target="tpu_custom_call" | custom-call | flops 4000000000 | bytes 8388608 | tf_op jit(solution)/shard_map/row_matrices/pallas_call | solution.py:143
  35.7 7.1 %second_half.1.refs_0_ = bf16[128,16,512]{2,1,0:T(8,128)(2,1)} custom-call(bf16[4,1024,512]{2,1,0:T(8,128)(2,1)} %get-tuple-element.20.section_ref, bf16[4,2,512,1024]{3,2,1,0:T(8,128)(2,1)} %row_matrices.1.rows_ref), custom_call_target="tpu_custom_call" | custom-call | flops 3000000000 | bytes 10485760 | tf_op jit(solution)/shard_map/second_half/pallas_call | solution.py:381
  42.8 10.9 %waves.1.refs_2_.wave_ref = bf16[4,4,512,512]{3,2,1,0:T(8,128)(2,1)} custom-call(s32[1]{0:T(128)} %bitcast.place_ref, f32[3]{0:T(128)} %bragg_ref.15, f32[4]{0:T(128)} %scales_ref.11, bf16[3,8,512,256]{3,2,1,0:T(8,128)(2,1)} %disp_ref.15, bf16[8,512,256]{2,1,0:T(8,128)(2,1)} %amp_ref.19, s32[8,512,256]{2,1,0:T(8,128)} %mask_ref.3), custom_call_target="tpu_custom_call" | custom-call | flops 10000000000 | bytes 25165824 | tf_op jit(solution)/shard_map/waves/pallas_call | solution.py:269
  53.7 6.3 %all-to-all-done.refs_1_.got_ref = bf16[128,16,512]{2,1,0:T(8,128)(2,1)} async-done(((bf16[128,16,512]{2,1,0:T(8,128)(2,1)}), bf16[128,16,512]{2,1,0:T(8,128)(2,1)}, u32[]{:S(2)}, u32[]{:S(2)}) %all-to-all-start) | async-done | bytes 2097184 | tf_op jit(solution)/shard_map/all_to_all | solution.py:668
  60.0 0.0 copy-start.6
  60.0 4.9 %all-to-all-start.1 = ((bf16[128,16,512]{2,1,0:T(8,128)(2,1)}), bf16[128,16,512]{2,1,0:T(8,128)(2,1)}, u32[]{:S(2)}, u32[]{:S(2)}) async-start(bf16[128,16,512]{2,1,0:T(8,128)(2,1)} %after.4), calls=%async_computation.1 | async-start | bytes 4194304 | tf_op jit(solution)/shard_map/all_to_all | solution.py:668
  64.9 0.0 copy-done.6
  64.9 0.2 constant_dynamic-slice_fusion
  65.1 0.4 copy.26
  65.5 0.1 fusion
  65.6 1.0 copy.28.counts_ref
  66.6 5.7 %column_matrices.1 = (bf16[4,2,512,1024]{3,2,1,0:T(8,128)(2,1)}, bf16[4,256,512]{2,1,0:T(8,128)(2,1)}) custom-call(f32[4]{0:T(128)} %scales_ref.11), custom_call_target="tpu_custom_call" | custom-call | flops 4000000000 | bytes 8388608 | tf_op jit(solution)/shard_map/column_matrices/pallas_call | solution.py:187
  72.3 16.1 %middle.3.refs_0_ = bf16[128,32,256]{2,1,0:T(8,128)(2,1)} custom-call(f32[4]{0:T(128)} %weights_ref.3, bf16[128,16,512]{2,1,0:T(8,128)(2,1)} %all-to-all-done.refs_1_.got_ref, s32[512,256]{1,0:T(8,128)} %copy.28.counts_ref, bf16[4,2,512,1024]{3,2,1,0:T(8,128)(2,1)} %get-tuple-element.22.cols_ref.real_cols_ref.imag_cols_ref, ...), custom_call_target="tpu_custom_call" | custom-call | flops 8999999488 | bytes 23068672 | tf_op jit(solution)/shard_map/middle/pallas_call | solution.py:462
  88.4 7.3 %all-to-all-done.1.got_ref.refs_1_ = bf16[128,16,512]{2,1,0:T(8,128)(2,1)} async-done(((bf16[128,16,512]{2,1,0:T(8,128)(2,1)}), bf16[128,16,512]{2,1,0:T(8,128)(2,1)}, u32[]{:S(2)}, u32[]{:S(2)}) %all-to-all-start.1) | async-done | bytes 2097184 | tf_op jit(solution)/shard_map/all_to_all | solution.py:668
  95.7 4.9 %all-to-all-start.2 = ((bf16[128,32,256]{2,1,0:T(8,128)(2,1)}), bf16[128,32,256]{2,1,0:T(8,128)(2,1)}, u32[]{:S(2)}, u32[]{:S(2)}) async-start(bf16[128,32,256]{2,1,0:T(8,128)(2,1)} %after.5), calls=%async_computation.2 | async-start | bytes 4194304 | tf_op jit(solution)/shard_map/all_to_all | solution.py:668
  100.6 1.0 copy.27.counts_ref
  101.6 16.0 %middle.2 = (bf16[128,16,256]{2,1,0:T(8,128)(2,1)}, bf16[128,16,256]{2,1,0:T(8,128)(2,1)}) custom-call(f32[4]{0:T(128)} %weights_ref.3, bf16[128,16,512]{2,1,0:T(8,128)(2,1)} %all-to-all-done.1.got_ref.refs_1_, s32[512,256]{1,0:T(8,128)} %copy.27.counts_ref, bf16[4,2,512,1024]{3,2,1,0:T(8,128)(2,1)} %get-tuple-element.22.cols_ref.real_cols_ref.imag_cols_ref, ...), custom_call_target="tpu_custom_call" | custom-call | flops 8999999488 | bytes 23068672 | tf_op jit(solution)/shard_map/middle/pallas_call | solution.py:462
  117.6 13.6 %all-to-all-done.2.got_ref.refs_1_ = bf16[128,32,256]{2,1,0:T(8,128)(2,1)} async-done(((bf16[128,32,256]{2,1,0:T(8,128)(2,1)}), bf16[128,32,256]{2,1,0:T(8,128)(2,1)}, u32[]{:S(2)}, u32[]{:S(2)}) %all-to-all-start.2) | async-done | bytes 2097184 | tf_op jit(solution)/shard_map/all_to_all | solution.py:668
  131.2 4.7 %all-to-all-start.3 = ((bf16[128,16,256]{2,1,0:T(8,128)(2,1)}), bf16[128,16,256]{2,1,0:T(8,128)(2,1)}, u32[]{:S(2)}, u32[]{:S(2)}) async-start(bf16[128,16,256]{2,1,0:T(8,128)(2,1)} %after.6), calls=%async_computation.3 | async-start | bytes 2097152 | tf_op jit(solution)/shard_map/all_to_all | solution.py:668
  135.9 8.0 %early_part.1.refs_1_.real_part_ref.imag_part_ref = bf16[4,2,512,512]{3,2,1,0:T(8,128)(2,1)} custom-call(bf16[128,32,256]{2,1,0:T(8,128)(2,1)} %all-to-all-done.2.got_ref.refs_1_, bf16[4,2,512,1024]{3,2,1,0:T(8,128)(2,1)} %get-tuple-element.22.cols_ref.real_cols_ref.imag_cols_ref), custom_call_target="tpu_custom_call" | custom-call | flops 4000000000 | bytes 10485760 | tf_op jit(solution)/shard_map/early_part/pallas_call | solution.py:515
  143.9 11.6 %all-to-all-done.3.refs_2_.late_ref = bf16[128,16,256]{2,1,0:T(8,128)(2,1)} async-done(((bf16[128,16,256]{2,1,0:T(8,128)(2,1)}), bf16[128,16,256]{2,1,0:T(8,128)(2,1)}, u32[]{:S(2)}, u32[]{:S(2)}) %all-to-all-start.3) | async-done | bytes 1048608 | tf_op jit(solution)/shard_map/all_to_all | solution.py:668
  155.5 4.7 %all-to-all-start.4 = ((bf16[128,16,256]{2,1,0:T(8,128)(2,1)}), bf16[128,16,256]{2,1,0:T(8,128)(2,1)}, u32[]{:S(2)}, u32[]{:S(2)}) async-start(bf16[128,16,256]{2,1,0:T(8,128)(2,1)} %after.7), calls=%async_computation.4 | async-start | bytes 2097152 | tf_op jit(solution)/shard_map/all_to_all | solution.py:668
  160.2 10.5 %last.3.sums_ref = bf16[2,2,512,256]{3,2,1,0:T(8,128)(2,1)} custom-call(s32[1]{0:T(128)} %bitcast.place_ref, f32[4]{0:T(128)} %scales_ref.11, bf16[128,16,256]{2,1,0:T(8,128)(2,1)} %all-to-all-done.3.refs_2_.late_ref, bf16[4,2,512,1024]{3,2,1,0:T(8,128)(2,1)} %get-tuple-element.22.cols_ref.real_cols_ref.imag_cols_ref, ...), custom_call_target="tpu_custom_call" | custom-call | flops 4000000000 | bytes 16777216 | tf_op jit(solution)/shard_map/last/pallas_call | solution.py:592
  170.7 0.0 copy-start.5
  170.7 1.4 collective-permute-start.2
  172.1 7.6 %all-to-all-done.4.late_ref = bf16[128,16,256]{2,1,0:T(8,128)(2,1)} async-done(((bf16[128,16,256]{2,1,0:T(8,128)(2,1)}), bf16[128,16,256]{2,1,0:T(8,128)(2,1)}, u32[]{:S(2)}, u32[]{:S(2)}) %all-to-all-start.4) | async-done | bytes 1048608 | tf_op jit(solution)/shard_map/all_to_all | solution.py:668
  179.7 10.5 %last.2 = (bf16[1,2,512,256]{3,2,1,0:T(8,128)(2,1)}, bf16[1,2,512,256]{3,2,1,0:T(8,128)(2,1)}) custom-call(s32[1]{0:T(128)} %bitcast.place_ref, f32[4]{0:T(128)} %scales_ref.11, bf16[128,16,256]{2,1,0:T(8,128)(2,1)} %all-to-all-done.4.late_ref, bf16[4,2,512,1024]{3,2,1,0:T(8,128)(2,1)} %get-tuple-element.22.cols_ref.real_cols_ref.imag_cols_ref, ...), custom_call_target="tpu_custom_call" | custom-call | flops 4000000000 | bytes 16777216 | tf_op jit(solution)/shard_map/last/pallas_call | solution.py:592
  190.2 0.4 collective-permute-start.1
  190.6 1.1 collective-permute-start
  191.7 0.0 copy-done.5
  191.7 0.0 copy-start
  191.7 2.8 %copy-done = bf16[3,8,512,256]{3,2,1,0:T(8,128)(2,1)S(1)} copy-done((bf16[3,8,512,256]{3,2,1,0:T(8,128)(2,1)S(1)}, bf16[3,8,512,256]{3,2,1,0:T(8,128)(2,1)}, u32[]{:S(2)}) %copy-start) | copy-done | bytes 6291480
  194.5 0.0 copy-start.1
  194.5 1.6 copy-done.1
  196.0 0.0 copy-start.2
  196.0 1.2 copy-done.2
  197.3 0.0 copy-start.4
  197.3 2.3 %finish.6 = (f32[8,512,256]{2,1,0:T(8,128)}, bf16[3,8,512,256]{3,2,1,0:T(8,128)(2,1)}) custom-call(s32[1]{0:T(128)} %bitcast.place_ref, f32[3]{0:T(128)S(1)} %copy-done.5, bf16[2,2,512,256]{3,2,1,0:T(8,128)(2,1)S(1)} %copy-done.2, bf16[8,512,256]{2,1,0:T(8,128)(2,1)S(1)} %copy-done.1, bf16[3,8,512,256]{3,2,1,0:T(8,128)(2,1)S(1)} %copy-done), custom_call_target="tpu_custom_call" | custom-call | flops 10000000 | bytes 6291456 | tf_op jit(solution)/shard_map/finish/pallas_call | solution.py:643
  199.6 0.0 copy-done.4
  199.6 0.0 copy-start.3
  199.6 1.7 finish.7
  201.3 0.0 copy-done.3
  201.3 1.7 finish.8
  203.0 0.0 collective-permute-done.2.sums_ref
  203.0 3.2 %finish.9 = (f32[8,512,256]{2,1,0:T(8,128)}, bf16[3,8,512,256]{3,2,1,0:T(8,128)(2,1)}) custom-call(s32[1]{0:T(128)} %bitcast.place_ref, f32[3]{0:T(128)S(1)} %copy-done.5, bf16[2,2,512,256]{3,2,1,0:T(8,128)(2,1)} %collective-permute-done.2.sums_ref, bf16[8,512,256]{2,1,0:T(8,128)(2,1)S(1)} %copy-done.1, ...), custom_call_target="tpu_custom_call", output_to_operand_aliasing={{0}: (5, {}), {1}: (6, {})} | custom-call | flops 10000000 | bytes 6291456 | tf_op jit(solution)/shard_map/finish/pallas_call | solution.py:643
  206.2 1.1 collective-permute-done.1.sums_ref
  207.3 1.7 finish.10
  209.1 9.5 %collective-permute-done.sums_ref = bf16[1,2,512,256]{3,2,1,0:T(8,128)(2,1)S(1)} collective-permute-done((bf16[1,2,512,256]{3,2,1,0:T(8,128)(2,1)}, bf16[1,2,512,256]{3,2,1,0:T(8,128)(2,1)S(1)}, u32[]{:S(2)}, u32[]{:S(2)}) %collective-permute-start) | collective-permute-done | bytes 524320 | tf_op jit(solution)/shard_map/ppermute | solution.py:672
  218.6 1.7 finish.11
  (4 shorter events, 0.0 us)
Async XLA Ops:
  17.4 42.6 %all-to-all-start = ((bf16[128,16,512]{2,1,0:T(8,128)(2,1)}), bf16[128,16,512]{2,1,0:T(8,128)(2,1)}, u32[]{:S(2)}, u32[]{:S(2)}) async-start(bf16[128,16,512]{2,1,0:T(8,128)(2,1)} %get-tuple-element.21), calls=%async_computation | async-start | bytes 4194304 | tf_op jit(solution)/shard_map/all_to_all | solution.py:668
  60.0 4.9 %copy-start.6 = (s32[512,8,128]{2,1,0:T(8,128)S(1)}, s32[512,8,128]{2,1,0:T(8,128)}, u32[]{:S(2)}) copy-start(s32[512,8,128]{2,1,0:T(8,128)} %param.10) | copy-start | bytes 6291460
  60.0 35.7 %all-to-all-start.1 = ((bf16[128,16,512]{2,1,0:T(8,128)(2,1)}), bf16[128,16,512]{2,1,0:T(8,128)(2,1)}, u32[]{:S(2)}, u32[]{:S(2)}) async-start(bf16[128,16,512]{2,1,0:T(8,128)(2,1)} %after.4), calls=%async_computation.1 | async-start | bytes 4194304 | tf_op jit(solution)/shard_map/all_to_all | solution.py:668
  95.7 35.5 %all-to-all-start.2 = ((bf16[128,32,256]{2,1,0:T(8,128)(2,1)}), bf16[128,32,256]{2,1,0:T(8,128)(2,1)}, u32[]{:S(2)}, u32[]{:S(2)}) async-start(bf16[128,32,256]{2,1,0:T(8,128)(2,1)} %after.5), calls=%async_computation.2 | async-start | bytes 4194304 | tf_op jit(solution)/shard_map/all_to_all | solution.py:668
  131.2 24.3 %all-to-all-start.3 = ((bf16[128,16,256]{2,1,0:T(8,128)(2,1)}), bf16[128,16,256]{2,1,0:T(8,128)(2,1)}, u32[]{:S(2)}, u32[]{:S(2)}) async-start(bf16[128,16,256]{2,1,0:T(8,128)(2,1)} %after.6), calls=%async_computation.3 | async-start | bytes 2097152 | tf_op jit(solution)/shard_map/all_to_all | solution.py:668
  155.5 24.2 %all-to-all-start.4 = ((bf16[128,16,256]{2,1,0:T(8,128)(2,1)}), bf16[128,16,256]{2,1,0:T(8,128)(2,1)}, u32[]{:S(2)}, u32[]{:S(2)}) async-start(bf16[128,16,256]{2,1,0:T(8,128)(2,1)} %after.7), calls=%async_computation.4 | async-start | bytes 2097152 | tf_op jit(solution)/shard_map/all_to_all | solution.py:668
  170.7 21.0 %copy-start.5 = (f32[3]{0:T(128)S(1)}, f32[3]{0:T(128)}, u32[]{:S(2)}) copy-start(f32[3]{0:T(128)} %bragg_ref.15) | copy-start | bytes 40
  170.7 32.3 %collective-permute-start.2 = (bf16[2,2,512,256]{3,2,1,0:T(8,128)(2,1)}, bf16[2,2,512,256]{3,2,1,0:T(8,128)(2,1)}, u32[]{:S(2)}, u32[]{:S(2)}) collective-permute-start(bf16[2,2,512,256]{3,2,1,0:T(8,128)(2,1)} %last.3.sums_ref), channel_id=1, source_target_pairs={{0,64},{64,0},{1,65},{65,1},{2,66},{66,2},{3,67},{67,3},{4,68},{68... | collective-permute-start | bytes 3145736 | tf_op jit(solution)/shard_map/ppermute | solution.py:672
  190.2 17.1 %collective-permute-start.1 = (bf16[1,2,512,256]{3,2,1,0:T(8,128)(2,1)}, bf16[1,2,512,256]{3,2,1,0:T(8,128)(2,1)S(1)}, u32[]{:S(2)}, u32[]{:S(2)}) collective-permute-start(bf16[1,2,512,256]{3,2,1,0:T(8,128)(2,1)} %get-tuple-element.27.sums_ref), channel_id=1, source_target_pairs={{0,64},{64,0},{1,65},{65,1},{2,66},{66,2},{3,67},{67,3},{4,68},{68... | collective-permute-start | bytes 1572872 | tf_op jit(solution)/shard_map/ppermute | solution.py:672
  190.6 28.0 %collective-permute-start = (bf16[1,2,512,256]{3,2,1,0:T(8,128)(2,1)}, bf16[1,2,512,256]{3,2,1,0:T(8,128)(2,1)S(1)}, u32[]{:S(2)}, u32[]{:S(2)}) collective-permute-start(bf16[1,2,512,256]{3,2,1,0:T(8,128)(2,1)} %get-tuple-element.26.sums_ref), channel_id=1, source_target_pairs={{0,64},{64,0},{1,65},{65,1},{2,66},{66,2},{3,67},{67,3},{4,68},{68... | collective-permute-start | bytes 1572872 | tf_op jit(solution)/shard_map/ppermute | solution.py:672
  191.7 2.8 %copy-start = (bf16[3,8,512,256]{3,2,1,0:T(8,128)(2,1)S(1)}, bf16[3,8,512,256]{3,2,1,0:T(8,128)(2,1)}, u32[]{:S(2)}) copy-start(bf16[3,8,512,256]{3,2,1,0:T(8,128)(2,1)} %disp_ref.15) | copy-start | bytes 18874372
  194.5 1.6 copy-start.1
  196.0 1.2 copy-start.2
  197.3 2.3 %copy-start.4 = (bf16[1,2,512,256]{3,2,1,0:T(8,128)(2,1)S(1)}, bf16[1,2,512,256]{3,2,1,0:T(8,128)(2,1)}, u32[]{:S(2)}) copy-start(bf16[1,2,512,256]{3,2,1,0:T(8,128)(2,1)} %get-tuple-element.27.sums_ref) | copy-start | bytes 1572868
  199.6 1.7 copy-start.3
